TPU v7x, 32 devices: a whole 2x2x4 slice. The times are simulated.
32 devices in a mesh: tm: 8 (over y, x, core), space: 4 (over z).
Axes of the slice: x: 2, y: 2, z: 4, core: 2. Of those that a mesh axis runs over, the one named last changes fastest.
Arguments:
- tokens: bfloat16 [32, 12, 80, 1024], P('tm', 'space'), may hold values from -6 to 6
- w_in: bfloat16 [1024, 4416], replicated, may hold values from -0.1875 to 0.1875
- w_out: bfloat16 [2048, 1024], replicated, may hold values from -0.125 to 0.125
- a_log_time: float32 [32], replicated, may hold values from -16 to -3
- a_log_space: float32 [32], replicated, may hold values from -14 to -3
- dt_bias_time: float32 [32], replicated, may hold values from -1 to 1
- dt_bias_space: float32 [32], replicated, may hold values from -1 to 1
- skip_time: float32 [32], replicated, may hold values from 0.5 to 1.5
- skip_space: float32 [32], replicated, may hold values from 0.5 to 1.5
- norm_gain: float32 [2048], replicated, may hold values from 0.25 to 1.75
Outputs:
- mixed: bfloat16 [32, 12, 80, 1024], P('tm', 'space')
All inputs are finite; a program needn't handle non-finite values.
Results may differ from a plain program's by a relative error of at most 0.0062.
The roundings to bfloat16 on the way count: a program that leaves them out, or rounds other values in their place, can miss the bound.
Values may be sent and summed in bfloat16 or wider, within the bound.
No kernel may reach another device: no remote copies, remote signals or barrier semaphores. Data moves between devices by JAX's collectives and lax.ppermute only.
A program may use at most 192 MiB of HBM per device.

v0:
```python
import jax
import jax.numpy as jnp
from jax import lax
from jax.sharding import PartitionSpec as P

D = 1024
HEADS = 32
HEAD_DIM = 64
STATE = 64
DI = 2048


def from_behind(value, axis, steps):
    count = lax.axis_size(axis)
    leading, last = (max(0, -steps), min(count, count - steps))
    return lax.ppermute(value, axis, [(source, source + steps) for source in range(leading, last)])


def local_scan(inner_seq, inject, readout, log_decay, step_size):
    signal = inner_seq.astype(jnp.float32)
    cum_decay = jnp.cumsum(log_decay, axis=0)
    scores = jnp.dot(readout, inject.T, preferred_element_type=jnp.float32)
    log_span = cum_decay[:, None, :] - cum_decay[None, :, :]
    length = log_decay.shape[0]
    causal = jnp.arange(length)[:, None] >= jnp.arange(length)[None, :]
    decay_mask = jnp.where(causal[:, :, None], jnp.exp(jnp.minimum(log_span, 0.0)), 0.0)
    weights = decay_mask * scores[:, :, None] * step_size[None, :, :]
    local_out = jnp.einsum("srh,rhp->shp", weights, signal, precision=lax.Precision.HIGHEST)
    tail_weight = jnp.exp(cum_decay[-1][None, :] - cum_decay) * step_size
    end_state = jnp.einsum(
        "rhp,rn->hpn",
        tail_weight[:, :, None] * signal,
        inject.astype(jnp.float32),
        precision=lax.Precision.HIGHEST,
    )
    return (local_out, end_state, cum_decay[-1], cum_decay)


def apply_start(local_out, cum_decay, readout, inner_seq, skip_gain, start_state):
    carried = jnp.einsum(
        "sn,hpn->shp", readout.astype(jnp.float32), start_state, precision=lax.Precision.HIGHEST
    )
    return (
        local_out
        + jnp.exp(cum_decay)[:, :, None] * carried
        + skip_gain[None, :, None] * inner_seq.astype(jnp.float32)
    )


def space_carry(end_state, total_decay):
    growth = jnp.exp(total_decay)[..., None, None]

    def relay_step(loop_index, start_state):
        return from_behind(growth * start_state + end_state, "space", 1)

    return lax.fori_loop(0, lax.axis_size("space") - 1, relay_step, jnp.zeros_like(end_state))


def body(
    tokens,
    w_in,
    w_out,
    a_log_time,
    a_log_space,
    dt_bias_time,
    dt_bias_space,
    skip_time,
    skip_space,
    norm_gain,
):
    base = 2 * DI
    w_time = jnp.concatenate(
        [
            w_in[:, DI:base],
            w_in[:, base : base + 2 * STATE],
            w_in[:, base + 4 * STATE : base + 4 * STATE + HEADS],
        ],
        axis=1,
    )
    w_home = jnp.concatenate(
        [
            w_in[:, :DI],
            w_in[:, base + 2 * STATE : base + 4 * STATE],
            w_in[:, base + 4 * STATE + HEADS :],
        ],
        axis=1,
    )
    fr_dev, rows_dev, cols_dev = (tokens.shape[0], tokens.shape[1], tokens.shape[2])
    n_tm = lax.axis_size("tm")
    flat_tokens = tokens.reshape(-1, D)
    home = jnp.dot(flat_tokens, w_home, preferred_element_type=jnp.float32)
    gate_z = home[:, :DI].astype(jnp.bfloat16)
    b_space = home[:, DI : DI + STATE].astype(jnp.bfloat16)
    c_space = home[:, DI + STATE : DI + 2 * STATE].astype(jnp.bfloat16)
    step_space = jax.nn.softplus(home[:, DI + 2 * STATE :] + dt_bias_space)
    decay_space = -jnp.exp(a_log_space) * step_space
    scan_all = jax.vmap(local_scan)
    time_pack = jnp.dot(flat_tokens, w_time, preferred_element_type=jnp.float32).astype(
        jnp.bfloat16
    )
    sending = time_pack.reshape(fr_dev, n_tm, -1, time_pack.shape[-1])
    time_pack = lax.all_to_all(sending, "tm", split_axis=1, concat_axis=0, tiled=True)
    frames = time_pack.shape[0]
    item_count = time_pack.shape[2]
    sequences = jnp.swapaxes(time_pack[:, 0], 0, 1)
    inner_seq = sequences[..., :DI].reshape(item_count, frames, HEADS, HEAD_DIM)
    inject = sequences[..., DI : DI + STATE]
    readout = sequences[..., DI + STATE : DI + 2 * STATE]
    raw_step = sequences[..., DI + 2 * STATE :].astype(jnp.float32)
    step_size = jax.nn.softplus(raw_step + dt_bias_time)
    log_decay = -jnp.exp(a_log_time) * step_size
    time_local_out, unused_end, unused_total, unused_cum = scan_all(
        inner_seq, inject, readout, log_decay, step_size
    )
    result = time_local_out + skip_time[None, None, :, None] * inner_seq.astype(jnp.float32)
    result = result.astype(jnp.bfloat16).reshape(item_count, frames, DI)
    returned = jnp.swapaxes(result, 0, 1)[:, None]
    time_out = lax.all_to_all(returned, "tm", split_axis=0, concat_axis=1, tiled=True)
    space_in = time_out.reshape(fr_dev, rows_dev, cols_dev, HEADS, HEAD_DIM)
    inject_grid = b_space.reshape(fr_dev, rows_dev, cols_dev, STATE)
    readout_grid = c_space.reshape(fr_dev, rows_dev, cols_dev, STATE)
    decay_grid = decay_space.reshape(fr_dev, rows_dev, cols_dev, HEADS)
    step_grid = step_space.reshape(fr_dev, rows_dev, cols_dev, HEADS)
    apply_all = jax.vmap(apply_start, in_axes=(0, 0, 0, 0, None, 0))
    state_now = jnp.zeros((fr_dev, HEADS, HEAD_DIM, STATE), jnp.float32)
    decay_sum = jnp.zeros((fr_dev, HEADS), jnp.float32)
    row_results = []
    row_offsets = []
    for row_index in range(rows_dev):
        inner_row = space_in[:, row_index]
        readout_row = readout_grid[:, row_index]
        local_out, end_state, total_decay, cum_decay = scan_all(
            inner_row,
            inject_grid[:, row_index],
            readout_row,
            decay_grid[:, row_index],
            step_grid[:, row_index],
        )
        row_results.append(
            apply_all(local_out, cum_decay, readout_row, inner_row, skip_space, state_now)
        )
        row_offsets.append(cum_decay + decay_sum[:, None, :])
        state_now = jnp.exp(total_decay)[..., None, None] * state_now + end_state
        decay_sum = decay_sum + total_decay
    space_start = space_carry(state_now, decay_sum)
    finished = []
    for row_index in range(rows_dev):
        carried = jnp.einsum(
            "fsn,fhpn->fshp",
            readout_grid[:, row_index].astype(jnp.float32),
            space_start,
            precision=lax.Precision.HIGHEST,
        )
        finished.append(
            row_results[row_index] + jnp.exp(row_offsets[row_index])[..., None] * carried
        )
    space_out = jnp.stack(finished, axis=1).reshape(-1, DI)
    gated = space_out * jax.nn.silu(gate_z.astype(jnp.float32))
    inv_scale = lax.rsqrt(jnp.mean(gated * gated, axis=-1, keepdims=True) + 1e-05)
    normed = (gated * inv_scale * norm_gain).astype(jnp.bfloat16)
    summed = jnp.dot(normed, w_out, preferred_element_type=jnp.float32) + flat_tokens.astype(
        jnp.float32
    )
    return summed.astype(jnp.bfloat16).reshape(tokens.shape)


def solution(mesh):
    placed = (P("tm", "space", None, None), P(), P(), P(), P(), P(), P(), P(), P(), P())
    return jax.shard_map(
        body, mesh=mesh, in_specs=placed, out_specs=P("tm", "space", None, None), check_vma=False
    )
```

profile of v0, /device:TPU:18, one launch (start us, length us, event | category | flops | bytes accessed | tf_op | source)
XLA Modules:
  0.0 667.1 jit_solution(18035700718439865655)
XLA Ops:
  3.8 6.4 fusion.42
  10.2 7.2 %reshape.156 = bf16[4,8,30,2208]{3,2,1,0:T(8,128)(2,1)} reshape(bf16[960,2208]{1,0:T(8,128)(2,1)} %fusion.42) | data formatting | bytes 8478720 | tf_op jit(solution)/shard_map/reshape | solution.py:101
  17.4 7.9 %copy.128 = bf16[4,8,30,2208]{3,0,2,1:T(4,128)(2,1)} copy(bf16[4,8,30,2208]{3,2,1,0:T(8,128)(2,1)} %reshape.156) | data formatting | bytes 8478720 | tf_op jit(solution)/shard_map/reshape | solution.py:101
  25.2 5.3 all-to-all-start
  30.5 4.7 slice.111
  35.3 45.3 %all-to-all-done = bf16[4,8,30,2208]{3,0,2,1:T(4,128)(2,1)} async-done(((bf16[4,8,30,2208]{3,0,2,1:T(4,128)(2,1)}), bf16[4,8,30,2208]{3,0,2,1:T(4,128)(2,1)}, u32[]{:S(2)}, u32[]{:S(2)}) %all-to-all-start) | async-done | bytes 4239392 | tf_op jit(solution)/shard_map/all_to_all | solution.py:102
  80.7 6.6 copy.129
  87.3 7.5 %squeeze.58 = bf16[32,30,2208]{2,0,1:T(8,128)(2,1)} reshape(bf16[8,4,1,30,2208]{4,1,0,3,2:T(4,128)(2,1)} %copy.129) | data formatting | bytes 8478720 | tf_op jit(solution)/shard_map/squeeze | solution.py:105
  94.7 4.5 slice.135
  102.7 12.3 %reshape.157 = bf16[30,32,32,64]{3,2,1,0:T(8,128)(2,1)} reshape(bf16[30,32,2048]{2,1,0:T(8,128)(2,1)} %slice.135) | data formatting | bytes 7864320 | tf_op jit(solution)/shard_map/reshape | solution.py:106
  115.1 16.9 %fusion = bf16[30,32,32,64]{3,1,2,0:T(8,128)(2,1)S(1)} fusion(bf16[30,32,32,64]{3,2,1,0:T(8,128)(2,1)} %reshape.157, f32[32]{0:T(128)S(1)} %copy-done.26, f32[30,32,32]{1,2,0:T(8,128)S(1)} %copy.133, f32[30,32,32]{2,1,0:T(8,128)S(1)} %fusion.104, f32[30,32,32]{1,2,0:T(8,128)S(1)} %copy.131, pred[32,32]{1,0:T(8,128)(4,1)S(1)} %iota_compare_fusion.1), kind=kOutput, calls=%fused_computation.2 | convolution fusion | flops 767754240 | bytes 8234112 | tf_op jit(solution)/shard_map/vmap(srh,rhp->shp)/dot_general | solution.py:28
  131.9 6.7 %copy.136 = bf16[30,32,32,64]{3,2,1,0:T(8,128)(2,1)} copy(bf16[30,32,32,64]{3,1,2,0:T(8,128)(2,1)S(1)} %fusion) | data formatting | bytes 7864320 | tf_op jit(solution)/shard_map/convert_element_type | solution.py:116
  138.6 11.8 %reshape.158 = bf16[30,32,2048]{2,1,0:T(8,128)(2,1)} reshape(bf16[30,32,32,64]{3,2,1,0:T(8,128)(2,1)} %copy.136) | data formatting | bytes 7864320 | tf_op jit(solution)/shard_map/reshape | solution.py:116
  150.4 6.2 copy.137
  156.7 6.6 all-to-all-start.1
  163.3 9.0 %fusion.155 = (bf16[960,2208]{1,0:T(8,128)(2,1)}, f32[960,2208]{1,0:T(8,128)S(1)}) fusion(bf16[960,1024]{1,0:T(8,128)(2,1)S(1)} %bitcast.220, bf16[1024,32]{0,1:T(8,128)(2,1)S(1)} %get-tuple-element.41, bf16[1024,128]{0,1:T(8,128)(2,1)S(1)} %slice-done.1, bf16[1024,2048]{0,1:T(8,128)(2,1)} %slice.111), kind=kOutput, calls=%fused_computation.194 | convolution fusion | flops 4356790272 | bytes 19206144 | tf_op jit(solution)/shard_map/dot_general | solution.py:91
  181.5 3.3 fusion.100
  184.8 26.2 %all-to-all-done.1 = bf16[32,1,30,2048]{3,2,1,0:T(8,128)(2,1)} async-done(((bf16[32,1,30,2048]{3,2,1,0:T(8,128)(2,1)}), bf16[32,1,30,2048]{3,2,1,0:T(8,128)(2,1)}, u32[]{:S(2)}, u32[]{:S(2)}) %all-to-all-start.1) | async-done | bytes 3932192 | tf_op jit(solution)/shard_map/all_to_all | solution.py:118
  211.0 7.1 %copy.198 = bf16[8,4,1,30,2048]{4,1,3,0,2:T(4,128)(2,1)} copy(bf16[8,4,1,30,2048]{4,3,1,0,2:T(8,128)(2,1)} %bitcast.9) | data formatting | bytes 7864320 | tf_op jit(solution)/shard_map/all_to_all | solution.py:118
  218.1 12.2 %reshape.159 = bf16[4,3,80,32,64]{4,3,0,2,1:T(8,128)(2,1)} reshape(bf16[4,8,1,30,2048]{4,0,3,1,2:T(4,128)(2,1)} %bitcast.191) | data formatting | bytes 7864320 | tf_op jit(solution)/shard_map/reshape | solution.py:119
  230.3 6.1 fusion.152
  236.4 4.3 copy.178
  240.7 5.4 copy.186
  246.1 5.2 copy.189
  253.6 3.8 fusion.63
  260.1 3.6 fusion.109
  263.7 3.9 multiply_add_fusion.1
  270.2 299.3 %while.10 = (s32[]{:T(128)}, f32[4,32,64,64]{3,2,1,0:T(8,128)}, f32[4,32,1,1]{1,0,3,2:T(4,128)S(1)}, f32[4,32,64,64]{3,2,1,0:T(8,128)}, s32[]{:T(128)}) while((s32[]{:T(128)}, f32[4,32,64,64]{3,2,1,0:T(8,128)}, f32[4,32,1,1]{1,0,3,2:T(4,128)S(1)}, f32[4,32,64,64]{3,2,1,0:T(8,128)}, s32[]{:T(128)}) %tuple.48), condition=%wide.region_5.6_spmd, body=%wide.region_4.5_spmd.sunk | while | flops 1048578 | bytes 14680677 | solution.py:56
  270.2 5.9 multiply_add_fusion.4
  276.1 3.5 collective-permute-start
  279.5 91.3 %collective-permute-done = f32[4,32,64,64]{3,2,1,0:T(8,128)} collective-permute-done((f32[4,32,64,64]{3,2,1,0:T(8,128)}, f32[4,32,64,64]{3,2,1,0:T(8,128)}, u32[]{:S(2)}, u32[]{:S(2)}) %collective-permute-start) | collective-permute-done | bytes 2097184 | tf_op jit(solution)/shard_map/while/body/eval_jaxpr/ppermute | solution.py:16
  370.8 5.9 multiply_add_fusion.4
  376.7 3.5 collective-permute-start
  380.2 90.4 %collective-permute-done = f32[4,32,64,64]{3,2,1,0:T(8,128)} collective-permute-done((f32[4,32,64,64]{3,2,1,0:T(8,128)}, f32[4,32,64,64]{3,2,1,0:T(8,128)}, u32[]{:S(2)}, u32[]{:S(2)}) %collective-permute-start) | collective-permute-done | bytes 2097184 | tf_op jit(solution)/shard_map/while/body/eval_jaxpr/ppermute | solution.py:16
  470.6 5.9 multiply_add_fusion.4
  476.5 3.5 collective-permute-start
  480.0 89.5 %collective-permute-done = f32[4,32,64,64]{3,2,1,0:T(8,128)} collective-permute-done((f32[4,32,64,64]{3,2,1,0:T(8,128)}, f32[4,32,64,64]{3,2,1,0:T(8,128)}, u32[]{:S(2)}, u32[]{:S(2)}) %collective-permute-start) | collective-permute-done | bytes 2097184 | tf_op jit(solution)/shard_map/while/body/eval_jaxpr/ppermute | solution.py:16
  569.5 4.2 fusion.114
  573.7 4.0 fusion.107
  577.7 5.6 fusion.35
  583.4 7.6 %fusion.53 = f32[4,1,80,32,64]{2,4,3,0,1:T(8,128)} fusion(f32[4,32,64,80]{3,2,1,0:T(8,128)S(1)} %fusion.35, f32[4,80,32,64]{1,3,2,0:T(8,128)S(1)} %copy-done.1, f32[4,32,64,64]{3,2,1,0:T(8,128)} %get-tuple-element.27, bf16[4,1,80,32,64]{2,4,3,0,1:T(8,128)(2,1)S(1)} %copy.178, f32[32]{0:T(128)S(1)} %copy-done.17, f32[4,80,32]{1,2,0:T(8,128)S(1)} %copy.147, ...), kind=kOutput, calls=%fused_computation.66 | convolution fusion | flops 507904000 | bytes 15352320 | tf_op jit(solution)/shard_map/fsn,fhpn->fshp/dot_general | solution.py:148
  591.1 8.1 %fusion.58 = f32[4,1,80,32,64]{2,4,3,0,1:T(8,128)} fusion(f32[4,80,32,64]{1,3,2,0:T(8,128)S(1)} %fusion.114, f32[4,80,32,64]{1,3,2,0:T(8,128)S(1)} %copy-done.7, f32[4,80,32]{1,2,0:T(8,128)S(1)} %copy-done.14, f32[4,80,80]{2,1,0:T(8,128)S(1)} %fusion.117, f32[4,80,32]{1,2,0:T(8,128)S(1)} %copy.159, pred[80,80]{1,0:T(8,128)(4,1)S(1)} %copy-done.16, ...), kind=kOutput, calls=%fused_computation.71 | convolution fusion | flops 637829120 | bytes 9447808 | tf_op jit(solution)/shard_map/vmap(srh,rhp->shp)/dot_general | solution.py:28
  599.2 7.9 %fusion.62 = f32[4,1,80,32,64]{2,4,3,0,1:T(8,128)} fusion(f32[4,80,32,64]{1,3,2,0:T(8,128)S(1)} %fusion.107, f32[4,80,32,64]{1,3,2,0:T(8,128)S(1)} %copy-done.8, f32[4,80,32]{1,2,0:T(8,128)S(1)} %copy-done.13, f32[4,80,80]{2,1,0:T(8,128)S(1)} %fusion.111, f32[4,80,32]{1,2,0:T(8,128)S(1)} %copy.165, pred[80,80]{1,0:T(8,128)(4,1)S(1)} %copy-done.16, ...), kind=kOutput, calls=%fused_computation.75 | convolution fusion | flops 637829120 | bytes 9447808 | tf_op jit(solution)/shard_map/vmap(srh,rhp->shp)/dot_general | solution.py:28
  607.1 10.6 %pad_maximum_fusion = f32[4,3,80,32,64]{2,4,3,0,1:T(8,128)} fusion(f32[4,1,80,32,64]{2,4,3,0,1:T(8,128)} %fusion.62, f32[4,1,80,32,64]{2,4,3,0,1:T(8,128)} %fusion.58, f32[4,1,80,32,64]{2,4,3,0,1:T(8,128)S(1)} %copy-done.2), kind=kLoop, calls=%fused_computation.10 | loop fusion | flops 3932160 | bytes 15728640 | tf_op jit(solution)/shard_map/stack | solution.py:157
  617.7 17.9 %copy.171 = f32[4,3,80,32,64]{4,3,2,1,0:T(8,128)} copy(f32[4,3,80,32,64]{2,4,3,0,1:T(8,128)} %pad_maximum_fusion) | data formatting | bytes 15728640 | tf_op jit(solution)/shard_map/stack | solution.py:157
  635.6 14.5 %reshape.164 = f32[960,2048]{1,0:T(8,128)} reshape(f32[4,3,80,32,64]{4,3,2,1,0:T(8,128)} %copy.171) | data formatting | bytes 15728640 | tf_op jit(solution)/shard_map/reshape | solution.py:157
  650.1 5.8 multiply_reduce_fusion
  657.3 9.3 %add_convert_fusion = bf16[960,1024]{1,0:T(8,128)(2,1)} fusion(bf16[960,1024]{1,0:T(8,128)(2,1)S(1)} %bitcast.221, bf16[2048,1024]{1,0:T(8,128)(2,1)} %param.14, f32[2048]{0:T(1024)S(1)} %copy-done.23, f32[960]{0:T(1024)S(1)} %add_rsqrt_fusion, f32[960,2048]{1,0:T(8,128)S(1)} %copy-done, bf16[960,2208]{1,0:T(8,128)(2,1)} %get-tuple-element.72), kind=kOutput, calls=%fused_computation.85 | convolution fusion | flops 4047175680 | bytes 19934976 | tf_op jit(solution)/shard_map/dot_general | solution.py:161
  (101 shorter events, 25.4 us)
Async XLA Ops:
  0.9 2.3 slice-start
  0.9 2.9 copy-start.20
  25.2 55.4 %all-to-all-start = ((bf16[4,8,30,2208]{3,0,2,1:T(4,128)(2,1)}), bf16[4,8,30,2208]{3,0,2,1:T(4,128)(2,1)}, u32[]{:S(2)}, u32[]{:S(2)}) async-start(bf16[4,8,30,2208]{3,0,2,1:T(4,128)(2,1)} %copy.128), calls=%async_computation | async-start | bytes 8847360 | tf_op jit(solution)/shard_map/all_to_all | solution.py:102
  30.5 4.8 copy-start.24
  30.5 4.8 copy-start.25
  94.7 5.9 copy-start.19
  102.7 12.4 %copy-start.26 = (f32[32]{0:T(128)S(1)}, f32[32]{0:T(128)}, u32[]{:S(2)}) copy-start(f32[32]{0:T(128)} %param.19) | copy-start | bytes 388
  156.7 6.6 slice-start.1
  156.7 6.6 copy-start.21
  156.7 54.3 %all-to-all-start.1 = ((bf16[32,1,30,2048]{3,2,1,0:T(8,128)(2,1)}), bf16[32,1,30,2048]{3,2,1,0:T(8,128)(2,1)}, u32[]{:S(2)}, u32[]{:S(2)}) async-start(bf16[32,1,30,2048]{3,2,1,0:T(8,128)(2,1)} %copy.137), calls=%async_computation.1 | async-start | bytes 8388608 | tf_op jit(solution)/shard_map/all_to_all | solution.py:118
  163.3 9.0 %copy-start.18 = (f32[32]{0:T(128)S(1)}, f32[32]{0:T(128)}, u32[]{:S(2)}) copy-start(f32[32]{0:T(128)} %param.18) | copy-start | bytes 388
  253.6 3.8 copy-start.3
  260.1 3.6 copy-start.5
  276.1 94.7 %collective-permute-start = (f32[4,32,64,64]{3,2,1,0:T(8,128)}, f32[4,32,64,64]{3,2,1,0:T(8,128)}, u32[]{:S(2)}, u32[]{:S(2)}) collective-permute-start(f32[4,32,64,64]{3,2,1,0:T(8,128)} %multiply_add_fusion.4), channel_id=1, source_target_pairs={{0,1},{1,2},{2,3},{4,5},{5,6},{6,7},{8,9},{9,10},{10,11},{12,13},{... | collective-permute-start | bytes 6291464 | tf_op jit(solution)/shard_map/while/body/eval_jaxpr/ppermute | solution.py:16
  376.7 93.9 %collective-permute-start = (f32[4,32,64,64]{3,2,1,0:T(8,128)}, f32[4,32,64,64]{3,2,1,0:T(8,128)}, u32[]{:S(2)}, u32[]{:S(2)}) collective-permute-start(f32[4,32,64,64]{3,2,1,0:T(8,128)} %multiply_add_fusion.4), channel_id=1, source_target_pairs={{0,1},{1,2},{2,3},{4,5},{5,6},{6,7},{8,9},{9,10},{10,11},{12,13},{... | collective-permute-start | bytes 6291464 | tf_op jit(solution)/shard_map/while/body/eval_jaxpr/ppermute | solution.py:16
  476.5 93.0 %collective-permute-start = (f32[4,32,64,64]{3,2,1,0:T(8,128)}, f32[4,32,64,64]{3,2,1,0:T(8,128)}, u32[]{:S(2)}, u32[]{:S(2)}) collective-permute-start(f32[4,32,64,64]{3,2,1,0:T(8,128)} %multiply_add_fusion.4), channel_id=1, source_target_pairs={{0,1},{1,2},{2,3},{4,5},{5,6},{6,7},{8,9},{9,10},{10,11},{12,13},{... | collective-permute-start | bytes 6291464 | tf_op jit(solution)/shard_map/while/body/eval_jaxpr/ppermute | solution.py:16
  573.6 4.0 copy-start.15
  573.7 4.0 copy-start.16
  577.7 5.6 copy-start.1
  577.7 5.6 copy-start.17
  583.3 7.7 %copy-start.4 = (bf16[4,1,80,32,64]{2,4,3,0,1:T(8,128)(2,1)S(1)}, bf16[4,1,80,32,64]{2,4,3,0,1:T(8,128)(2,1)}, u32[]{:S(2)}) copy-start(bf16[4,1,80,32,64]{2,4,3,0,1:T(8,128)(2,1)} %copy.186) | copy-start | bytes 3932164
  583.3 7.7 %copy-start.7 = (f32[4,80,32,64]{1,3,2,0:T(8,128)S(1)}, f32[4,80,32,64]{1,3,2,0:T(8,128)}, u32[]{:S(2)}) copy-start(f32[4,80,32,64]{1,3,2,0:T(8,128)} %fusion.63) | copy-start | bytes 7864324
  583.3 7.7 %copy-start.11 = (f32[4,80,32]{1,2,0:T(8,128)S(1)}, f32[4,80,32]{1,2,0:T(8,128)}, u32[]{:S(2)}) copy-start(f32[4,80,32]{1,2,0:T(8,128)} %copy.163) | copy-start | bytes 122884
  583.3 7.7 %copy-start.12 = (f32[4,80,32]{1,2,0:T(8,128)S(1)}, f32[4,80,32]{1,2,0:T(8,128)}, u32[]{:S(2)}) copy-start(f32[4,80,32]{1,2,0:T(8,128)} %copy.164) | copy-start | bytes 122884
  583.4 7.7 %copy-start.14 = (f32[4,80,32]{1,2,0:T(8,128)S(1)}, f32[4,80,32]{1,2,0:T(8,128)}, u32[]{:S(2)}) copy-start(f32[4,80,32]{1,2,0:T(8,128)} %copy.162) | copy-start | bytes 122884
  591.0 8.2 %copy-start.6 = (bf16[4,1,80,32,64]{2,4,3,0,1:T(8,128)(2,1)S(1)}, bf16[4,1,80,32,64]{2,4,3,0,1:T(8,128)(2,1)}, u32[]{:S(2)}) copy-start(bf16[4,1,80,32,64]{2,4,3,0,1:T(8,128)(2,1)} %copy.189) | copy-start | bytes 3932164
  591.0 8.2 %copy-start.8 = (f32[4,80,32,64]{1,3,2,0:T(8,128)S(1)}, f32[4,80,32,64]{1,3,2,0:T(8,128)}, u32[]{:S(2)}) copy-start(f32[4,80,32,64]{1,3,2,0:T(8,128)} %fusion.109) | copy-start | bytes 7864324
  591.0 8.2 %copy-start.9 = (f32[4,80,32]{1,2,0:T(8,128)S(1)}, f32[4,80,32]{1,2,0:T(8,128)}, u32[]{:S(2)}) copy-start(f32[4,80,32]{1,2,0:T(8,128)} %copy.169) | copy-start | bytes 122884
  591.1 8.2 %copy-start.10 = (f32[4,80,32]{1,2,0:T(8,128)S(1)}, f32[4,80,32]{1,2,0:T(8,128)}, u32[]{:S(2)}) copy-start(f32[4,80,32]{1,2,0:T(8,128)} %copy.170) | copy-start | bytes 122884
  591.1 8.2 %copy-start.13 = (f32[4,80,32]{1,2,0:T(8,128)S(1)}, f32[4,80,32]{1,2,0:T(8,128)}, u32[]{:S(2)}) copy-start(f32[4,80,32]{1,2,0:T(8,128)} %copy.168) | copy-start | bytes 122884
  599.2 7.9 %copy-start.2 = (f32[4,1,80,32,64]{2,4,3,0,1:T(8,128)S(1)}, f32[4,1,80,32,64]{2,4,3,0,1:T(8,128)}, u32[]{:S(2)}) copy-start(f32[4,1,80,32,64]{2,4,3,0,1:T(8,128)} %fusion.53) | copy-start | bytes 7864324
  650.1 6.7 %copy-start = (f32[960,2048]{1,0:T(8,128)S(1)}, f32[960,2048]{1,0:T(8,128)}, u32[]{:S(2)}) copy-start(f32[960,2048]{1,0:T(8,128)} %reshape.164) | copy-start | bytes 23592964
  650.1 7.2 %copy-start.22 = (bf16[4,3,80,1024]{3,2,1,0:T(8,128)(2,1)S(1)}, bf16[4,3,80,1024]{3,2,1,0:T(8,128)(2,1)}, u32[]{:S(2)}) copy-start(bf16[4,3,80,1024]{3,2,1,0:T(8,128)(2,1)} %param.12) | copy-start | bytes 5898244
  650.1 7.2 %copy-start.23 = (f32[2048]{0:T(1024)S(1)}, f32[2048]{0:T(1024)}, u32[]{:S(2)}) copy-start(f32[2048]{0:T(1024)} %param.21) | copy-start | bytes 24580
where the time goes:
time: 674 us; the launch traced here: 667 us
  waiting for transfers between devices  343 us (51%)
  local copies, waits for them, and re-layouts  163 us (24%)
  matrix products  100 us (15%)
  other arithmetic  37.3 us (6%)
  starting transfers between devices  22.3 us (3%)
    ppermute x3, waiting for transfers between devices, from_behind(): lax.ppermute(value, axis, [(source, source + steps) for source in range(l...  271 us
    all_to_all x1, waiting for transfers between devices, body(): lax.all_to_all(sending, 'tm', split_axis=1, concat_axis=0, tiled=True)  45.3 us
    dot_general x4, matrix products, local_scan(): jnp.einsum('srh,rhp->shp', weights, signal, precision=lax.Precision.HIGHEST)  38.4 us
    all_to_all x1, waiting for transfers between devices, body(): lax.all_to_all(returned, 'tm', split_axis=0, concat_axis=1, tiled=True)  26.2 us
    another operation x1, local copies, waits for them, and re-layouts, body(): space_out = jnp.stack(finished, axis=1).reshape(-1, DI)  17.9 us
    add x3, other arithmetic, relay_step(): return from_behind(growth * start_state + end_state, 'space', 1)  17.7 us
    unnamed x57, local copies, waits for them, and re-layouts  17 us
    dot_general x3, matrix products, body(): jnp.einsum('fsn,fhpn->fshp', readout_grid[:, row_index].astype(jnp.float3...  15.8 us
  transfers between devices with their start and end apart: 5, of which 5 were waited for; matrix products, arithmetic and copies ran while one was open for 4% of the time, Pallas kernels for 0%

commit v1 on v0

v1 whole, which is shorter than its diff:
```python
import functools

import jax
import jax.numpy as jnp
from jax import lax
from jax.experimental import pallas as pl
from jax.experimental.pallas import tpu as pltpu
from jax.sharding import PartitionSpec as P

D = 1024
HEADS = 32
HEAD_DIM = 64
STATE = 64
DI = 2048
BLK = 16
QUAD = 256
LANES = 128
LOG2E = 1.4426950408889634
TOP = 64.0
GROUPS = (8, 8, 8, 8)
BF = jnp.bfloat16
F32 = jnp.float32
VMEM = 56 * 1024 * 1024


def call(kernel, name, grid, in_specs, out_specs, out_shape, flops, moved, scratch=()):
    return pl.pallas_call(
        kernel,
        name=name,
        grid=grid,
        in_specs=in_specs,
        out_specs=out_specs,
        out_shape=out_shape,
        scratch_shapes=scratch,
        compiler_params=pltpu.CompilerParams(vmem_limit_bytes=VMEM),
        cost_estimate=pl.CostEstimate(flops=flops, bytes_accessed=moved, transcendentals=0),
    )


def dot(a, b):
    return jnp.dot(a, b, preferred_element_type=F32)


def dot_nt(a, b):
    return lax.dot_general(a, b, (((1,), (1,)), ((), ())), preferred_element_type=F32)


def dot_tn(a, b):
    return lax.dot_general(a, b, (((0,), (0,)), ((), ())), preferred_element_type=F32)


def softplus(x):
    return jnp.maximum(x, 0.0) + jnp.log1p(jnp.exp(-jnp.abs(x)))


def split2(v):
    high = v.astype(BF)
    return high, (v - high.astype(F32)).astype(BF)


def full(shape):
    return pl.BlockSpec(shape, lambda *_: (0,) * len(shape))


def arrange_kernel(n, spare, x_ref, o_ref):
    o_ref[:, 0, 0] = x_ref[0].reshape(n, BLK, D)
    if spare:

        @pl.when(pl.program_id(0) == pl.num_programs(0) - 1)
        def _():
            o_ref[n - spare :, 0, 0] = jnp.zeros((spare, BLK, D), BF)


def arrange(tok, n, m):
    fr, npos, _ = tok.shape
    spare = n * m - npos // BLK
    return call(
        functools.partial(arrange_kernel, n, spare),
        "arrange",
        (m, fr),
        [pl.BlockSpec((1, n * BLK, D), lambda h, f: (f, h, 0))],
        pl.BlockSpec((n, 1, 1, BLK, D), lambda h, f: (0, h, f, 0, 0)),
        jax.ShapeDtypeStruct((n, m, fr, BLK, D), BF),
        0,
        4 * fr * npos * D,
    )(tok)


def gate_kernel(x_ref, w_ref, o_ref):
    o_ref[...] = dot(x_ref[...], w_ref[...]).astype(BF)


def gate_proj(flat, w_in):
    rows = flat.shape[0]
    return call(
        gate_kernel,
        "gate_proj",
        (DI // 512,),
        [full((rows, D)), pl.BlockSpec((D, 512), lambda j: (0, j))],
        pl.BlockSpec((rows, 512), lambda j: (0, j)),
        jax.ShapeDtypeStruct((rows, DI), BF),
        2 * rows * D * DI,
        2 * (rows * D + D * DI + rows * DI),
    )(flat, w_in)


def space_prep_kernel(
    npos, x_ref, w_ref, bias_ref, rate_ref, score_ref, cum_ref, row_ref, tail_ref, ecum_ref, b_ref, c_ref, tot_ref
):
    size = score_ref.shape[1]
    proj = dot(x_ref[0], w_ref[...])
    pad = jnp.zeros((size - npos, LANES), F32)
    bc = jnp.concatenate([proj[:, LANES : 2 * LANES].astype(BF).astype(F32), pad], axis=0)
    b = bc[:, :STATE].astype(BF)
    c = bc[:, STATE:].astype(BF)
    step = softplus(proj[:, 2 * LANES :] + bias_ref[...])
    step = jnp.concatenate([step, pad], axis=0)
    dec = step * rate_ref[...]
    ri = lax.broadcasted_iota(jnp.int32, (size, size), 0)
    ci = lax.broadcasted_iota(jnp.int32, (size, size), 1)
    causal = ri >= ci
    cum = jnp.dot(
        causal.astype(F32), dec, precision=lax.Precision.HIGHEST, preferred_element_type=F32
    )
    total = cum[npos - 1 : npos]
    rowterm = jnp.log2(step) - cum
    score_ref[0] = jnp.where(causal, dot_nt(c, b), 0.0)
    cum_ref[0] = cum
    row_ref[0] = rowterm.T[HEADS : 2 * HEADS]
    tail = jnp.exp2(jnp.minimum(total + rowterm, TOP))
    t_hi, t_lo = split2(tail)
    tail_ref[0, 0] = t_hi
    tail_ref[0, 1] = t_lo
    e_hi, e_lo = split2(jnp.exp2(cum))
    ecum_ref[0, 0] = e_hi
    ecum_ref[0, 1] = e_lo
    b_ref[0] = b
    c_ref[0] = c
    tot_ref[0] = total


def space_prep(tok, w_small, bias, rate, size):
    fr, npos, _ = tok.shape

    def per_frame(shape):
        return pl.BlockSpec((1,) + shape, lambda f: (f,) + (0,) * len(shape))

    shapes = [
        ((size, size), F32),
        ((size, LANES), F32),
        ((HEADS, size), F32),
        ((2, size, LANES), BF),
        ((2, size, LANES), BF),
        ((size, STATE), BF),
        ((size, STATE), BF),
        ((1, LANES), F32),
    ]
    return call(
        functools.partial(space_prep_kernel, npos),
        "space_prep",
        (fr,),
        [per_frame((npos, D)), full(w_small.shape), full((1, LANES)), full((1, LANES))],
        [per_frame(s) for s, _ in shapes],
        [jax.ShapeDtypeStruct((fr,) + s, t) for s, t in shapes],
        2 * fr * npos * D * 384,
        6 * 1024 * 1024,
    )(tok, w_small, bias, rate)


def time_prep_kernel(n, m, fr, x_ref, w_ref, bias_ref, rate_ref, score_ref, cum_ref, row_ref):
    proj = dot(x_ref[...], w_ref[...])
    shape = (n, m, fr, 2, 8, LANES)
    q_rows = n * fr * 8
    bc = proj[:, :LANES].astype(BF).astype(F32).reshape(shape)
    raw = proj[:, 2 * LANES :].astype(BF).astype(F32)
    step = softplus(raw + bias_ref[...])
    dec = (step * rate_ref[...]).reshape(shape)
    step = step.reshape(shape)
    ri = lax.broadcasted_iota(jnp.int32, (q_rows, q_rows), 0)
    ci = lax.broadcasted_iota(jnp.int32, (q_rows, q_rows), 1)
    keep = (ri >= ci) & ((ri & 7) == (ci & 7))
    for h in range(m):
        for e in range(2):
            q = 2 * h + e
            running = jnp.zeros((8, LANES), F32)
            parts = []
            for s in range(n):
                for f in range(fr):
                    running = running + dec[s, h, f, e]
                    parts.append(running)
            cum = jnp.concatenate(parts, axis=0)
            bcq = bc[:, h, :, e].reshape(q_rows, LANES)
            b = bcq[:, :STATE].astype(BF)
            c = bcq[:, STATE:].astype(BF)
            score_ref[q] = jnp.where(keep, dot_nt(c, b), 0.0)
            cum_ref[q] = cum
            rowterm = jnp.log2(step[:, h, :, e].reshape(q_rows, LANES)) - cum
            row_ref[q] = rowterm.T[:HEADS]


def time_prep(tok_t, w_small, bias, rate):
    n, m, fr = tok_t.shape[:3]
    rows = n * m * fr * BLK
    q_rows = n * fr * 8
    flat = tok_t.reshape(rows, D)
    return call(
        functools.partial(time_prep_kernel, n, m, fr),
        "time_prep",
        (1,),
        [full((rows, D)), full(w_small.shape), full((1, LANES)), full((1, LANES))],
        [full((2 * m, q_rows, q_rows)), full((2 * m, q_rows, LANES)), full((2 * m, HEADS, q_rows))],
        [
            jax.ShapeDtypeStruct((2 * m, q_rows, q_rows), F32),
            jax.ShapeDtypeStruct((2 * m, q_rows, LANES), F32),
            jax.ShapeDtypeStruct((2 * m, HEADS, q_rows), F32),
        ],
        2 * rows * D * 384,
        6 * 1024 * 1024,
    )(flat, w_small, bias, rate)


def head_pair(score, cum, row, x_pair, rows_in):
    lane = lax.broadcasted_iota(jnp.int32, (1, LANES), 1)
    left = jnp.where(lane < HEAD_DIM, 1.0, 0.0).astype(BF)
    halves = (x_pair * left, x_pair * (1 - left))
    out = []
    for i in range(rows_in // LANES):
        lo, hi = i * LANES, (i + 1) * LANES
        pieces = []
        for k in range(2):
            col = jnp.broadcast_to(cum[k][lo:hi], (LANES, LANES))
            for j in range(i + 1):
                span = col + row[k][:, j * LANES : (j + 1) * LANES]
                weight = jnp.exp2(jnp.minimum(span, TOP)) * score[lo:hi, j * LANES : (j + 1) * LANES]
                pieces.append(weight.astype(BF))
        left_side = jnp.concatenate(pieces, axis=1)
        right_side = jnp.concatenate([halves[0][:hi], halves[1][:hi]], axis=0)
        out.append(dot(left_side, right_side))
    return jnp.concatenate(out, axis=0)


def time_scan_kernel(n, m, fr, head0, x_ref, w_ref, score_ref, cum_ref, row_ref, skip_ref, o_ref):
    base = head0 + 4 * pl.program_id(0)
    q_rows = n * fr * 8
    x = dot(x_ref[...], w_ref[...]).astype(BF).astype(F32)
    x = x.reshape(n, m, fr, 2, 8, QUAD)
    for h in range(m):
        ys = []
        for e in range(2):
            q = 2 * h + e
            xq = x[:, h, :, e].reshape(q_rows, QUAD)
            xb = xq.astype(BF)
            cum = pltpu.roll(cum_ref[q], LANES - base, 1)
            y = []
            for p in range(2):
                a = p * LANES
                heads = (2 * p, 2 * p + 1)
                y.append(
                    head_pair(
                        score_ref.at[q],
                        [cum[:, k : k + 1] for k in heads],
                        [row_ref[q, pl.ds(base + k, 1), :] for k in heads],
                        xb[:, a : a + LANES],
                        q_rows,
                    )
                )
            y = jnp.concatenate(y, axis=1) + skip_ref[...] * xq
            ys.append(y.reshape(n, fr, 8, QUAD))
        o_ref[:, h] = jnp.concatenate(ys, axis=2).astype(BF)


def time_scan(tok_t, w_in, prep, skip, head0, heads):
    n, m, fr = tok_t.shape[:3]
    rows = n * m * fr * BLK
    q_rows = n * fr * 8
    first = (DI + head0 * HEAD_DIM) // QUAD
    own = head0 * HEAD_DIM // QUAD
    cols = heads * HEAD_DIM
    return call(
        functools.partial(time_scan_kernel, n, m, fr, head0),
        "time_scan",
        (heads // 4,),
        [
            full((rows, D)),
            pl.BlockSpec((D, QUAD), lambda j: (0, first + j)),
            full((2 * m, q_rows, q_rows)),
            full((2 * m, q_rows, LANES)),
            full((2 * m, HEADS, q_rows)),
            pl.BlockSpec((1, QUAD), lambda j: (0, own + j)),
        ],
        pl.BlockSpec((n, m, fr, BLK, QUAD), lambda j: (0, 0, 0, 0, j)),
        jax.ShapeDtypeStruct((n, m, fr, BLK, cols), BF),
        2 * rows * D * cols + 4 * rows * q_rows * cols,
        2 * (rows * D + D * cols + rows * cols) + 2 * 1024 * 1024,
    )(tok_t.reshape(rows, D), w_in, *prep, skip)


def frame_rows(ref, frame):
    n, m, _, _, cols = ref.shape
    return jnp.concatenate([ref[:, h, frame].reshape(n * BLK, cols) for h in range(m)], axis=0)


def end_state_kernel(x_ref, tail_ref, b_ref, spread_ref, o_ref):
    spread = spread_ref[...]
    for f in range(x_ref.shape[2]):
        x = frame_rows(x_ref, f).astype(F32)
        wide = dot(tail_ref[f, 0], spread) + dot(tail_ref[f, 1], spread)
        o_ref[f] = dot_tn(b_ref[f], (x * wide).astype(BF)).astype(BF)


def end_state(time_out, tail, b, spread, head0):
    n, m, fr, _, cols = time_out.shape
    size = b.shape[1]
    own = head0 * HEAD_DIM // QUAD
    return call(
        end_state_kernel,
        "end_state",
        (cols // QUAD,),
        [
            pl.BlockSpec((n, m, fr, BLK, QUAD), lambda j: (0, 0, 0, 0, j)),
            full(tail.shape),
            full(b.shape),
            pl.BlockSpec((LANES, QUAD), lambda j: (0, own + j)),
        ],
        pl.BlockSpec((fr, STATE, QUAD), lambda j: (0, 0, j)),
        jax.ShapeDtypeStruct((fr, STATE, cols), BF),
        2 * fr * size * cols * (STATE + 2 * LANES),
        2 * fr * size * cols + 1024 * 1024,
    )(time_out, tail, b, spread)


def local_kernel(head0, npos, x_ref, score_ref, cum_ref, row_ref, skip_ref, o_ref):
    base = head0 + 4 * pl.program_id(1)
    size = score_ref.shape[1]
    xb = frame_rows(x_ref, 0)
    cum = pltpu.roll(cum_ref[0], LANES - HEADS - base, 1)
    y = []
    for p in range(2):
        a = p * LANES
        heads = (2 * p, 2 * p + 1)
        y.append(
            head_pair(
                score_ref.at[0],
                [cum[:, k : k + 1] for k in heads],
                [row_ref[0, pl.ds(base + k, 1), :] for k in heads],
                xb[:, a : a + LANES],
                size,
            )
        )
    y = jnp.concatenate(y, axis=1) + skip_ref[...] * xb.astype(F32)
    o_ref[0] = y[:npos]


def local_scan(time_out, score, cum, row, skip, head0, npos):
    n, m, fr, _, cols = time_out.shape
    size = score.shape[1]
    own = head0 * HEAD_DIM // QUAD
    return call(
        functools.partial(local_kernel, head0, npos),
        "local_scan",
        (fr, cols // QUAD),
        [
            pl.BlockSpec((n, m, 1, BLK, QUAD), lambda f, j: (0, 0, f, 0, j)),
            pl.BlockSpec((1, size, size), lambda f, j: (f, 0, 0)),
            pl.BlockSpec((1, size, LANES), lambda f, j: (f, 0, 0)),
            pl.BlockSpec((1, HEADS, size), lambda f, j: (f, 0, 0)),
            pl.BlockSpec((1, QUAD), lambda f, j: (0, own + j)),
        ],
        pl.BlockSpec((1, npos, QUAD), lambda f, j: (f, 0, j)),
        jax.ShapeDtypeStruct((fr, npos, cols), F32),
        4 * fr * size * size * cols,
        6 * fr * size * cols + 2 * 1024 * 1024,
    )(time_out, score, cum, row, skip)


def gated_of(npos, local_ref, z_ref, ecum_ref, c_ref, spread_ref, prev_ref, states):
    state = states[0][0].astype(F32)
    if len(states) > 1:
        state = state + states[1][0].astype(F32) + prev_ref[0] * states[2][0].astype(F32)
    carried = dot(c_ref[0], state.astype(BF))[:npos]
    spread = spread_ref[...]
    wide = (dot(ecum_ref[0, 0], spread) + dot(ecum_ref[0, 1], spread))[:npos]
    z = z_ref[0].astype(F32)
    return (local_ref[0] + wide * carried) * (z * jax.nn.sigmoid(z))


def lane_sums(v):
    return sum(v[:, a : a + LANES] for a in range(0, v.shape[1], LANES))


def finish_kernel(npos, local_ref, z_ref, ecum_ref, c_ref, spread_ref, prev_ref, gain_ref, *rest):
    *states, o_ref, sq_ref = rest
    gated = gated_of(npos, local_ref, z_ref, ecum_ref, c_ref, spread_ref, prev_ref, states)
    o_ref[0] = (gated * gain_ref[...]).astype(BF)
    part = lane_sums(gated * gated)

    @pl.when(pl.program_id(1) == 0)
    def _():
        sq_ref[0] = part

    @pl.when(pl.program_id(1) > 0)
    def _():
        sq_ref[0] = sq_ref[0] + part


def finish(local, gate, ecum, c, spread, prev, gain, states, head0):
    fr, npos, cols = local.shape
    size = c.shape[1]
    own = head0 * HEAD_DIM // QUAD
    state_spec = pl.BlockSpec((1, STATE, QUAD), lambda f, j: (f, 0, j))
    return call(
        functools.partial(finish_kernel, npos),
        "finish",
        (fr, cols // QUAD),
        [
            pl.BlockSpec((1, npos, QUAD), lambda f, j: (f, 0, j)),
            pl.BlockSpec((1, npos, QUAD), lambda f, j: (f, 0, own + j)),
            pl.BlockSpec((1, 2, size, LANES), lambda f, j: (f, 0, 0, 0)),
            pl.BlockSpec((1, size, STATE), lambda f, j: (f, 0, 0)),
            pl.BlockSpec((LANES, QUAD), lambda f, j: (0, own + j)),
            pl.BlockSpec((1, 1, QUAD), lambda f, j: (f, 0, own + j)),
            pl.BlockSpec((1, QUAD), lambda f, j: (0, own + j)),
        ]
        + [state_spec] * len(states),
        [
            pl.BlockSpec((1, npos, QUAD), lambda f, j: (f, 0, j)),
            pl.BlockSpec((1, npos, LANES), lambda f, j: (f, 0, 0)),
        ],
        [
            jax.ShapeDtypeStruct((fr, npos, cols), BF),
            jax.ShapeDtypeStruct((fr, npos, LANES), F32),
        ],
        2 * fr * size * cols * (STATE + 2 * LANES),
        8 * fr * size * cols + 1024 * 1024,
    )(local, gate, ecum, c, spread, prev, gain, *states)


def project_kernel(offsets, w_ref, *rest):
    count = len(offsets)
    gated, squares, (o_ref, sq_ref) = rest[:count], rest[count : 2 * count], rest[2 * count :]
    total = None
    for ref, (lo, hi) in zip(gated, offsets):
        part = dot(ref[0], w_ref[lo:hi])
        total = part if total is None else total + part
    o_ref[0] = total
    sq_ref[0] = sum(ref[0] for ref in squares)


def project(gated, squares, w_out, offsets):
    fr, npos, _ = gated[0].shape
    cols = sum(g.shape[2] for g in gated)
    return call(
        functools.partial(project_kernel, offsets),
        "project",
        (fr,),
        [full(w_out.shape)]
        + [pl.BlockSpec((1, npos, g.shape[2]), lambda f: (f, 0, 0)) for g in gated]
        + [pl.BlockSpec((1, npos, LANES), lambda f: (f, 0, 0)) for _ in squares],
        [
            pl.BlockSpec((1, npos, D), lambda f: (f, 0, 0)),
            pl.BlockSpec((1, npos, LANES), lambda f: (f, 0, 0)),
        ],
        [
            jax.ShapeDtypeStruct((fr, npos, D), F32),
            jax.ShapeDtypeStruct((fr, npos, LANES), F32),
        ],
        2 * fr * npos * cols * D,
        2 * (fr * npos * cols + cols * D) + 4 * fr * npos * D,
    )(w_out, *gated, *squares)


def last_kernel(npos, local_ref, z_ref, ecum_ref, c_ref, spread_ref, prev_ref, gain_ref, w_ref, acc_ref, sq_ref, tok_ref, *rest):
    *states, o_ref = rest
    gated = gated_of(npos, local_ref, z_ref, ecum_ref, c_ref, spread_ref, prev_ref, states)
    squares = sq_ref[0] + lane_sums(gated * gated)
    mean = jnp.sum(squares, axis=1, keepdims=True) * (1.0 / DI)
    inv_scale = lax.rsqrt(mean + 1e-05)
    total = acc_ref[0] + dot((gated * gain_ref[...]).astype(BF), w_ref[...])
    o_ref[0] = (total * inv_scale + tok_ref[0].astype(F32)).astype(BF)


def last(local, gate, ecum, c, spread, prev, gain, w_out, acc, squares, tok, states, head0):
    fr, npos, cols = local.shape
    size = c.shape[1]
    own = head0 * HEAD_DIM // cols
    per_frame = lambda f: (f, 0, 0)
    return call(
        functools.partial(last_kernel, npos),
        "last",
        (fr,),
        [
            pl.BlockSpec((1, npos, cols), per_frame),
            pl.BlockSpec((1, npos, cols), lambda f: (f, 0, own)),
            pl.BlockSpec((1, 2, size, LANES), lambda f: (f, 0, 0, 0)),
            pl.BlockSpec((1, size, STATE), per_frame),
            pl.BlockSpec((LANES, cols), lambda f: (0, own)),
            pl.BlockSpec((1, 1, cols), lambda f: (f, 0, own)),
            pl.BlockSpec((1, cols), lambda f: (0, own)),
            pl.BlockSpec((cols, D), lambda f: (own, 0)),
            pl.BlockSpec((1, npos, D), per_frame),
            pl.BlockSpec((1, npos, LANES), per_frame),
            pl.BlockSpec((1, npos, D), per_frame),
        ]
        + [pl.BlockSpec((1, STATE, cols), per_frame)] * len(states),
        pl.BlockSpec((1, npos, D), per_frame),
        jax.ShapeDtypeStruct((fr, npos, D), BF),
        2 * fr * npos * cols * D,
        8 * fr * npos * D,
    )(local, gate, ecum, c, spread, prev, gain, w_out, acc, squares, tok, *states)


def relay(end, growth):
    count = lax.axis_size("space")
    if count == 4:
        first = lax.ppermute(end, "space", [(0, 1), (2, 3)])
        joined = (end.astype(F32) + growth * first.astype(F32)).astype(BF)
        second = lax.ppermute(joined, "space", [(1, 2)])
        third = lax.ppermute(joined, "space", [(1, 3)])
        return [first, second, third]
    start = jnp.zeros_like(end)
    for _ in range(count - 1):
        moving = (end.astype(F32) + growth * start.astype(F32)).astype(BF)
        start = lax.ppermute(moving, "space", [(i, i + 1) for i in range(count - 1)])
    return [start]


def body(
    tokens, w_in, w_out, a_log_time, a_log_space, dt_bias_time, dt_bias_space, skip_time, skip_space, norm_gain
):
    fr, rows_dev, cols_dev, _ = tokens.shape
    n = lax.axis_size("tm")
    npos = rows_dev * cols_dev
    m = -(-(npos // BLK) // n)
    size = m * n * BLK
    tok = tokens.reshape(fr, npos, D)
    flat = tokens.reshape(fr * npos, D)

    tok_t = lax.all_to_all(arrange(tok, n, m), "tm", split_axis=0, concat_axis=0, tiled=True)

    base = 2 * DI
    w_small = jnp.pad(w_in[:, base:], ((0, 0), (0, 64)))
    pad = jnp.zeros((LANES - 2 * HEADS,), F32)
    bias = jnp.concatenate([dt_bias_time, dt_bias_space, pad])[None]
    rate = jnp.concatenate([-jnp.exp(a_log_time) * LOG2E, -jnp.exp(a_log_space) * LOG2E, pad])[None]
    skip_t = jnp.repeat(skip_time, HEAD_DIM)[None]
    skip_s = jnp.repeat(skip_space, HEAD_DIM)[None]
    gain = norm_gain[None]
    lane_head = jnp.arange(LANES)[:, None] - HEADS
    spread = (lane_head == jnp.arange(DI)[None, :] // HEAD_DIM).astype(BF)

    gate = gate_proj(flat, w_in).reshape(fr, npos, DI)
    score, cum, row, tail, ecum, b, c, total = space_prep(tok, w_small, bias, rate, size)
    growth = jnp.repeat(jnp.exp2(total[:, :, HEADS : 2 * HEADS]), HEAD_DIM, axis=2)
    count = lax.axis_size("space")
    prev = lax.ppermute(growth, "space", [(i, i + 1) for i in range(count - 1)])

    prep = time_prep(tok_t, w_small, bias, rate)
    starts = [sum(GROUPS[:i]) for i in range(len(GROUPS))]
    returned = []
    for head0, heads in zip(starts, GROUPS):
        out = time_scan(tok_t, w_in, prep, skip_t, head0, heads)
        returned.append(lax.all_to_all(out, "tm", split_axis=0, concat_axis=0, tiled=True))
    gated, squares, offsets = [], [], []
    for index, (head0, heads) in enumerate(zip(starts, GROUPS)):
        arrived = returned[index]
        lo, hi = head0 * HEAD_DIM, (head0 + heads) * HEAD_DIM
        states = relay(end_state(arrived, tail, b, spread, head0), growth[:, :, lo:hi])
        local = local_scan(arrived, score, cum, row, skip_s, head0, npos)
        if index < len(GROUPS) - 1:
            g, sq = finish(local, gate, ecum, c, spread, prev, gain, states, head0)
            gated.append(g)
            squares.append(sq)
            offsets.append((lo, hi))
        else:
            acc, sq = project(gated, squares, w_out, offsets)
            out = last(
                local, gate, ecum, c, spread, prev, gain, w_out, acc, sq, tok, states, head0
            )
    return out.reshape(tokens.shape)


def solution(mesh):
    placed = (P("tm", "space", None, None), P(), P(), P(), P(), P(), P(), P(), P(), P())
    return jax.shard_map(
        body, mesh=mesh, in_specs=placed, out_specs=P("tm", "space", None, None), check_vma=False
    )
```

time: 674 us -> 244 us (0.36)
  waiting for transfers between devices: 343 us -> 37.4 us
  local copies, waits for them, and re-layouts: 163 us -> 20.7 us
  Pallas kernels: 0 us -> 140 us
  matrix products: 100 us -> 0 us
  other arithmetic: 37.3 us -> 2.68 us
  starting transfers between devices: 22.3 us -> 40.4 us
    ppermute x3 -> x13, waiting for transfers between devices: 271 us -> 14.4 us  [the longest x4 14.4 us: relay(): second = lax.ppermute(joined, 'space', [(1, 2)])]
    pallas_call x0 -> x21, Pallas kernels: none -> 140 us  [the longest x4 31.1 us: local_scan(): call(functools.partial(local_kernel, head0, npos), 'local_scan', (fr, col...]
    dot_general x20 -> x0, matrix products: 100 us -> none  [the longest x4 38.4 us: local_scan(): jnp.einsum('srh,rhp->shp', weights, signal, precision=lax.Precision.HIGHEST)]
    reshape x6 -> x0, local copies, waits for them, and re-layouts: 65.8 us -> none  [the longest x2 15 us: body(): sending = time_pack.reshape(fr_dev, n_tm, -1, time_pack.shape[-1])]
    all_to_all x2 -> x5, waiting for transfers between devices: 71.5 us -> 22.9 us  [the longest x4 13.6 us: body(): lax.all_to_all(out, 'tm', split_axis=0, concat_axis=0, tiled=True)]
    another operation x6 -> x2, local copies, waits for them, and re-layouts: 21.1 us -> 1.36 us  [the longest x1 0.68 us: body(): skip_s = jnp.repeat(skip_space, HEAD_DIM)[None]]
    slice x9 -> x3, local copies, waits for them, and re-layouts: 19.7 us -> 1.12 us  [the longest x2 1.11 us: body(): w_small = jnp.pad(w_in[:, base:], ((0, 0), (0, 64)))]
    add x3 -> x0, other arithmetic: 17.7 us -> none  [relay_step(): return from_behind(growth * start_state + end_state, 'space', 1)]
  transfers between devices with their start and end apart: 5 -> 18, of which waited for: 5 -> 6; matrix products, arithmetic and copies ran while one was open for 4% -> 7% of each run, Pallas kernels for 0% -> 47%
where the time goes in v1:
time: 244 us; the launch traced here: 242 us
  Pallas kernels  140 us (57%)
  starting transfers between devices  40.4 us (17%)
  waiting for transfers between devices  37.4 us (15%)
  local copies, waits for them, and re-layouts  20.7 us (8%)
  other arithmetic  2.68 us (1%)
    pallas_call x4, Pallas kernels, local_scan(): call(functools.partial(local_kernel, head0, npos), 'local_scan', (fr, col...  31.1 us
    pallas_call x4, Pallas kernels, time_scan(): call(functools.partial(time_scan_kernel, n, m, fr, head0), 'time_scan', (...  28.5 us
    pallas_call x3, Pallas kernels, finish(): call(functools.partial(finish_kernel, npos), 'finish', (fr, cols // QUAD)...  21.6 us
    all_to_all x4, starting transfers between devices, body(): lax.all_to_all(out, 'tm', split_axis=0, concat_axis=0, tiled=True)  19.2 us
    pallas_call x4, Pallas kernels, end_state(): call(end_state_kernel, 'end_state', (cols // QUAD,), [pl.BlockSpec((n, m,...  17.7 us
    unnamed x61, local copies, waits for them, and re-layouts  16.9 us
    ppermute x4, waiting for transfers between devices, relay(): second = lax.ppermute(joined, 'space', [(1, 2)])  14.4 us
    all_to_all x4, waiting for transfers between devices, body(): lax.all_to_all(out, 'tm', split_axis=0, concat_axis=0, tiled=True)  13.6 us
  transfers between devices with their start and end apart: 18, of which 6 were waited for; matrix products, arithmetic and copies ran while one was open for 7% of the time, Pallas kernels for 47%

profile of v1, /device:TPU:18, one launch (start us, length us, event | category | flops | bytes accessed | tf_op | source)
XLA Modules:
  0.0 241.6 jit_solution(9506021113653474107)
XLA Ops:
  0.0 5.7 %arrange.1 = bf16[8,2,4,16,1024]{4,3,2,1,0:T(8,128)(2,1)} custom-call(bf16[4,240,1024]{2,1,0:T(8,128)(2,1)} %bitcast.32), custom_call_target="tpu_custom_call" | custom-call | bytes 3932160 | tf_op jit(solution)/shard_map/arrange/pallas_call | solution.py:77
  5.7 4.4 %all-to-all-start = ((bf16[8,2,4,16,1024]{4,3,2,1,0:T(8,128)(2,1)}), bf16[8,2,4,16,1024]{4,3,2,1,0:T(8,128)(2,1)S(1)}, u32[]{:S(2)}, u32[]{:S(2)}) async-start(bf16[8,2,4,16,1024]{4,3,2,1,0:T(8,128)(2,1)} %arrange.1), calls=%async_computation | async-start | bytes 4194304 | tf_op jit(solution)/shard_map/all_to_all | solution.py:538
  10.8 12.2 %copy.12.w_ref = bf16[1024,4416]{1,0:T(8,128)(2,1)} copy(bf16[1024,4416]{0,1:T(8,128)(2,1)} %param.11) | data formatting | bytes 18087936 | tf_op args[1]
  23.0 1.1 slice-done
  24.2 1.0 pad.4.w_ref
  25.8 9.4 %all-to-all-done = bf16[8,2,4,16,1024]{4,3,2,1,0:T(8,128)(2,1)S(1)} async-done(((bf16[8,2,4,16,1024]{4,3,2,1,0:T(8,128)(2,1)}), bf16[8,2,4,16,1024]{4,3,2,1,0:T(8,128)(2,1)S(1)}, u32[]{:S(2)}, u32[]{:S(2)}) %all-to-all-start) | async-done | bytes 2097184 | tf_op jit(solution)/shard_map/all_to_all | solution.py:538
  35.2 1.3 copy-done
  36.5 4.5 %time_prep.1 = (f32[4,256,256]{2,1,0:T(8,128)}, f32[4,256,128]{2,1,0:T(8,128)}, f32[4,32,256]{2,1,0:T(8,128)}) custom-call(bf16[1024,1024]{1,0:T(8,128)(2,1)} %bitcast.27, bf16[1024,384]{1,0:T(8,128)(2,1)} %pad.4.w_ref, f32[1,128]{1,0:T(1,128)} %get-tuple-element.48.bias_ref, f32[1,128]{1,0:T(1,128)} %get-tuple-element.47.rate_ref), custom_call_target="tpu_custom_call" | custom-call | flops 805306368 | bytes 6291456 | tf_op jit(solution)/shard_map/time_prep/pallas_call | solution.py:206
  41.0 7.1 %time_scan.7 = bf16[8,2,4,16,512]{4,3,2,1,0:T(8,128)(2,1)} custom-call(bf16[1024,1024]{1,0:T(8,128)(2,1)} %bitcast.28, bf16[1024,4416]{1,0:T(8,128)(2,1)} %copy.12.w_ref, f32[4,256,256]{2,1,0:T(8,128)} %get-tuple-element.24.score_ref, f32[4,256,128]{2,1,0:T(8,128)} %get-tuple-element.25.cum_ref, f32[4,32,256]{2,1,0:T(8,128)} %get-tuple-element.26.row_ref, ...), custom_call_target="tpu_custom_call" | custom-call | flops 1610612736 | bytes 6291456 | tf_op jit(solution)/shard_map/time_scan/pallas_call | solution.py:279
  48.1 5.0 %all-to-all-start.4 = ((bf16[8,2,4,16,512]{4,3,2,1,0:T(8,128)(2,1)}), bf16[8,2,4,16,512]{4,3,2,1,0:T(8,128)(2,1)S(1)}, u32[]{:S(2)}, u32[]{:S(2)}) async-start(bf16[8,2,4,16,512]{4,3,2,1,0:T(8,128)(2,1)} %time_scan.7), calls=%async_computation.4 | async-start | bytes 2097152 | tf_op jit(solution)/shard_map/all_to_all | solution.py:562
  53.1 7.1 %time_scan.6 = bf16[8,2,4,16,512]{4,3,2,1,0:T(8,128)(2,1)} custom-call(bf16[1024,1024]{1,0:T(8,128)(2,1)} %bitcast.29, bf16[1024,4416]{1,0:T(8,128)(2,1)} %copy.12.w_ref, f32[4,256,256]{2,1,0:T(8,128)} %get-tuple-element.24.score_ref, f32[4,256,128]{2,1,0:T(8,128)} %get-tuple-element.25.cum_ref, f32[4,32,256]{2,1,0:T(8,128)} %get-tuple-element.26.row_ref, ...), custom_call_target="tpu_custom_call" | custom-call | flops 1610612736 | bytes 6291456 | tf_op jit(solution)/shard_map/time_scan/pallas_call | solution.py:279
  60.2 6.8 %all-to-all-done.4.x_ref = bf16[8,2,4,16,512]{4,3,2,1,0:T(8,128)(2,1)S(1)} async-done(((bf16[8,2,4,16,512]{4,3,2,1,0:T(8,128)(2,1)}), bf16[8,2,4,16,512]{4,3,2,1,0:T(8,128)(2,1)S(1)}, u32[]{:S(2)}, u32[]{:S(2)}) %all-to-all-start.4) | async-done | bytes 1048608 | tf_op jit(solution)/shard_map/all_to_all | solution.py:562
  67.0 5.0 %all-to-all-start.3 = ((bf16[8,2,4,16,512]{4,3,2,1,0:T(8,128)(2,1)}), bf16[8,2,4,16,512]{4,3,2,1,0:T(8,128)(2,1)S(1)}, u32[]{:S(2)}, u32[]{:S(2)}) async-start(bf16[8,2,4,16,512]{4,3,2,1,0:T(8,128)(2,1)} %time_scan.6), calls=%async_computation.3 | async-start | bytes 2097152 | tf_op jit(solution)/shard_map/all_to_all | solution.py:562
  72.0 7.1 %time_scan.5 = bf16[8,2,4,16,512]{4,3,2,1,0:T(8,128)(2,1)} custom-call(bf16[1024,1024]{1,0:T(8,128)(2,1)} %bitcast.30, bf16[1024,4416]{1,0:T(8,128)(2,1)} %copy.12.w_ref, f32[4,256,256]{2,1,0:T(8,128)} %get-tuple-element.24.score_ref, f32[4,256,128]{2,1,0:T(8,128)} %get-tuple-element.25.cum_ref, f32[4,32,256]{2,1,0:T(8,128)} %get-tuple-element.26.row_ref, ...), custom_call_target="tpu_custom_call" | custom-call | flops 1610612736 | bytes 6291456 | tf_op jit(solution)/shard_map/time_scan/pallas_call | solution.py:279
  79.1 6.8 %all-to-all-done.3.x_ref = bf16[8,2,4,16,512]{4,3,2,1,0:T(8,128)(2,1)S(1)} async-done(((bf16[8,2,4,16,512]{4,3,2,1,0:T(8,128)(2,1)}), bf16[8,2,4,16,512]{4,3,2,1,0:T(8,128)(2,1)S(1)}, u32[]{:S(2)}, u32[]{:S(2)}) %all-to-all-start.3) | async-done | bytes 1048608 | tf_op jit(solution)/shard_map/all_to_all | solution.py:562
  85.9 5.0 %all-to-all-start.2 = ((bf16[8,2,4,16,512]{4,3,2,1,0:T(8,128)(2,1)}), bf16[8,2,4,16,512]{4,3,2,1,0:T(8,128)(2,1)S(1)}, u32[]{:S(2)}, u32[]{:S(2)}) async-start(bf16[8,2,4,16,512]{4,3,2,1,0:T(8,128)(2,1)} %time_scan.5), calls=%async_computation.2 | async-start | bytes 2097152 | tf_op jit(solution)/shard_map/all_to_all | solution.py:562
  90.9 6.4 %space_prep.1 = (f32[4,256,256]{2,1,0:T(8,128)}, f32[4,256,128]{2,1,0:T(8,128)}, f32[4,32,256]{2,1,0:T(8,128)}, bf16[4,2,256,128]{3,2,1,0:T(8,128)(2,1)}, bf16[4...) custom-call(bf16[4,240,1024]{2,1,0:T(8,128)(2,1)} %bitcast.33, ...), custom_call_target="tpu_custom_call" | custom-call | flops 754974720 | bytes 6291456 | tf_op jit(solution)/shard_map/space_prep/pallas_call | solution.py:158
  98.3 3.5 %collective-permute-start = (f32[4,1,2048]{2,1,0:T(1,128)S(1)}, f32[4,1,2048]{2,1,0:T(1,128)S(1)}, u32[]{:S(2)}, u32[]{:S(2)}) collective-permute-start(f32[4,1,2048]{2,1,0:T(1,128)S(1)} %broadcast_in_dim.31), channel_id=1, source_target_pairs={{0,1},{1,2},{2,3},{4,5},{5,6},{6,7},{8,9},{9,10},{10,11},{12,13},{... | collective-permute-start | bytes 98312 | tf_op jit(solution)/shard_map/ppermute | solution.py:555
  102.6 7.1 %time_scan.4 = bf16[8,2,4,16,512]{4,3,2,1,0:T(8,128)(2,1)} custom-call(bf16[1024,1024]{1,0:T(8,128)(2,1)} %bitcast.31, bf16[1024,4416]{1,0:T(8,128)(2,1)} %copy.12.w_ref, f32[4,256,256]{2,1,0:T(8,128)} %get-tuple-element.24.score_ref, f32[4,256,128]{2,1,0:T(8,128)} %get-tuple-element.25.cum_ref, f32[4,32,256]{2,1,0:T(8,128)} %get-tuple-element.26.row_ref, ...), custom_call_target="tpu_custom_call" | custom-call | flops 1610612736 | bytes 6291456 | tf_op jit(solution)/shard_map/time_scan/pallas_call | solution.py:279
  109.7 4.2 %all-to-all-start.1 = ((bf16[8,2,4,16,512]{4,3,2,1,0:T(8,128)(2,1)}), bf16[8,2,4,16,512]{4,3,2,1,0:T(8,128)(2,1)S(1)}, u32[]{:S(2)}, u32[]{:S(2)}) async-start(bf16[8,2,4,16,512]{4,3,2,1,0:T(8,128)(2,1)} %time_scan.4), calls=%async_computation.1 | async-start | bytes 2097152 | tf_op jit(solution)/shard_map/all_to_all | solution.py:562
  113.9 8.1 %gate_proj.1 = bf16[960,2048]{1,0:T(8,128)(2,1)} custom-call(bf16[960,1024]{1,0:T(8,128)(2,1)} %bitcast.34, bf16[1024,4416]{1,0:T(8,128)(2,1)} %copy.12.w_ref), custom_call_target="tpu_custom_call" | custom-call | flops 4026531840 | bytes 10092544 | tf_op jit(solution)/shard_map/gate_proj/pallas_call | solution.py:95
  122.0 0.9 compare_convert_fusion.spread_ref
  123.0 4.4 %end_state.4 = bf16[4,64,512]{2,1,0:T(8,128)(2,1)} custom-call(bf16[8,2,4,16,512]{4,3,2,1,0:T(8,128)(2,1)} %copy-done.3, bf16[4,2,256,128]{3,2,1,0:T(8,128)(2,1)} %get-tuple-element.33.tail_ref, bf16[4,256,64]{2,1,0:T(8,128)(2,1)} %get-tuple-element.34.b_ref, bf16[128,2048]{1,0:T(8,128)(2,1)} %compare_convert_fusion.spread_ref), custom_call_target="tpu_custom_call" | custom-call | flops 335544320 | bytes 2097152 | tf_op jit(solution)/shard_map/end_state/pallas_call | solution.py:315
  127.4 1.5 collective-permute-start.1
  128.9 4.4 %end_state.5 = bf16[4,64,512]{2,1,0:T(8,128)(2,1)} custom-call(bf16[8,2,4,16,512]{4,3,2,1,0:T(8,128)(2,1)} %copy-done.2, bf16[4,2,256,128]{3,2,1,0:T(8,128)(2,1)} %get-tuple-element.33.tail_ref, bf16[4,256,64]{2,1,0:T(8,128)(2,1)} %get-tuple-element.34.b_ref, bf16[128,2048]{1,0:T(8,128)(2,1)} %compare_convert_fusion.spread_ref), custom_call_target="tpu_custom_call" | custom-call | flops 335544320 | bytes 2097152 | tf_op jit(solution)/shard_map/end_state/pallas_call | solution.py:315
  133.3 1.3 collective-permute-start.4
  134.6 4.4 %end_state.6 = bf16[4,64,512]{2,1,0:T(8,128)(2,1)} custom-call(bf16[8,2,4,16,512]{4,3,2,1,0:T(8,128)(2,1)} %copy-done.1, bf16[4,2,256,128]{3,2,1,0:T(8,128)(2,1)} %get-tuple-element.33.tail_ref, bf16[4,256,64]{2,1,0:T(8,128)(2,1)} %get-tuple-element.34.b_ref, bf16[128,2048]{1,0:T(8,128)(2,1)} %compare_convert_fusion.spread_ref), custom_call_target="tpu_custom_call" | custom-call | flops 335544320 | bytes 2097152 | tf_op jit(solution)/shard_map/end_state/pallas_call | solution.py:315
  139.1 1.3 collective-permute-start.7
  140.4 1.0 copy-done.4
  141.4 4.4 %end_state.7 = bf16[4,64,512]{2,1,0:T(8,128)(2,1)} custom-call(bf16[8,2,4,16,512]{4,3,2,1,0:T(8,128)(2,1)} %copy-done.4, bf16[4,2,256,128]{3,2,1,0:T(8,128)(2,1)} %get-tuple-element.33.tail_ref, bf16[4,256,64]{2,1,0:T(8,128)(2,1)} %get-tuple-element.34.b_ref, bf16[128,2048]{1,0:T(8,128)(2,1)} %compare_convert_fusion.spread_ref), custom_call_target="tpu_custom_call" | custom-call | flops 335544320 | bytes 2097152 | tf_op jit(solution)/shard_map/end_state/pallas_call | solution.py:315
  145.8 1.3 collective-permute-start.10
  147.1 7.7 %local_scan.5.local_ref = f32[4,240,512]{2,1,0:T(8,128)} custom-call(bf16[8,2,4,16,512]{4,3,2,1,0:T(8,128)(2,1)} %copy-done.3, f32[4,256,256]{2,1,0:T(8,128)} %get-tuple-element.27.score_ref, f32[4,256,128]{2,1,0:T(8,128)} %get-tuple-element.28.cum_ref, f32[4,32,256]{2,1,0:T(8,128)} %get-tuple-element.29.row_ref, f32[1,2048]{1,0:T(1,128)} %broadcast_in_dim_reshape.7.skip_ref), custom_call_target="tpu_custom_call" | custom-call | flops 536870912 | bytes 5242880 | tf_op jit(solution)/shard_map/local_scan/pallas_call | solution.py:358
  154.8 7.8 %local_scan.6.local_ref = f32[4,240,512]{2,1,0:T(8,128)} custom-call(bf16[8,2,4,16,512]{4,3,2,1,0:T(8,128)(2,1)} %copy-done.2, f32[4,256,256]{2,1,0:T(8,128)} %get-tuple-element.27.score_ref, f32[4,256,128]{2,1,0:T(8,128)} %get-tuple-element.28.cum_ref, f32[4,32,256]{2,1,0:T(8,128)} %get-tuple-element.29.row_ref, f32[1,2048]{1,0:T(1,128)} %broadcast_in_dim_reshape.7.skip_ref), custom_call_target="tpu_custom_call" | custom-call | flops 536870912 | bytes 5242880 | tf_op jit(solution)/shard_map/local_scan/pallas_call | solution.py:358
  162.6 7.8 %local_scan.7.local_ref = f32[4,240,512]{2,1,0:T(8,128)} custom-call(bf16[8,2,4,16,512]{4,3,2,1,0:T(8,128)(2,1)} %copy-done.1, f32[4,256,256]{2,1,0:T(8,128)} %get-tuple-element.27.score_ref, f32[4,256,128]{2,1,0:T(8,128)} %get-tuple-element.28.cum_ref, f32[4,32,256]{2,1,0:T(8,128)} %get-tuple-element.29.row_ref, f32[1,2048]{1,0:T(1,128)} %broadcast_in_dim_reshape.7.skip_ref), custom_call_target="tpu_custom_call" | custom-call | flops 536870912 | bytes 5242880 | tf_op jit(solution)/shard_map/local_scan/pallas_call | solution.py:358
  170.4 7.8 %local_scan.4.local_ref = f32[4,240,512]{2,1,0:T(8,128)} custom-call(bf16[8,2,4,16,512]{4,3,2,1,0:T(8,128)(2,1)} %copy-done.4, f32[4,256,256]{2,1,0:T(8,128)} %get-tuple-element.27.score_ref, f32[4,256,128]{2,1,0:T(8,128)} %get-tuple-element.28.cum_ref, f32[4,32,256]{2,1,0:T(8,128)} %get-tuple-element.29.row_ref, f32[1,2048]{1,0:T(1,128)} %broadcast_in_dim_reshape.7.skip_ref), custom_call_target="tpu_custom_call" | custom-call | flops 536870912 | bytes 5242880 | tf_op jit(solution)/shard_map/local_scan/pallas_call | solution.py:358
  178.4 0.8 collective-permute-start.3
  179.2 1.3 collective-permute-start.2
  181.5 1.3 collective-permute-start.5
  183.5 1.3 collective-permute-start.8
  184.9 9.1 %collective-permute-done.2.rest_1_ = bf16[4,64,512]{2,1,0:T(8,128)(2,1)S(1)} collective-permute-done((bf16[4,64,512]{2,1,0:T(8,128)(2,1)S(1)}, bf16[4,64,512]{2,1,0:T(8,128)(2,1)S(1)}, u32[]{:S(2)}, u32[]{:S(2)}) %collective-permute-start.2) | collective-permute-done | bytes 262176 | tf_op jit(solution)/shard_map/ppermute | solution.py:517
  194.7 7.2 %finish.3 = (bf16[4,240,512]{2,1,0:T(8,128)(2,1)}, f32[4,240,128]{2,1,0:T(8,128)}) custom-call(f32[4,240,512]{2,1,0:T(8,128)} %local_scan.5.local_ref, bf16[4,240,2048]{2,1,0:T(8,128)(2,1)} %bitcast.23, bf16[4,2,256,128]{3,2,1,0:T(8,128)(2,1)} %get-tuple-element.30.ecum_ref, bf16[4,256,64]{2,1,0:T(8,128)(2,1)} %get-tuple-element.31.c_ref, ...), custom_call_target="tpu_custom_call" | custom-call | flops 335544320 | bytes 5242880 | tf_op jit(solution)/shard_map/finish/pallas_call | solution.py:411
  201.9 1.3 collective-permute-start.11
  203.2 2.0 collective-permute-done.5.rest_1_
  205.9 7.2 %finish.4 = (bf16[4,240,512]{2,1,0:T(8,128)(2,1)}, f32[4,240,128]{2,1,0:T(8,128)}) custom-call(f32[4,240,512]{2,1,0:T(8,128)} %local_scan.6.local_ref, bf16[4,240,2048]{2,1,0:T(8,128)(2,1)} %bitcast.24, bf16[4,2,256,128]{3,2,1,0:T(8,128)(2,1)} %get-tuple-element.30.ecum_ref, bf16[4,256,64]{2,1,0:T(8,128)(2,1)} %get-tuple-element.31.c_ref, ...), custom_call_target="tpu_custom_call" | custom-call | flops 335544320 | bytes 5242880 | tf_op jit(solution)/shard_map/finish/pallas_call | solution.py:411
  213.1 3.4 %collective-permute-done.8.rest_1_ = bf16[4,64,512]{2,1,0:T(8,128)(2,1)S(1)} collective-permute-done((bf16[4,64,512]{2,1,0:T(8,128)(2,1)S(1)}, bf16[4,64,512]{2,1,0:T(8,128)(2,1)S(1)}, u32[]{:S(2)}, u32[]{:S(2)}) %collective-permute-start.8) | collective-permute-done | bytes 262176 | tf_op jit(solution)/shard_map/ppermute | solution.py:517
  217.1 7.2 %finish.5 = (bf16[4,240,512]{2,1,0:T(8,128)(2,1)}, f32[4,240,128]{2,1,0:T(8,128)}) custom-call(f32[4,240,512]{2,1,0:T(8,128)} %local_scan.7.local_ref, bf16[4,240,2048]{2,1,0:T(8,128)(2,1)} %bitcast.25, bf16[4,2,256,128]{3,2,1,0:T(8,128)(2,1)} %get-tuple-element.30.ecum_ref, bf16[4,256,64]{2,1,0:T(8,128)(2,1)} %get-tuple-element.31.c_ref, ...), custom_call_target="tpu_custom_call" | custom-call | flops 335544320 | bytes 5242880 | tf_op jit(solution)/shard_map/finish/pallas_call | solution.py:411
  224.3 8.3 %project.1 = (f32[4,240,1024]{2,1,0:T(8,128)}, f32[4,240,128]{2,1,0:T(8,128)}) custom-call(bf16[2048,1024]{1,0:T(8,128)(2,1)} %w_ref.8, bf16[4,240,512]{2,1,0:T(8,128)(2,1)} %get-tuple-element.35.rest_0_, bf16[4,240,512]{2,1,0:T(8,128)(2,1)} %get-tuple-element.36.rest_1_, bf16[4,240,512]{2,1,0:T(8,128)(2,1)} %get-tuple-element.37.rest_2_, ...), custom_call_target="tpu_custom_call" | custom-call | flops 3019898880 | bytes 10027008 | tf_op jit(solution)/shard_map/project/pallas_call | solution.py:452
  233.5 8.2 %last.1 = bf16[4,240,1024]{2,1,0:T(8,128)(2,1)} custom-call(f32[4,240,512]{2,1,0:T(8,128)} %local_scan.4.local_ref, bf16[4,240,2048]{2,1,0:T(8,128)(2,1)} %bitcast.26, bf16[4,2,256,128]{3,2,1,0:T(8,128)(2,1)} %get-tuple-element.30.ecum_ref, bf16[4,256,64]{2,1,0:T(8,128)(2,1)} %get-tuple-element.31.c_ref, bf16[128,2048]{1,0:T(8,128)(2,1)} %compare_convert_fusion.spread_ref, ...), custom_call_target="tpu_custom_call" | custom-call | flops 1006632960 | bytes 7864320 | tf_op jit(solution)/shard_map/last/pallas_call | solution.py:487
  (91 shorter events, 7.8 us)
Async XLA Ops:
  5.7 4.4 %copy-start.22 = (f32[32]{0:T(128)S(1)}, f32[32]{0:T(128)}, u32[]{:S(2)}) copy-start(f32[32]{0:T(128)} %param.17) | copy-start | bytes 388
  5.7 29.5 %all-to-all-start = ((bf16[8,2,4,16,1024]{4,3,2,1,0:T(8,128)(2,1)}), bf16[8,2,4,16,1024]{4,3,2,1,0:T(8,128)(2,1)S(1)}, u32[]{:S(2)}, u32[]{:S(2)}) async-start(bf16[8,2,4,16,1024]{4,3,2,1,0:T(8,128)(2,1)} %arrange.1), calls=%async_computation | async-start | bytes 4194304 | tf_op jit(solution)/shard_map/all_to_all | solution.py:538
  23.0 1.1 slice-start
  23.0 2.1 copy-start.26
  23.0 2.1 copy-start.27
  23.0 2.1 copy-start.23
  23.0 2.1 copy-start.24
  35.2 1.3 copy-start
  48.1 18.9 %all-to-all-start.4 = ((bf16[8,2,4,16,512]{4,3,2,1,0:T(8,128)(2,1)}), bf16[8,2,4,16,512]{4,3,2,1,0:T(8,128)(2,1)S(1)}, u32[]{:S(2)}, u32[]{:S(2)}) async-start(bf16[8,2,4,16,512]{4,3,2,1,0:T(8,128)(2,1)} %time_scan.7), calls=%async_computation.4 | async-start | bytes 2097152 | tf_op jit(solution)/shard_map/all_to_all | solution.py:562
  67.0 12.1 %copy-start.1 = (bf16[8,2,4,16,512]{4,3,2,1,0:T(8,128)(2,1)}, bf16[8,2,4,16,512]{4,3,2,1,0:T(8,128)(2,1)S(1)}, u32[]{:S(2)}) copy-start(bf16[8,2,4,16,512]{4,3,2,1,0:T(8,128)(2,1)S(1)} %all-to-all-done.4.x_ref) | copy-start | bytes 3145732
  67.0 18.9 %all-to-all-start.3 = ((bf16[8,2,4,16,512]{4,3,2,1,0:T(8,128)(2,1)}), bf16[8,2,4,16,512]{4,3,2,1,0:T(8,128)(2,1)S(1)}, u32[]{:S(2)}, u32[]{:S(2)}) async-start(bf16[8,2,4,16,512]{4,3,2,1,0:T(8,128)(2,1)} %time_scan.6), calls=%async_computation.3 | async-start | bytes 2097152 | tf_op jit(solution)/shard_map/all_to_all | solution.py:562
  79.1 22.6 %copy-start.25 = (f32[32]{0:T(128)S(1)}, f32[32]{0:T(128)}, u32[]{:S(2)}) copy-start(f32[32]{0:T(128)} %param.18) | copy-start | bytes 388
  85.9 11.4 %copy-start.2 = (bf16[8,2,4,16,512]{4,3,2,1,0:T(8,128)(2,1)}, bf16[8,2,4,16,512]{4,3,2,1,0:T(8,128)(2,1)S(1)}, u32[]{:S(2)}) copy-start(bf16[8,2,4,16,512]{4,3,2,1,0:T(8,128)(2,1)S(1)} %all-to-all-done.3.x_ref) | copy-start | bytes 3145732
  85.9 23.8 %all-to-all-start.2 = ((bf16[8,2,4,16,512]{4,3,2,1,0:T(8,128)(2,1)}), bf16[8,2,4,16,512]{4,3,2,1,0:T(8,128)(2,1)S(1)}, u32[]{:S(2)}, u32[]{:S(2)}) async-start(bf16[8,2,4,16,512]{4,3,2,1,0:T(8,128)(2,1)} %time_scan.5), calls=%async_computation.2 | async-start | bytes 2097152 | tf_op jit(solution)/shard_map/all_to_all | solution.py:562
  98.3 83.2 %collective-permute-start = (f32[4,1,2048]{2,1,0:T(1,128)S(1)}, f32[4,1,2048]{2,1,0:T(1,128)S(1)}, u32[]{:S(2)}, u32[]{:S(2)}) collective-permute-start(f32[4,1,2048]{2,1,0:T(1,128)S(1)} %broadcast_in_dim.31), channel_id=1, source_target_pairs={{0,1},{1,2},{2,3},{4,5},{5,6},{6,7},{8,9},{9,10},{10,11},{12,13},{... | collective-permute-start | bytes 98312 | tf_op jit(solution)/shard_map/ppermute | solution.py:555
  109.7 12.3 %copy-start.3 = (bf16[8,2,4,16,512]{4,3,2,1,0:T(8,128)(2,1)}, bf16[8,2,4,16,512]{4,3,2,1,0:T(8,128)(2,1)S(1)}, u32[]{:S(2)}) copy-start(bf16[8,2,4,16,512]{4,3,2,1,0:T(8,128)(2,1)S(1)} %all-to-all-done.2.x_ref) | copy-start | bytes 3145732
  109.7 30.7 %all-to-all-start.1 = ((bf16[8,2,4,16,512]{4,3,2,1,0:T(8,128)(2,1)}), bf16[8,2,4,16,512]{4,3,2,1,0:T(8,128)(2,1)S(1)}, u32[]{:S(2)}, u32[]{:S(2)}) async-start(bf16[8,2,4,16,512]{4,3,2,1,0:T(8,128)(2,1)} %time_scan.4), calls=%async_computation.1 | async-start | bytes 2097152 | tf_op jit(solution)/shard_map/all_to_all | solution.py:562
  127.4 50.9 %collective-permute-start.1 = (bf16[4,64,512]{2,1,0:T(8,128)(2,1)}, bf16[4,64,512]{2,1,0:T(8,128)(2,1)S(1)}, u32[]{:S(2)}, u32[]{:S(2)}) collective-permute-start(bf16[4,64,512]{2,1,0:T(8,128)(2,1)} %end_state.4), channel_id=1, source_target_pairs={{0,1},{2,3},{4,5},{6,7},{8,9},{10,11},{12,13},{14,15},{16,17},{18,... | collective-permute-start | bytes 786440 | tf_op jit(solution)/shard_map/ppermute | solution.py:515
  133.3 45.9 %collective-permute-start.4 = (bf16[4,64,512]{2,1,0:T(8,128)(2,1)}, bf16[4,64,512]{2,1,0:T(8,128)(2,1)S(1)}, u32[]{:S(2)}, u32[]{:S(2)}) collective-permute-start(bf16[4,64,512]{2,1,0:T(8,128)(2,1)} %end_state.5), channel_id=1, source_target_pairs={{0,1},{2,3},{4,5},{6,7},{8,9},{10,11},{12,13},{14,15},{16,17},{18,... | collective-permute-start | bytes 786440 | tf_op jit(solution)/shard_map/ppermute | solution.py:515
  139.1 41.6 %collective-permute-start.7 = (bf16[4,64,512]{2,1,0:T(8,128)(2,1)}, bf16[4,64,512]{2,1,0:T(8,128)(2,1)S(1)}, u32[]{:S(2)}, u32[]{:S(2)}) collective-permute-start(bf16[4,64,512]{2,1,0:T(8,128)(2,1)} %end_state.6), channel_id=1, source_target_pairs={{0,1},{2,3},{4,5},{6,7},{8,9},{10,11},{12,13},{14,15},{16,17},{18,... | collective-permute-start | bytes 786440 | tf_op jit(solution)/shard_map/ppermute | solution.py:515
  140.4 1.1 copy-start.4
  145.8 36.9 %collective-permute-start.10 = (bf16[4,64,512]{2,1,0:T(8,128)(2,1)}, bf16[4,64,512]{2,1,0:T(8,128)(2,1)S(1)}, u32[]{:S(2)}, u32[]{:S(2)}) collective-permute-start(bf16[4,64,512]{2,1,0:T(8,128)(2,1)} %end_state.7), channel_id=1, source_target_pairs={{0,1},{2,3},{4,5},{6,7},{8,9},{10,11},{12,13},{14,15},{16,17},{18,... | collective-permute-start | bytes 786440 | tf_op jit(solution)/shard_map/ppermute | solution.py:515
  170.4 7.9 %copy-start.12 = (bf16[4,64,512]{2,1,0:T(8,128)(2,1)S(1)}, bf16[4,64,512]{2,1,0:T(8,128)(2,1)}, u32[]{:S(2)}) copy-start(bf16[4,64,512]{2,1,0:T(8,128)(2,1)} %end_state.4) | copy-start | bytes 786436
  170.4 10.1 %copy-start.11 = (bf16[4,64,512]{2,1,0:T(8,128)(2,1)S(1)}, bf16[4,64,512]{2,1,0:T(8,128)(2,1)}, u32[]{:S(2)}) copy-start(bf16[4,64,512]{2,1,0:T(8,128)(2,1)} %end_state.5) | copy-start | bytes 786436
  170.4 10.9 %copy-start.10 = (bf16[4,64,512]{2,1,0:T(8,128)(2,1)S(1)}, bf16[4,64,512]{2,1,0:T(8,128)(2,1)}, u32[]{:S(2)}) copy-start(bf16[4,64,512]{2,1,0:T(8,128)(2,1)} %end_state.6) | copy-start | bytes 786436
  178.3 6.5 %copy-start.9 = (bf16[4,64,512]{2,1,0:T(8,128)(2,1)S(1)}, bf16[4,64,512]{2,1,0:T(8,128)(2,1)}, u32[]{:S(2)}) copy-start(bf16[4,64,512]{2,1,0:T(8,128)(2,1)} %end_state.7) | copy-start | bytes 786436
  178.3 16.4 %copy-start.8 = (bf16[4,64,512]{2,1,0:T(8,128)(2,1)}, bf16[4,64,512]{2,1,0:T(8,128)(2,1)S(1)}, u32[]{:S(2)}) copy-start(bf16[4,64,512]{2,1,0:T(8,128)(2,1)S(1)} %collective-permute-done.1.rest_0_) | copy-start | bytes 786436
  178.4 5.1 %collective-permute-start.3 = (bf16[4,64,512]{2,1,0:T(8,128)(2,1)S(1)}, bf16[4,64,512]{2,1,0:T(8,128)(2,1)S(1)}, u32[]{:S(2)}, u32[]{:S(2)}) collective-permute-start(bf16[4,64,512]{2,1,0:T(8,128)(2,1)S(1)} %add_convert_fusion.3), channel_id=1, source_target_pairs={{1,3},{5,7},{9,11},{13,15},{17,19},{21,23},{25,27},{29,31}} | collective-permute-start | bytes 786440 | tf_op jit(solution)/shard_map/ppermute | solution.py:518
  179.2 22.7 %copy-start.7 = (bf16[4,64,512]{2,1,0:T(8,128)(2,1)}, bf16[4,64,512]{2,1,0:T(8,128)(2,1)S(1)}, u32[]{:S(2)}) copy-start(bf16[4,64,512]{2,1,0:T(8,128)(2,1)S(1)} %collective-permute-done.4.rest_0_) | copy-start | bytes 786436
  179.2 14.7 %collective-permute-start.2 = (bf16[4,64,512]{2,1,0:T(8,128)(2,1)S(1)}, bf16[4,64,512]{2,1,0:T(8,128)(2,1)S(1)}, u32[]{:S(2)}, u32[]{:S(2)}) collective-permute-start(bf16[4,64,512]{2,1,0:T(8,128)(2,1)S(1)} %add_convert_fusion.3), channel_id=1, source_target_pairs={{1,2},{5,6},{9,10},{13,14},{17,18},{21,22},{25,26},{29,30}} | collective-permute-start | bytes 786440 | tf_op jit(solution)/shard_map/ppermute | solution.py:517
  180.6 21.2 %copy-start.6 = (bf16[4,64,512]{2,1,0:T(8,128)(2,1)}, bf16[4,64,512]{2,1,0:T(8,128)(2,1)S(1)}, u32[]{:S(2)}) copy-start(bf16[4,64,512]{2,1,0:T(8,128)(2,1)S(1)} %collective-permute-done.7.rest_0_) | copy-start | bytes 786436
  180.7 21.2 %collective-permute-start.6 = (bf16[4,64,512]{2,1,0:T(8,128)(2,1)S(1)}, bf16[4,64,512]{2,1,0:T(8,128)(2,1)S(1)}, u32[]{:S(2)}, u32[]{:S(2)}) collective-permute-start(bf16[4,64,512]{2,1,0:T(8,128)(2,1)S(1)} %add_convert_fusion.2), channel_id=1, source_target_pairs={{1,3},{5,7},{9,11},{13,15},{17,19},{21,23},{25,27},{29,31}} | collective-permute-start | bytes 786440 | tf_op jit(solution)/shard_map/ppermute | solution.py:518
  181.4 13.2 %copy-start.13 = (f32[4,1,2048]{2,1,0:T(1,128)}, f32[4,1,2048]{2,1,0:T(1,128)S(1)}, u32[]{:S(2)}) copy-start(f32[4,1,2048]{2,1,0:T(1,128)S(1)} %collective-permute-done.prev_ref) | copy-start | bytes 98308
  181.5 23.7 %collective-permute-start.5 = (bf16[4,64,512]{2,1,0:T(8,128)(2,1)S(1)}, bf16[4,64,512]{2,1,0:T(8,128)(2,1)S(1)}, u32[]{:S(2)}, u32[]{:S(2)}) collective-permute-start(bf16[4,64,512]{2,1,0:T(8,128)(2,1)S(1)} %add_convert_fusion.2), channel_id=1, source_target_pairs={{1,2},{5,6},{9,10},{13,14},{17,18},{21,22},{25,26},{29,30}} | collective-permute-start | bytes 786440 | tf_op jit(solution)/shard_map/ppermute | solution.py:517
  182.8 19.1 %copy-start.5 = (bf16[4,64,512]{2,1,0:T(8,128)(2,1)}, bf16[4,64,512]{2,1,0:T(8,128)(2,1)S(1)}, u32[]{:S(2)}) copy-start(bf16[4,64,512]{2,1,0:T(8,128)(2,1)S(1)} %collective-permute-done.10.rest_0_) | copy-start | bytes 786436
  182.8 30.3 %collective-permute-start.9 = (bf16[4,64,512]{2,1,0:T(8,128)(2,1)S(1)}, bf16[4,64,512]{2,1,0:T(8,128)(2,1)S(1)}, u32[]{:S(2)}, u32[]{:S(2)}) collective-permute-start(bf16[4,64,512]{2,1,0:T(8,128)(2,1)S(1)} %add_convert_fusion.1), channel_id=1, source_target_pairs={{1,3},{5,7},{9,11},{13,15},{17,19},{21,23},{25,27},{29,31}} | collective-permute-start | bytes 786440 | tf_op jit(solution)/shard_map/ppermute | solution.py:518
  183.5 11.2 %copy-start.17 = (bf16[4,64,512]{2,1,0:T(8,128)(2,1)}, bf16[4,64,512]{2,1,0:T(8,128)(2,1)S(1)}, u32[]{:S(2)}) copy-start(bf16[4,64,512]{2,1,0:T(8,128)(2,1)S(1)} %collective-permute-done.3.rest_2_) | copy-start | bytes 786436
  183.5 32.9 %collective-permute-start.8 = (bf16[4,64,512]{2,1,0:T(8,128)(2,1)S(1)}, bf16[4,64,512]{2,1,0:T(8,128)(2,1)S(1)}, u32[]{:S(2)}, u32[]{:S(2)}) collective-permute-start(bf16[4,64,512]{2,1,0:T(8,128)(2,1)S(1)} %add_convert_fusion.1), channel_id=1, source_target_pairs={{1,2},{5,6},{9,10},{13,14},{17,18},{21,22},{25,26},{29,30}} | collective-permute-start | bytes 786440 | tf_op jit(solution)/shard_map/ppermute | solution.py:517
  194.0 0.7 copy-start.19
  194.0 38.7 %collective-permute-start.12 = (bf16[4,64,512]{2,1,0:T(8,128)(2,1)S(1)}, bf16[4,64,512]{2,1,0:T(8,128)(2,1)S(1)}, u32[]{:S(2)}, u32[]{:S(2)}) collective-permute-start(bf16[4,64,512]{2,1,0:T(8,128)(2,1)S(1)} %add_convert_fusion), channel_id=1, source_target_pairs={{1,3},{5,7},{9,11},{13,15},{17,19},{21,23},{25,27},{29,31}} | collective-permute-start | bytes 786440 | tf_op jit(solution)/shard_map/ppermute | solution.py:518
  201.9 3.3 %copy-start.16 = (bf16[4,64,512]{2,1,0:T(8,128)(2,1)}, bf16[4,64,512]{2,1,0:T(8,128)(2,1)S(1)}, u32[]{:S(2)}) copy-start(bf16[4,64,512]{2,1,0:T(8,128)(2,1)S(1)} %collective-permute-done.6.rest_2_) | copy-start | bytes 786436
  201.9 30.7 %collective-permute-start.11 = (bf16[4,64,512]{2,1,0:T(8,128)(2,1)S(1)}, bf16[4,64,512]{2,1,0:T(8,128)(2,1)S(1)}, u32[]{:S(2)}, u32[]{:S(2)}) collective-permute-start(bf16[4,64,512]{2,1,0:T(8,128)(2,1)S(1)} %add_convert_fusion), channel_id=1, source_target_pairs={{1,2},{5,6},{9,10},{13,14},{17,18},{21,22},{25,26},{29,30}} | collective-permute-start | bytes 786440 | tf_op jit(solution)/shard_map/ppermute | solution.py:517
  205.2 0.7 copy-start.20
  213.1 3.4 %copy-start.18 = (bf16[4,64,512]{2,1,0:T(8,128)(2,1)}, bf16[4,64,512]{2,1,0:T(8,128)(2,1)S(1)}, u32[]{:S(2)}) copy-start(bf16[4,64,512]{2,1,0:T(8,128)(2,1)S(1)} %collective-permute-done.9.rest_2_) | copy-start | bytes 786436
  216.4 0.7 copy-start.21
  232.6 0.7 copy-start.14
  232.7 0.8 copy-start.15

commit v2 on v0

v2 whole, which is shorter than its diff:
```python
import functools

import jax
import jax.numpy as jnp
from jax import lax
from jax.experimental import pallas as pl
from jax.experimental.pallas import tpu as pltpu
from jax.sharding import PartitionSpec as P

D = 1024
HEADS = 32
HEAD_DIM = 64
STATE = 64
DI = 2048
BLK = 16
LANES = 128
LOG2E = 1.4426950408889634
TOP = 64.0
GROUPS = (16, 8, 8)
RELAY = 8
EARLY = 1
TIME_STEP = 8
BF = jnp.bfloat16
F32 = jnp.float32
VMEM = 58 * 1024 * 1024
VMEM_TAIL = 58 * 1024 * 1024


def call(kernel, name, grid, in_specs, out_specs, out_shape, flops, moved, scratch=(), vmem=VMEM):
    return pl.pallas_call(
        kernel,
        name=name,
        grid=grid,
        in_specs=in_specs,
        out_specs=out_specs,
        out_shape=out_shape,
        scratch_shapes=scratch,
        compiler_params=pltpu.CompilerParams(vmem_limit_bytes=vmem),
        cost_estimate=pl.CostEstimate(flops=flops, bytes_accessed=moved, transcendentals=0),
    )


def dot(a, b):
    return jnp.dot(a, b, preferred_element_type=F32)


def dot_nt(a, b):
    return lax.dot_general(a, b, (((1,), (1,)), ((), ())), preferred_element_type=F32)


def dot_tn(a, b):
    return lax.dot_general(a, b, (((0,), (0,)), ((), ())), preferred_element_type=F32)


def softplus(x):
    return jnp.maximum(x, 0.0) + jnp.log1p(jnp.exp(-jnp.abs(x)))


def split2(v):
    high = v.astype(BF)
    return high, (v - high.astype(F32)).astype(BF)


def spread_heads(head0, cols):
    row = lax.broadcasted_iota(jnp.int32, (LANES, cols), 0)
    col = lax.broadcasted_iota(jnp.int32, (LANES, cols), 1)
    return jnp.where(row - HEADS - head0 == col // HEAD_DIM, 1.0, 0.0).astype(BF)


def widen(values, spread):
    high, low = split2(values)
    return dot(high, spread) + dot(low, spread)


def full(shape):
    return pl.BlockSpec(shape, lambda *_: (0,) * len(shape))


def arrange_kernel(n, spare, x_ref, o_ref):
    for f in range(x_ref.shape[0]):
        o_ref[:, 0, f] = x_ref[f].reshape(n, BLK, D)
    if spare:

        @pl.when(pl.program_id(0) == pl.num_programs(0) - 1)
        def _():
            o_ref[n - spare :, 0] = jnp.zeros((spare,) + o_ref.shape[2:], BF)


def arrange(tok, n, m):
    fr, npos, _ = tok.shape
    spare = n * m - npos // BLK
    return call(
        functools.partial(arrange_kernel, n, spare),
        "arrange",
        (m,),
        [pl.BlockSpec((fr, n * BLK, D), lambda h: (0, h, 0))],
        pl.BlockSpec((n, 1, fr, BLK, D), lambda h: (0, h, 0, 0, 0)),
        jax.ShapeDtypeStruct((n, m, fr, BLK, D), BF),
        0,
        4 * fr * npos * D,
    )(tok)


def gate_kernel(x_ref, w_ref, o_ref):
    o_ref[...] = dot_nt(x_ref[...], w_ref[...]).astype(BF)


def gate_proj(flat, w_t):
    rows = flat.shape[0]
    return call(
        gate_kernel,
        "gate_proj",
        (2,),
        [full((rows, D)), pl.BlockSpec((DI // 2, D), lambda j: (j, 0))],
        pl.BlockSpec((rows, DI // 2), lambda j: (0, j)),
        jax.ShapeDtypeStruct((rows, DI), BF),
        2 * rows * D * DI,
        2 * (rows * D + D * DI + rows * DI),
    )(flat, w_t)


def small_proj(x, w_ref, raw_w_ref):
    raw = dot_nt(x, raw_w_ref[...])
    zeros = jnp.zeros((raw.shape[0], LANES - raw.shape[1]), F32)
    return dot_nt(x, w_ref[...]), jnp.concatenate([raw, zeros], axis=1)


def small_specs(group):
    first = 2 * DI // LANES + group
    raw = (2 * DI + 4 * STATE) // (2 * HEADS)
    return [
        pl.BlockSpec((LANES, D), lambda *_: (first, 0)),
        pl.BlockSpec((2 * HEADS, D), lambda *_: (raw, 0)),
    ]


def space_prep_kernel(
    npos, x_ref, w_ref, raw_w_ref, par_ref, score_ref, cum_ref, row_ref, tail_ref, ecum_ref, b_ref, c_ref, grow_ref
):
    size = score_ref.shape[1]
    bc, raw = small_proj(x_ref[0], w_ref, raw_w_ref)
    pad = jnp.zeros((size - npos, LANES), F32)
    bc = jnp.concatenate([bc.astype(BF).astype(F32), pad], axis=0)
    b = bc[:, :STATE].astype(BF)
    c = bc[:, STATE:].astype(BF)
    step = softplus(raw + par_ref[0:1])
    step = jnp.concatenate([step, pad], axis=0)
    dec = step * par_ref[1:2]
    ri = lax.broadcasted_iota(jnp.int32, (size, size), 0)
    ci = lax.broadcasted_iota(jnp.int32, (size, size), 1)
    causal = ri >= ci
    cum = jnp.dot(
        causal.astype(F32), dec, precision=lax.Precision.HIGHEST, preferred_element_type=F32
    )
    total = cum[npos - 1 : npos]
    rowterm = jnp.log2(step) - cum
    score_ref[0] = jnp.where(causal, dot_nt(c, b), 0.0)
    cum_ref[0] = cum
    row_ref[0] = rowterm.T[HEADS : 2 * HEADS]
    tail = jnp.exp2(jnp.minimum(total + rowterm, TOP))
    t_hi, t_lo = split2(tail)
    tail_ref[0, 0] = t_hi
    tail_ref[0, 1] = t_lo
    e_hi, e_lo = split2(jnp.exp2(cum))
    ecum_ref[0, 0] = e_hi
    ecum_ref[0, 1] = e_lo
    b_ref[0] = b
    c_ref[0] = c
    growth = jnp.broadcast_to(jnp.exp2(total), (8, LANES))
    grow_ref[0] = widen(growth, spread_heads(0, DI))[0:1]


def space_prep(tok, w_t, params, size):
    fr, npos, _ = tok.shape

    def per_frame(shape):
        return pl.BlockSpec((1,) + shape, lambda f: (f,) + (0,) * len(shape))

    shapes = [
        ((size, size), F32),
        ((size, LANES), F32),
        ((HEADS, size), F32),
        ((2, size, LANES), BF),
        ((2, size, LANES), BF),
        ((size, STATE), BF),
        ((size, STATE), BF),
        ((1, DI), F32),
    ]
    return call(
        functools.partial(space_prep_kernel, npos),
        "space_prep",
        (fr,),
        [per_frame((npos, D))] + small_specs(1) + [full(params.shape)],
        [per_frame(s) for s, _ in shapes],
        [jax.ShapeDtypeStruct((fr,) + s, t) for s, t in shapes],
        2 * fr * npos * D * 256,
        6 * 1024 * 1024,
    )(tok, w_t, w_t, params)


def time_prep(n, m, fr, x, w_ref, raw_w_ref, par_ref, score_ref, cum_ref, row_ref):
    bc, raw = small_proj(x, w_ref, raw_w_ref)
    shape = (n, m, fr, 2, 8, LANES)
    q_rows = n * fr * 8
    bc = bc.astype(BF).astype(F32).reshape(shape)
    step = softplus(raw.astype(BF).astype(F32) + par_ref[0:1])
    dec = (step * par_ref[1:2]).reshape(shape)
    step = step.reshape(shape)
    ri = lax.broadcasted_iota(jnp.int32, (q_rows, q_rows), 0)
    ci = lax.broadcasted_iota(jnp.int32, (q_rows, q_rows), 1)
    keep = (ri >= ci) & ((ri & 7) == (ci & 7))
    for h in range(m):
        for e in range(2):
            q = 2 * h + e
            running = jnp.zeros((8, LANES), F32)
            parts = []
            for s in range(n):
                for f in range(fr):
                    running = running + dec[s, h, f, e]
                    parts.append(running)
            cum = jnp.concatenate(parts, axis=0)
            bcq = bc[:, h, :, e].reshape(q_rows, LANES)
            b = bcq[:, :STATE].astype(BF)
            c = bcq[:, STATE:].astype(BF)
            score_ref[q] = jnp.where(keep, dot_nt(c, b), 0.0)
            cum_ref[q] = cum
            rowterm = jnp.log2(step[:, h, :, e].reshape(q_rows, LANES)) - cum
            row_ref[q] = rowterm.T[:HEADS]


def head_pair(score, cum, row, x_pair):
    rows = x_pair.shape[0]
    lane = lax.broadcasted_iota(jnp.int32, (1, LANES), 1)
    left = jnp.where(lane < HEAD_DIM, 1.0, 0.0).astype(BF)
    halves = (x_pair * left, x_pair * (1 - left))
    cols = [jnp.broadcast_to(c, (rows, LANES)) for c in cum]
    out = [None] * (rows // LANES)
    for j in range(rows // LANES):
        lo, hi = j * LANES, (j + 1) * LANES
        pieces = []
        for k in range(2):
            span = cols[k][lo:] + row[k][:, lo:hi]
            pieces.append((jnp.exp2(jnp.minimum(span, TOP)) * score[lo:, lo:hi]).astype(BF))
        keys = jnp.concatenate([halves[0][lo:hi], halves[1][lo:hi]], axis=0)
        part = dot(jnp.concatenate(pieces, axis=1), keys)
        for i in range(j, rows // LANES):
            block = part[(i - j) * LANES : (i - j + 1) * LANES]
            out[i] = block if out[i] is None else out[i] + block
    return jnp.concatenate(out, axis=0)


def head_pairs(score, cum, row_ref, row_at, head0, lane0, x):
    ys = []
    for p in range(x.shape[1] // LANES):
        pair = (2 * p, 2 * p + 1)
        ys.append(
            head_pair(
                score,
                [cum[:, lane0 + k : lane0 + k + 1] for k in pair],
                [row_ref[row_at, pl.ds(head0 + k, 1), :] for k in pair],
                x[:, p * LANES : (p + 1) * LANES],
            )
        )
    return jnp.concatenate(ys, axis=1)


def time_scan_kernel(n, m, fr, head0, first, x_ref, w_ref, *rest):
    if first:
        small, (par_ref, o_ref, score_ref, cum_ref, row_ref) = rest[:2], rest[2:]

        @pl.when(pl.program_id(0) == 0)
        def _():
            time_prep(n, m, fr, x_ref[...], *small, par_ref, score_ref, cum_ref, row_ref)

    else:
        score_ref, cum_ref, row_ref, par_ref, o_ref = rest
    q_rows = n * fr * 8
    cols = w_ref.shape[0]
    base = head0 + cols // HEAD_DIM * pl.program_id(0)
    skip = widen(par_ref[...], spread_heads(base, cols))[2:3]
    x = dot_nt(x_ref[...], w_ref[...]).astype(BF).astype(F32)
    x = x.reshape(n, m, fr, 2, 8, cols)
    for h in range(m):
        ys = []
        for e in range(2):
            q = 2 * h + e
            xq = x[:, h, :, e].reshape(q_rows, cols)
            cum = pltpu.roll(cum_ref[q], LANES - base, 1)
            y = head_pairs(score_ref.at[q], cum, row_ref, q, base, 0, xq.astype(BF))
            y = y + skip * xq
            ys.append(y.reshape(n, fr, 8, cols))
        o_ref[:, h] = jnp.concatenate(ys, axis=2).astype(BF)


def time_scan(tok_t, w_t, prep, params, head0, heads):
    n, m, fr = tok_t.shape[:3]
    rows = n * m * fr * BLK
    q_rows = n * fr * 8
    cols = heads * HEAD_DIM
    block = TIME_STEP * HEAD_DIM
    lo = (DI + head0 * HEAD_DIM) // block
    shapes = [(2 * m, q_rows, q_rows), (2 * m, q_rows, LANES), (2 * m, HEADS, q_rows)]
    prep_specs = [full(s) for s in shapes]
    out_specs = [pl.BlockSpec((n, m, fr, BLK, block), lambda j: (0, 0, 0, 0, j))]
    out_shapes = [jax.ShapeDtypeStruct((n, m, fr, BLK, cols), BF)]
    in_specs = [full((rows, D)), pl.BlockSpec((block, D), lambda j: (lo + j, 0))]
    if prep is None:
        in_specs += small_specs(0) + [full(params.shape)]
        args = (w_t, w_t, params)
        out_specs += prep_specs
        out_shapes += [jax.ShapeDtypeStruct(s, F32) for s in shapes]
    else:
        in_specs += prep_specs + [full(params.shape)]
        args = (*prep, params)
    return call(
        functools.partial(time_scan_kernel, n, m, fr, head0, prep is None),
        "time_scan",
        (cols // block,),
        in_specs,
        out_specs,
        out_shapes,
        2 * rows * D * cols + 4 * rows * q_rows * cols,
        2 * (rows * D + D * cols + rows * cols) + 2 * 1024 * 1024,
    )(tok_t.reshape(rows, D), w_t, *args)


def frame_rows(ref, frame):
    n, m, _, _, cols = ref.shape
    return jnp.concatenate([ref[:, h, frame].reshape(n * BLK, cols) for h in range(m)], axis=0)


def end_of(x, f, tail_ref, b_ref, spread):
    wide = dot(tail_ref[f, 0], spread) + dot(tail_ref[f, 1], spread)
    return dot_tn(b_ref[f], (x.astype(F32) * wide).astype(BF)).astype(BF)


def local_of(x, f, head0, score_ref, cum_ref, row_ref, skip):
    y = head_pairs(score_ref.at[f], cum_ref[f], row_ref, f, head0, HEADS + head0, x)
    return y + skip * x.astype(F32)


def space_kernel(head0, npos, local, x_ref, score_ref, cum_ref, row_ref, tail_ref, b_ref, par_ref, *outs):
    spread = spread_heads(head0, x_ref.shape[4])
    skip = widen(par_ref[...], spread)[3:4]
    for f in range(x_ref.shape[2]):
        x = frame_rows(x_ref, f)
        for i, ref in enumerate(outs[local:]):
            own = slice(i * RELAY * HEAD_DIM, i * RELAY * HEAD_DIM + ref.shape[2])
            ref[f] = end_of(x[:, own], f, tail_ref, b_ref, spread[:, own])
        if local:
            outs[0][f] = local_of(x, f, head0, score_ref, cum_ref, row_ref, skip)[:npos]


def space_parts(time_out, space, params, head0, npos, local, end):
    n, m, fr, _, cols = time_out.shape
    size = space[0].shape[1]
    step = 2 if fr % 2 == 0 else 1

    def frames(shape):
        return pl.BlockSpec((step,) + shape, lambda f: (f,) + (0,) * len(shape))

    def unused(shape):
        return pl.BlockSpec(memory_space=pl.ANY)

    l_frames = frames if local else unused
    e_frames = frames if end else unused
    outs = []
    if local:
        outs.append((frames((npos, cols)), jax.ShapeDtypeStruct((fr, npos, cols), F32)))
    if end:
        width = RELAY * HEAD_DIM
        for at in range(0, cols, width):
            piece = min(width, cols - at)
            outs.append((frames((STATE, piece)), jax.ShapeDtypeStruct((fr, STATE, piece), BF)))
    return call(
        functools.partial(space_kernel, head0, npos, local),
        "space" + "_local" * local + "_end" * end,
        (fr // step,),
        [
            pl.BlockSpec((n, m, step, BLK, cols), lambda f: (0, 0, f, 0, 0)),
            l_frames((size, size)),
            l_frames((size, LANES)),
            l_frames((HEADS, size)),
            e_frames((2, size, LANES)),
            e_frames((size, STATE)),
            full(params.shape),
        ],
        [spec for spec, _ in outs],
        [shape for _, shape in outs],
        4 * fr * size * size * cols,
        6 * fr * size * cols + 2 * 1024 * 1024,
    )(time_out, *space, params)


def gated_of(local, z, ecum_ref, c_ref, spread, states):
    state = sum(ref[0].astype(F32) for ref in states)
    npos = local.shape[0]
    carried = dot(c_ref[0], state.astype(BF))[:npos]
    wide = (dot(ecum_ref[0, 0], spread) + dot(ecum_ref[0, 1], spread))[:npos]
    z = z.astype(F32)
    return (local + wide * carried) * (z * jax.nn.sigmoid(z))


def lane_sums(v):
    return sum(v[:, a : a + LANES] for a in range(0, v.shape[1], LANES))


def finish_heads(cuts, locals_, states, z_ref, ecum_ref, c_ref, gain_ref, w_ref):
    total, squares, used = None, None, 0
    base = cuts[0][0]
    for local, (lo, hi) in zip(locals_, cuts):
        pieces = -(-(hi - lo) // (RELAY * HEAD_DIM))
        hops = len(states) // sum(-(-(b - a) // (RELAY * HEAD_DIM)) for a, b in cuts)
        for p in range(pieces):
            at, to = lo + p * RELAY * HEAD_DIM, min(hi, lo + (p + 1) * RELAY * HEAD_DIM)
            own = slice(at - base, to - base)
            gated = gated_of(
                local[0, :, at - lo : to - lo],
                z_ref[0, :, own],
                ecum_ref,
                c_ref,
                spread_heads(at // HEAD_DIM, to - at),
                states[used : used + hops],
            )
            used += hops
            part = dot((gated * gain_ref[:, own]).astype(BF), w_ref[own])
            square = lane_sums(gated * gated)
            total = part if total is None else total + part
            squares = square if squares is None else squares + square
    return total, squares


def early_kernel(cuts, z_ref, ecum_ref, c_ref, gain_ref, w_ref, *rest):
    count = len(cuts)
    locals_, states, (o_ref, sq_ref) = rest[:count], rest[count:-2], rest[-2:]
    o_ref[0], sq_ref[0] = finish_heads(cuts, locals_, states, z_ref, ecum_ref, c_ref, gain_ref, w_ref)


def last_kernel(cuts, z_ref, ecum_ref, c_ref, gain_ref, w_ref, acc_ref, sq_ref, tok_ref, *rest):
    count = len(cuts)
    locals_, states, o_ref = rest[:count], rest[count:-1], rest[-1]
    total, squares = finish_heads(cuts, locals_, states, z_ref, ecum_ref, c_ref, gain_ref, w_ref)
    mean = jnp.sum(squares + sq_ref[0], axis=1, keepdims=True) * (1.0 / DI)
    inv_scale = lax.rsqrt(mean + 1e-05)
    o_ref[0] = ((total + acc_ref[0]) * inv_scale + tok_ref[0].astype(F32)).astype(BF)


def finish(cuts, locals_, states, gate, ecum, c, gain, w_out, before=None):
    fr, npos, _ = gate.shape
    size = c.shape[1]
    cols = cuts[-1][1] - cuts[0][0]
    own = cuts[0][0] // cols
    per_frame = lambda f: (f, 0, 0)
    wide, narrow = pl.BlockSpec((1, npos, D), per_frame), pl.BlockSpec((1, npos, LANES), per_frame)
    in_specs = [
        pl.BlockSpec((1, npos, cols), lambda f: (f, 0, own)),
        pl.BlockSpec((1, 2, size, LANES), lambda f: (f, 0, 0, 0)),
        pl.BlockSpec((1, size, STATE), per_frame),
        pl.BlockSpec((1, cols), lambda f: (0, own)),
        pl.BlockSpec((cols, D), lambda f: (own, 0)),
    ]
    if before is None:
        kernel, before, name = early_kernel, (), "early"
        out_specs = [wide, narrow]
        out_shape = [
            jax.ShapeDtypeStruct((fr, npos, D), F32),
            jax.ShapeDtypeStruct((fr, npos, LANES), F32),
        ]
    else:
        kernel, name = last_kernel, "last"
        in_specs += [wide, narrow, wide]
        out_specs, out_shape = wide, jax.ShapeDtypeStruct((fr, npos, D), BF)
    return call(
        functools.partial(kernel, cuts),
        name,
        (fr,),
        in_specs + [pl.BlockSpec((1,) + v.shape[1:], per_frame) for v in (*locals_, *states)],
        out_specs,
        out_shape,
        2 * fr * npos * cols * D,
        8 * fr * npos * cols + 2 * cols * D + 4 * fr * npos * D,
        vmem=VMEM_TAIL,
    )(gate, ecum, c, gain, w_out, *before, *locals_, *states)


def hop(state, k):
    return lax.ppermute(state, "space", [(k, k + 1)])


def join(end, growth, start):
    return (end.astype(F32) + growth * start.astype(F32)).astype(BF)


def after(value, other):
    return lax.optimization_barrier((value, other))[0]


def body(
    tokens, w_in, w_out, a_log_time, a_log_space, dt_bias_time, dt_bias_space, skip_time, skip_space, norm_gain
):
    fr, rows_dev, cols_dev, _ = tokens.shape
    n = lax.axis_size("tm")
    npos = rows_dev * cols_dev
    m = -(-(npos // BLK) // n)
    size = m * n * BLK
    tok = tokens.reshape(fr, npos, D)
    flat = tokens.reshape(fr * npos, D)

    tok_t = lax.all_to_all(arrange(tok, n, m), "tm", split_axis=0, concat_axis=0, tiled=True)

    w_t = w_in.T
    fill = jnp.zeros((LANES - 2 * HEADS,), F32)
    none = jnp.zeros((HEADS,), F32)
    params = jnp.stack(
        [
            jnp.concatenate([dt_bias_time, dt_bias_space, fill]),
            jnp.concatenate([-jnp.exp(a_log_time) * LOG2E, -jnp.exp(a_log_space) * LOG2E, fill]),
            jnp.concatenate([none, skip_time, fill]),
            jnp.concatenate([none, skip_space, fill]),
        ]
        + [jnp.zeros((LANES,), F32)] * 4
    )
    gain = norm_gain[None]

    gate = gate_proj(flat, w_t).reshape(fr, npos, DI)
    score, cum, row, tail, ecum, b, c, growth = space_prep(tok, w_t, params, size)
    tok_t, gate, growth = lax.optimization_barrier((tok_t, gate, growth))

    starts = [sum(GROUPS[:i]) for i in range(len(GROUPS))]
    space = (score, cum, row, tail, b)
    prep = None
    outs = []
    for head0, heads in zip(starts, GROUPS):
        out, *made = time_scan(tok_t, w_t, prep, params, head0, heads)
        prep = prep or made
        outs.append(out)
    hops = lax.axis_size("space") - 1
    locals_, cuts, ends, grows, states = [], [], [], [], []

    def send(i, k, beside):
        moving = ends[i]
        if k:
            got = after(states[i][k - 1], beside)
            moving = [join(e, g, r) for e, g, r in zip(ends[i], grows[i], got)]
        states[i].append([hop(e, k) for e in moving])
        return moving

    for i, head0 in enumerate(starts):
        arrived = lax.all_to_all(outs[i], "tm", split_axis=0, concat_axis=0, tiled=True)
        arrived, outs[i + 1 :] = after((arrived, outs[i + 1 :]), ends[-1:])
        lo, hi = head0 * HEAD_DIM, (head0 + GROUPS[i]) * HEAD_DIM
        if i < len(GROUPS) - 1:
            local, *end = space_parts(arrived, space, params, head0, npos, True, True)
        else:
            end = space_parts(arrived, space, params, head0, npos, False, True)
            (local,) = space_parts(arrived, space, params, head0, npos, True, False)
        locals_.append(local)
        cuts.append((lo, hi))
        ends.append(end)
        width = RELAY * HEAD_DIM
        grows.append([growth[:, :, at : min(hi, at + width)] for at in range(lo, hi, width)])
        states.append([])
        send(i, 0, None)
        for j in range(i):
            if i - j <= hops - 1:
                send(j, i - j, end)
    moved = []
    for j in range(EARLY, len(GROUPS)):
        if len(states[j]) < hops:
            moved.append(send(j, len(states[j]), locals_[-1]))
    for j in range(EARLY):
        while len(states[j]) < hops:
            send(j, len(states[j]), locals_[-1])
    flat_states = lambda a, b: [r[p] for i in range(a, b) for p in range(len(ends[i])) for r in states[i]]
    acc, squares = finish(
        cuts[:EARLY], locals_[:EARLY], flat_states(0, EARLY), after(gate, moved), ecum, c, gain, w_out
    )
    for j in range(EARLY, len(GROUPS)):
        while len(states[j]) < hops:
            send(j, len(states[j]), squares)
    out = finish(
        cuts[EARLY:],
        locals_[EARLY:],
        flat_states(EARLY, len(GROUPS)),
        gate,
        ecum,
        c,
        gain,
        w_out,
        (acc, squares, tok),
    )
    return out.reshape(tokens.shape)


def solution(mesh):
    placed = (P("tm", "space", None, None), P(), P(), P(), P(), P(), P(), P(), P(), P())
    return jax.shard_map(
        body, mesh=mesh, in_specs=placed, out_specs=P("tm", "space", None, None), check_vma=False
    )
```

time: 674 us -> 170 us (0.25)
  waiting for transfers between devices: 343 us -> 46.7 us
  local copies, waits for them, and re-layouts: 163 us -> 4.55 us
  matrix products: 100 us -> 0 us
  Pallas kernels: 0 us -> 77.8 us
  other arithmetic: 37.3 us -> 2.23 us
  starting transfers between devices: 22.3 us -> 36.1 us
    ppermute x3 -> x12, waiting for transfers between devices: 271 us -> 14.8 us  [hop(): return lax.ppermute(state, 'space', [(k, k + 1)])]
    dot_general x20 -> x0, matrix products: 100 us -> none  [the longest x4 38.4 us: local_scan(): jnp.einsum('srh,rhp->shp', weights, signal, precision=lax.Precision.HIGHEST)]
    pallas_call x0 -> x12, Pallas kernels: none -> 77.8 us  [the longest x3 21.6 us: time_scan(): call(functools.partial(time_scan_kernel, n, m, fr, head0, prep is None),...]
    reshape x6 -> x0, local copies, waits for them, and re-layouts: 65.8 us -> none  [the longest x2 15 us: body(): sending = time_pack.reshape(fr_dev, n_tm, -1, time_pack.shape[-1])]
    all_to_all x2 -> x4, waiting for transfers between devices: 71.5 us -> 31.9 us  [the longest x3 22 us: body(): lax.all_to_all(outs[i], 'tm', split_axis=0, concat_axis=0, tiled=True)]
    another operation x6 -> x2, local copies, waits for them, and re-layouts: 21.1 us -> 0.61 us  [body(): jnp.stack([jnp.concatenate([dt_bias_time, dt_bias_space, fill]), jnp.conc...]
    slice x9 -> x1, local copies, waits for them, and re-layouts: 19.7 us -> 0.01 us  [body(): growth[:, :, at:min(hi, at + width)]]
    add x3 -> x0, other arithmetic: 17.7 us -> none  [relay_step(): return from_behind(growth * start_state + end_state, 'space', 1)]
  transfers between devices with their start and end apart: 5 -> 16, of which waited for: 5 -> 8; matrix products, arithmetic and copies ran while one was open for 4% -> 2% of each run, Pallas kernels for 0% -> 33%
where the time goes in v2:
time: 170 us; the launch traced here: 168 us
  Pallas kernels  77.8 us (46%)
  waiting for transfers between devices  46.7 us (27%)
  starting transfers between devices  36.1 us (21%)
  local copies, waits for them, and re-layouts  4.55 us (3%)
  other arithmetic  2.23 us (1%)
    all_to_all x3, waiting for transfers between devices, body(): lax.all_to_all(outs[i], 'tm', split_axis=0, concat_axis=0, tiled=True)  22 us
    pallas_call x3, Pallas kernels, time_scan(): call(functools.partial(time_scan_kernel, n, m, fr, head0, prep is None),...  21.6 us
    pallas_call x4, Pallas kernels, space_parts(): call(functools.partial(space_kernel, head0, npos, local), 'space' + '_loc...  19.9 us
    pallas_call x2, Pallas kernels, finish(): call(functools.partial(kernel, cuts), name, (fr,), in_specs + [pl.BlockSp...  19.2 us
    ppermute x12, starting transfers between devices, hop(): return lax.ppermute(state, 'space', [(k, k + 1)])  16.7 us
    all_to_all x3, starting transfers between devices, body(): lax.all_to_all(outs[i], 'tm', split_axis=0, concat_axis=0, tiled=True)  15 us
    ppermute x12, waiting for transfers between devices, hop(): return lax.ppermute(state, 'space', [(k, k + 1)])  14.8 us
    all_to_all x1, waiting for transfers between devices, body(): lax.all_to_all(arrange(tok, n, m), 'tm', split_axis=0, concat_axis=0, til...  9.91 us
  transfers between devices with their start and end apart: 16, of which 8 were waited for; matrix products, arithmetic and copies ran while one was open for 2% of the time, Pallas kernels for 33%

profile of v2, /device:TPU:18, one launch (start us, length us, event | category | flops | bytes accessed | tf_op | source)
XLA Modules:
  0.0 168.0 jit_solution(2159630222716295181)
XLA Ops:
  0.0 2.7 %arrange.1 = bf16[8,2,4,16,1024]{4,3,2,1,0:T(8,128)(2,1)} custom-call(bf16[4,240,1024]{2,1,0:T(8,128)(2,1)} %bitcast.40), custom_call_target="tpu_custom_call" | custom-call | bytes 3932160 | tf_op jit(solution)/shard_map/arrange/pallas_call | solution.py:92
  2.7 4.4 %all-to-all-start = ((bf16[8,2,4,16,1024]{4,3,2,1,0:T(8,128)(2,1)}), bf16[8,2,4,16,1024]{4,3,2,1,0:T(8,128)(2,1)S(1)}, u32[]{:S(2)}, u32[]{:S(2)}) async-start(bf16[8,2,4,16,1024]{4,3,2,1,0:T(8,128)(2,1)} %arrange.1), calls=%async_computation | async-start | bytes 4194304 | tf_op jit(solution)/shard_map/all_to_all | solution.py:509
  7.3 0.6 stack.23.par_ref.rest_2_.rest_3_
  7.9 6.4 %space_prep.1 = (f32[4,256,256]{2,1,0:T(8,128)}, f32[4,256,128]{2,1,0:T(8,128)}, f32[4,32,256]{2,1,0:T(8,128)}, bf16[4,2,256,128]{3,2,1,0:T(8,128)(2,1)}, bf16[4...) custom-call(bf16[4,240,1024]{2,1,0:T(8,128)(2,1)} %bitcast.41, ...), custom_call_target="tpu_custom_call" | custom-call | flops 503316480 | bytes 6291456 | tf_op jit(solution)/shard_map/space_prep/pallas_call | solution.py:189
  14.3 8.0 %gate_proj.1 = bf16[960,2048]{1,0:T(8,128)(2,1)} custom-call(bf16[960,1024]{1,0:T(8,128)(2,1)} %bitcast.42, bf16[4416,1024]{1,0:T(8,128)(2,1)} %bitcast.29), custom_call_target="tpu_custom_call" | custom-call | flops 4026531840 | bytes 10092544 | tf_op jit(solution)/shard_map/gate_proj/pallas_call | solution.py:110
  22.3 9.9 %all-to-all-done = bf16[8,2,4,16,1024]{4,3,2,1,0:T(8,128)(2,1)S(1)} async-done(((bf16[8,2,4,16,1024]{4,3,2,1,0:T(8,128)(2,1)}), bf16[8,2,4,16,1024]{4,3,2,1,0:T(8,128)(2,1)S(1)}, u32[]{:S(2)}, u32[]{:S(2)}) %all-to-all-start) | async-done | bytes 2097184 | tf_op jit(solution)/shard_map/all_to_all | solution.py:509
  32.2 1.4 copy-done
  33.6 10.0 %time_scan.3 = (bf16[8,2,4,16,1024]{4,3,2,1,0:T(8,128)(2,1)}, f32[4,256,256]{2,1,0:T(8,128)}, f32[4,256,128]{2,1,0:T(8,128)}, f32[4,32,256]{2,1,0:T(8,128)}) custom-call(bf16[1024,1024]{1,0:T(8,128)(2,1)} %bitcast.37, bf16[4416,1024]{1,0:T(8,128)(2,1)} %bitcast.30, bf16[4416,1024]{1,0:T(8,128)(2,1)} %bitcast.31, bf16[4416,1024]{1,0:T(8,128)(2,1)} %bitcast.32, ...), custom_call_target="tpu_custom_call" | custom-call | flops 3221225472 | bytes 8388608 | tf_op jit(solution)/shard_map/time_scan/pallas_call | solution.py:315
  43.6 5.0 %all-to-all-start.1 = ((bf16[8,2,4,16,1024]{4,3,2,1,0:T(8,128)(2,1)}), bf16[8,2,4,16,1024]{4,3,2,1,0:T(8,128)(2,1)S(1)}, u32[]{:S(2)}, u32[]{:S(2)}) async-start(bf16[8,2,4,16,1024]{4,3,2,1,0:T(8,128)(2,1)} %get-tuple-element.47), calls=%async_computation.1 | async-start | bytes 4194304 | tf_op jit(solution)/shard_map/all_to_all | solution.py:549
  48.6 5.8 %time_scan.5 = bf16[8,2,4,16,512]{4,3,2,1,0:T(8,128)(2,1)} custom-call(bf16[1024,1024]{1,0:T(8,128)(2,1)} %bitcast.38, bf16[4416,1024]{1,0:T(8,128)(2,1)} %bitcast.33, f32[4,256,256]{2,1,0:T(8,128)} %get-tuple-element.48.rest_0_, f32[4,256,128]{2,1,0:T(8,128)} %get-tuple-element.49.rest_1_, f32[4,32,256]{2,1,0:T(8,128)} %get-tuple-element.50.rest_2_, ...), custom_call_target="tpu_custom_call" | custom-call | flops 1610612736 | bytes 6291456 | tf_op jit(solution)/shard_map/time_scan/pallas_call | solution.py:315
  54.5 5.8 %time_scan.4 = bf16[8,2,4,16,512]{4,3,2,1,0:T(8,128)(2,1)} custom-call(bf16[1024,1024]{1,0:T(8,128)(2,1)} %bitcast.39, bf16[4416,1024]{1,0:T(8,128)(2,1)} %bitcast.34, f32[4,256,256]{2,1,0:T(8,128)} %get-tuple-element.48.rest_0_, f32[4,256,128]{2,1,0:T(8,128)} %get-tuple-element.49.rest_1_, f32[4,32,256]{2,1,0:T(8,128)} %get-tuple-element.50.rest_2_, ...), custom_call_target="tpu_custom_call" | custom-call | flops 1610612736 | bytes 6291456 | tf_op jit(solution)/shard_map/time_scan/pallas_call | solution.py:315
  60.3 13.5 %all-to-all-done.1.x_ref = bf16[8,2,4,16,1024]{4,3,2,1,0:T(8,128)(2,1)S(1)} async-done(((bf16[8,2,4,16,1024]{4,3,2,1,0:T(8,128)(2,1)}), bf16[8,2,4,16,1024]{4,3,2,1,0:T(8,128)(2,1)S(1)}, u32[]{:S(2)}, u32[]{:S(2)}) %all-to-all-start.1) | async-done | bytes 2097184 | tf_op jit(solution)/shard_map/all_to_all | solution.py:549
  73.8 5.0 %all-to-all-start.2 = ((bf16[8,2,4,16,512]{4,3,2,1,0:T(8,128)(2,1)}), bf16[8,2,4,16,512]{4,3,2,1,0:T(8,128)(2,1)S(1)}, u32[]{:S(2)}, u32[]{:S(2)}) async-start(bf16[8,2,4,16,512]{4,3,2,1,0:T(8,128)(2,1)} %time_scan.4), calls=%async_computation.2 | async-start | bytes 2097152 | tf_op jit(solution)/shard_map/all_to_all | solution.py:549
  78.8 7.8 %space_local_end.2 = (f32[4,240,1024]{2,1,0:T(8,128)}, bf16[4,64,512]{2,1,0:T(8,128)(2,1)}, bf16[4,64,512]{2,1,0:T(8,128)(2,1)}) custom-call(bf16[8,2,4,16,1024]{4,3,2,1,0:T(8,128)(2,1)} %copy-done.2, f32[4,256,256]{2,1,0:T(8,128)} %get-tuple-element.54.score_ref, f32[4,256,128]{2,1,0:T(8,128)} %get-tuple-element.55.cum_ref, ...), custom_call_target="tpu_custom_call" | custom-call | flops 1073741824 | bytes 8388608 | tf_op jit(solution)/shard_map/space_local_end/pallas_call | solution.py:375
  86.5 0.7 collective-permute-start.3
  87.2 0.7 collective-permute-start.4
  87.9 4.8 %all-to-all-done.2.x_ref = bf16[8,2,4,16,512]{4,3,2,1,0:T(8,128)(2,1)S(1)} async-done(((bf16[8,2,4,16,512]{4,3,2,1,0:T(8,128)(2,1)}), bf16[8,2,4,16,512]{4,3,2,1,0:T(8,128)(2,1)S(1)}, u32[]{:S(2)}, u32[]{:S(2)}) %all-to-all-start.2) | async-done | bytes 1048608 | tf_op jit(solution)/shard_map/all_to_all | solution.py:549
  92.7 5.0 %all-to-all-start.3 = ((bf16[8,2,4,16,512]{4,3,2,1,0:T(8,128)(2,1)}), bf16[8,2,4,16,512]{4,3,2,1,0:T(8,128)(2,1)S(1)}, u32[]{:S(2)}, u32[]{:S(2)}) async-start(bf16[8,2,4,16,512]{4,3,2,1,0:T(8,128)(2,1)} %time_scan.5), calls=%async_computation.3 | async-start | bytes 2097152 | tf_op jit(solution)/shard_map/all_to_all | solution.py:549
  97.7 4.8 %space_local_end.3 = (f32[4,240,512]{2,1,0:T(8,128)}, bf16[4,64,512]{2,1,0:T(8,128)(2,1)}) custom-call(bf16[8,2,4,16,512]{4,3,2,1,0:T(8,128)(2,1)} %copy-done.3, f32[4,256,256]{2,1,0:T(8,128)} %get-tuple-element.54.score_ref, f32[4,256,128]{2,1,0:T(8,128)} %get-tuple-element.55.cum_ref, f32[4,32,256]{2,1,0:T(8,128)} %get-tuple-element.56.row_ref, ...), custom_call_target="tpu_custom_call" | custom-call | flops 536870912 | bytes 5242880 | tf_op jit(solution)/shard_map/space_local_end/pallas_call | solution.py:375
  102.6 0.8 fusion.6
  103.4 1.3 collective-permute-start.6
  104.7 0.8 fusion.4
  105.5 1.4 collective-permute-start.5
  107.0 0.8 collective-permute-start
  107.8 3.8 %all-to-all-done.3.x_ref = bf16[8,2,4,16,512]{4,3,2,1,0:T(8,128)(2,1)S(1)} async-done(((bf16[8,2,4,16,512]{4,3,2,1,0:T(8,128)(2,1)}), bf16[8,2,4,16,512]{4,3,2,1,0:T(8,128)(2,1)S(1)}, u32[]{:S(2)}, u32[]{:S(2)}) %all-to-all-start.3) | async-done | bytes 1048608 | tf_op jit(solution)/shard_map/all_to_all | solution.py:549
  111.6 1.1 copy-done.1
  112.6 3.2 %space_end.1 = bf16[4,64,512]{2,1,0:T(8,128)(2,1)} custom-call(bf16[8,2,4,16,512]{4,3,2,1,0:T(8,128)(2,1)} %copy-done.1, f32[4,256,256]{2,1,0:T(8,128)} %get-tuple-element.54.score_ref, f32[4,256,128]{2,1,0:T(8,128)} %get-tuple-element.55.cum_ref, f32[4,32,256]{2,1,0:T(8,128)} %get-tuple-element.56.row_ref, ...), custom_call_target="tpu_custom_call" | custom-call | flops 536870912 | bytes 5242880 | tf_op jit(solution)/shard_map/space_end/pallas_call | solution.py:375
  115.8 0.7 collective-permute-start.2
  116.5 3.0 %collective-permute-done.5.rest_2_ = bf16[4,64,512]{2,1,0:T(8,128)(2,1)S(1)} collective-permute-done((bf16[4,64,512]{2,1,0:T(8,128)(2,1)}, bf16[4,64,512]{2,1,0:T(8,128)(2,1)S(1)}, u32[]{:S(2)}, u32[]{:S(2)}) %collective-permute-start.5) | collective-permute-done | bytes 262176 | tf_op jit(solution)/shard_map/ppermute | solution.py:487
  119.5 0.1 fusion.7
  119.6 0.1 fusion
  119.7 1.3 collective-permute-start.1
  121.0 0.1 fusion.5
  121.1 4.1 %space_local.1.rest_1_ = f32[4,240,512]{2,1,0:T(8,128)} custom-call(bf16[8,2,4,16,512]{4,3,2,1,0:T(8,128)(2,1)} %copy-done.1, f32[4,256,256]{2,1,0:T(8,128)} %get-tuple-element.54.score_ref, f32[4,256,128]{2,1,0:T(8,128)} %get-tuple-element.55.cum_ref, f32[4,32,256]{2,1,0:T(8,128)} %get-tuple-element.56.row_ref, ...), custom_call_target="tpu_custom_call" | custom-call | flops 536870912 | bytes 5242880 | tf_op jit(solution)/shard_map/space_local/pallas_call | solution.py:375
  125.2 1.3 collective-permute-start.7
  126.5 1.3 collective-permute-start.8
  127.9 0.1 fusion.2
  128.0 1.3 collective-permute-start.10
  129.3 0.1 fusion.1
  129.4 1.5 collective-permute-start.9
  130.9 2.3 %collective-permute-done.7.rest_3_ = bf16[4,64,512]{2,1,0:T(8,128)(2,1)S(1)} collective-permute-done((bf16[4,64,512]{2,1,0:T(8,128)(2,1)S(1)}, bf16[4,64,512]{2,1,0:T(8,128)(2,1)S(1)}, u32[]{:S(2)}, u32[]{:S(2)}) %collective-permute-start.7) | collective-permute-done | bytes 262176 | tf_op jit(solution)/shard_map/ppermute | solution.py:487
  133.3 5.6 %collective-permute-done.8.rest_6_ = bf16[4,64,512]{2,1,0:T(8,128)(2,1)S(1)} collective-permute-done((bf16[4,64,512]{2,1,0:T(8,128)(2,1)S(1)}, bf16[4,64,512]{2,1,0:T(8,128)(2,1)S(1)}, u32[]{:S(2)}, u32[]{:S(2)}) %collective-permute-start.8) | collective-permute-done | bytes 262176 | tf_op jit(solution)/shard_map/ppermute | solution.py:487
  138.9 0.7 copy-done.18
  139.6 9.4 %early.1 = (f32[4,240,1024]{2,1,0:T(8,128)}, f32[4,240,128]{2,1,0:T(8,128)}) custom-call(bf16[4,240,2048]{2,1,0:T(8,128)(2,1)} %bitcast.35, bf16[4,2,256,128]{3,2,1,0:T(8,128)(2,1)} %get-tuple-element.44.ecum_ref, bf16[4,256,64]{2,1,0:T(8,128)(2,1)} %get-tuple-element.45.c_ref, f32[1,2048]{1,0:T(1,128)} %bitcast.52, bf16[2048,1024]{1,0:T(8,128)(2,1)} %w_ref.3, ...), custom_call_target="tpu_custom_call" | custom-call | flops 2013265920 | bytes 13893632 | tf_op jit(solution)/shard_map/early/pallas_call | solution.py:473
  149.1 4.4 %collective-permute-start.11 = (bf16[4,64,512]{2,1,0:T(8,128)(2,1)S(1)}, bf16[4,64,512]{2,1,0:T(8,128)(2,1)S(1)}, u32[]{:S(2)}, u32[]{:S(2)}) collective-permute-start(bf16[4,64,512]{2,1,0:T(8,128)(2,1)S(1)} %fusion.3), channel_id=1, source_target_pairs={{2,3},{6,7},{10,11},{14,15},{18,19},{22,23},{26,27},{30,31}} | collective-permute-start | bytes 786440 | tf_op jit(solution)/shard_map/ppermute | solution.py:487
  153.6 3.8 %collective-permute-done.11.rest_7_ = bf16[4,64,512]{2,1,0:T(8,128)(2,1)S(1)} collective-permute-done((bf16[4,64,512]{2,1,0:T(8,128)(2,1)S(1)}, bf16[4,64,512]{2,1,0:T(8,128)(2,1)S(1)}, u32[]{:S(2)}, u32[]{:S(2)}) %collective-permute-start.11) | collective-permute-done | bytes 262176 | tf_op jit(solution)/shard_map/ppermute | solution.py:487
  157.4 0.7 copy-done.20
  158.1 9.8 %last.1 = bf16[4,240,1024]{2,1,0:T(8,128)(2,1)} custom-call(bf16[4,240,2048]{2,1,0:T(8,128)(2,1)} %bitcast.36, bf16[4,2,256,128]{3,2,1,0:T(8,128)(2,1)} %get-tuple-element.44.ecum_ref, bf16[4,256,64]{2,1,0:T(8,128)(2,1)} %get-tuple-element.45.c_ref, f32[1,2048]{1,0:T(1,128)} %bitcast.53, bf16[2048,1024]{1,0:T(8,128)(2,1)} %w_ref.3, ...), custom_call_target="tpu_custom_call" | custom-call | flops 2013265920 | bytes 13893632 | tf_op jit(solution)/shard_map/last/pallas_call | solution.py:473
  (71 shorter events, 0.3 us)
Async XLA Ops:
  2.7 4.4 %copy-start.26 = (f32[32]{0:T(128)S(1)}, f32[32]{0:T(128)}, u32[]{:S(2)}) copy-start(f32[32]{0:T(128)} %param.14) | copy-start | bytes 388
  2.7 4.4 %copy-start.27 = (f32[32]{0:T(128)S(1)}, f32[32]{0:T(128)}, u32[]{:S(2)}) copy-start(f32[32]{0:T(128)} %param.13) | copy-start | bytes 388
  2.7 4.5 %copy-start.22 = (f32[32]{0:T(128)S(1)}, f32[32]{0:T(128)}, u32[]{:S(2)}) copy-start(f32[32]{0:T(128)} %param.18) | copy-start | bytes 388
  2.7 4.5 %copy-start.23 = (f32[32]{0:T(128)S(1)}, f32[32]{0:T(128)}, u32[]{:S(2)}) copy-start(f32[32]{0:T(128)} %param.17) | copy-start | bytes 388
  2.7 4.5 %copy-start.24 = (f32[32]{0:T(128)S(1)}, f32[32]{0:T(128)}, u32[]{:S(2)}) copy-start(f32[32]{0:T(128)} %param.16) | copy-start | bytes 388
  2.7 4.5 %copy-start.25 = (f32[32]{0:T(128)S(1)}, f32[32]{0:T(128)}, u32[]{:S(2)}) copy-start(f32[32]{0:T(128)} %param.15) | copy-start | bytes 388
  2.7 29.5 %all-to-all-start = ((bf16[8,2,4,16,1024]{4,3,2,1,0:T(8,128)(2,1)}), bf16[8,2,4,16,1024]{4,3,2,1,0:T(8,128)(2,1)S(1)}, u32[]{:S(2)}, u32[]{:S(2)}) async-start(bf16[8,2,4,16,1024]{4,3,2,1,0:T(8,128)(2,1)} %arrange.1), calls=%async_computation | async-start | bytes 4194304 | tf_op jit(solution)/shard_map/all_to_all | solution.py:509
  32.2 1.4 copy-start
  43.6 30.2 %all-to-all-start.1 = ((bf16[8,2,4,16,1024]{4,3,2,1,0:T(8,128)(2,1)}), bf16[8,2,4,16,1024]{4,3,2,1,0:T(8,128)(2,1)S(1)}, u32[]{:S(2)}, u32[]{:S(2)}) async-start(bf16[8,2,4,16,1024]{4,3,2,1,0:T(8,128)(2,1)} %get-tuple-element.47), calls=%async_computation.1 | async-start | bytes 4194304 | tf_op jit(solution)/shard_map/all_to_all | solution.py:549
  73.8 5.0 %copy-start.2 = (bf16[8,2,4,16,1024]{4,3,2,1,0:T(8,128)(2,1)}, bf16[8,2,4,16,1024]{4,3,2,1,0:T(8,128)(2,1)S(1)}, u32[]{:S(2)}) copy-start(bf16[8,2,4,16,1024]{4,3,2,1,0:T(8,128)(2,1)S(1)} %all-to-all-done.1.x_ref) | copy-start | bytes 6291460
  73.8 18.9 %all-to-all-start.2 = ((bf16[8,2,4,16,512]{4,3,2,1,0:T(8,128)(2,1)}), bf16[8,2,4,16,512]{4,3,2,1,0:T(8,128)(2,1)S(1)}, u32[]{:S(2)}, u32[]{:S(2)}) async-start(bf16[8,2,4,16,512]{4,3,2,1,0:T(8,128)(2,1)} %time_scan.4), calls=%async_computation.2 | async-start | bytes 2097152 | tf_op jit(solution)/shard_map/all_to_all | solution.py:549
  86.5 11.1 %copy-start.21 = (f32[4,1,2048]{2,1,0:T(1,128)S(1)}, f32[4,1,2048]{2,1,0:T(1,128)}, u32[]{:S(2)}) copy-start(f32[4,1,2048]{2,1,0:T(1,128)} %get-tuple-element.63) | copy-start | bytes 98308
  86.5 16.0 %collective-permute-start.3 = (bf16[4,64,512]{2,1,0:T(8,128)(2,1)}, bf16[4,64,512]{2,1,0:T(8,128)(2,1)S(1)}, u32[]{:S(2)}, u32[]{:S(2)}) collective-permute-start(bf16[4,64,512]{2,1,0:T(8,128)(2,1)} %get-tuple-element.59), channel_id=1, source_target_pairs={{0,1},{4,5},{8,9},{12,13},{16,17},{20,21},{24,25},{28,29}} | collective-permute-start | bytes 786440 | tf_op jit(solution)/shard_map/ppermute | solution.py:487
  87.2 15.3 %collective-permute-start.4 = (bf16[4,64,512]{2,1,0:T(8,128)(2,1)}, bf16[4,64,512]{2,1,0:T(8,128)(2,1)S(1)}, u32[]{:S(2)}, u32[]{:S(2)}) collective-permute-start(bf16[4,64,512]{2,1,0:T(8,128)(2,1)} %get-tuple-element.60), channel_id=1, source_target_pairs={{0,1},{4,5},{8,9},{12,13},{16,17},{20,21},{24,25},{28,29}} | collective-permute-start | bytes 786440 | tf_op jit(solution)/shard_map/ppermute | solution.py:487
  92.7 5.0 %copy-start.3 = (bf16[8,2,4,16,512]{4,3,2,1,0:T(8,128)(2,1)}, bf16[8,2,4,16,512]{4,3,2,1,0:T(8,128)(2,1)S(1)}, u32[]{:S(2)}) copy-start(bf16[8,2,4,16,512]{4,3,2,1,0:T(8,128)(2,1)S(1)} %all-to-all-done.2.x_ref) | copy-start | bytes 3145732
  92.7 18.9 %all-to-all-start.3 = ((bf16[8,2,4,16,512]{4,3,2,1,0:T(8,128)(2,1)}), bf16[8,2,4,16,512]{4,3,2,1,0:T(8,128)(2,1)S(1)}, u32[]{:S(2)}, u32[]{:S(2)}) async-start(bf16[8,2,4,16,512]{4,3,2,1,0:T(8,128)(2,1)} %time_scan.5), calls=%async_computation.3 | async-start | bytes 2097152 | tf_op jit(solution)/shard_map/all_to_all | solution.py:549
  97.7 4.9 %copy-start.11 = (bf16[4,64,512]{2,1,0:T(8,128)(2,1)S(1)}, bf16[4,64,512]{2,1,0:T(8,128)(2,1)}, u32[]{:S(2)}) copy-start(bf16[4,64,512]{2,1,0:T(8,128)(2,1)} %get-tuple-element.60) | copy-start | bytes 786436
  97.7 7.0 %copy-start.9 = (bf16[4,64,512]{2,1,0:T(8,128)(2,1)S(1)}, bf16[4,64,512]{2,1,0:T(8,128)(2,1)}, u32[]{:S(2)}) copy-start(bf16[4,64,512]{2,1,0:T(8,128)(2,1)} %get-tuple-element.59) | copy-start | bytes 786436
  102.6 13.3 %copy-start.5 = (bf16[4,64,512]{2,1,0:T(8,128)(2,1)}, bf16[4,64,512]{2,1,0:T(8,128)(2,1)S(1)}, u32[]{:S(2)}) copy-start(bf16[4,64,512]{2,1,0:T(8,128)(2,1)S(1)} %collective-permute-done.3.rest_1_) | copy-start | bytes 786436
  102.6 13.2 %copy-start.6 = (bf16[4,64,512]{2,1,0:T(8,128)(2,1)}, bf16[4,64,512]{2,1,0:T(8,128)(2,1)S(1)}, u32[]{:S(2)}) copy-start(bf16[4,64,512]{2,1,0:T(8,128)(2,1)S(1)} %collective-permute-done.4.rest_4_) | copy-start | bytes 786436
  103.4 13.1 %collective-permute-start.6 = (bf16[4,64,512]{2,1,0:T(8,128)(2,1)}, bf16[4,64,512]{2,1,0:T(8,128)(2,1)S(1)}, u32[]{:S(2)}, u32[]{:S(2)}) collective-permute-start(bf16[4,64,512]{2,1,0:T(8,128)(2,1)} %fusion.6), channel_id=1, source_target_pairs={{1,2},{5,6},{9,10},{13,14},{17,18},{21,22},{25,26},{29,30}} | collective-permute-start | bytes 786440 | tf_op jit(solution)/shard_map/ppermute | solution.py:487
  105.5 14.0 %copy-start.12 = (bf16[4,64,512]{2,1,0:T(8,128)(2,1)S(1)}, bf16[4,64,512]{2,1,0:T(8,128)(2,1)}, u32[]{:S(2)}) copy-start(bf16[4,64,512]{2,1,0:T(8,128)(2,1)} %get-tuple-element.60) | copy-start | bytes 786436
  105.5 14.0 %collective-permute-start.5 = (bf16[4,64,512]{2,1,0:T(8,128)(2,1)}, bf16[4,64,512]{2,1,0:T(8,128)(2,1)S(1)}, u32[]{:S(2)}, u32[]{:S(2)}) collective-permute-start(bf16[4,64,512]{2,1,0:T(8,128)(2,1)} %fusion.4), channel_id=1, source_target_pairs={{1,2},{5,6},{9,10},{13,14},{17,18},{21,22},{25,26},{29,30}} | collective-permute-start | bytes 786440 | tf_op jit(solution)/shard_map/ppermute | solution.py:487
  107.0 12.7 %copy-start.10 = (bf16[4,64,512]{2,1,0:T(8,128)(2,1)S(1)}, bf16[4,64,512]{2,1,0:T(8,128)(2,1)}, u32[]{:S(2)}) copy-start(bf16[4,64,512]{2,1,0:T(8,128)(2,1)} %get-tuple-element.62) | copy-start | bytes 786436
  107.0 12.6 %collective-permute-start = (bf16[4,64,512]{2,1,0:T(8,128)(2,1)}, bf16[4,64,512]{2,1,0:T(8,128)(2,1)S(1)}, u32[]{:S(2)}, u32[]{:S(2)}) collective-permute-start(bf16[4,64,512]{2,1,0:T(8,128)(2,1)} %get-tuple-element.62), channel_id=1, source_target_pairs={{0,1},{4,5},{8,9},{12,13},{16,17},{20,21},{24,25},{28,29}} | collective-permute-start | bytes 786440 | tf_op jit(solution)/shard_map/ppermute | solution.py:487
  111.6 1.1 copy-start.1
  115.8 12.0 %collective-permute-start.2 = (bf16[4,64,512]{2,1,0:T(8,128)(2,1)}, bf16[4,64,512]{2,1,0:T(8,128)(2,1)S(1)}, u32[]{:S(2)}, u32[]{:S(2)}) collective-permute-start(bf16[4,64,512]{2,1,0:T(8,128)(2,1)} %space_end.1), channel_id=1, source_target_pairs={{0,1},{4,5},{8,9},{12,13},{16,17},{20,21},{24,25},{28,29}} | collective-permute-start | bytes 786440 | tf_op jit(solution)/shard_map/ppermute | solution.py:487
  116.5 8.7 %copy-start.7 = (bf16[4,64,512]{2,1,0:T(8,128)(2,1)}, bf16[4,64,512]{2,1,0:T(8,128)(2,1)S(1)}, u32[]{:S(2)}) copy-start(bf16[4,64,512]{2,1,0:T(8,128)(2,1)S(1)} %collective-permute-done.6.rest_5_) | copy-start | bytes 786436
  119.5 5.7 %copy-start.8 = (bf16[4,64,512]{2,1,0:T(8,128)(2,1)}, bf16[4,64,512]{2,1,0:T(8,128)(2,1)S(1)}, u32[]{:S(2)}) copy-start(bf16[4,64,512]{2,1,0:T(8,128)(2,1)S(1)} %collective-permute-done.5.rest_2_) | copy-start | bytes 786436
  119.6 5.6 %copy-start.13 = (bf16[4,64,512]{2,1,0:T(8,128)(2,1)}, bf16[4,64,512]{2,1,0:T(8,128)(2,1)S(1)}, u32[]{:S(2)}) copy-start(bf16[4,64,512]{2,1,0:T(8,128)(2,1)S(1)} %collective-permute-done.rest_2_) | copy-start | bytes 786436
  119.7 9.5 %collective-permute-start.1 = (bf16[4,64,512]{2,1,0:T(8,128)(2,1)S(1)}, bf16[4,64,512]{2,1,0:T(8,128)(2,1)S(1)}, u32[]{:S(2)}, u32[]{:S(2)}) collective-permute-start(bf16[4,64,512]{2,1,0:T(8,128)(2,1)S(1)} %fusion), channel_id=1, source_target_pairs={{1,2},{5,6},{9,10},{13,14},{17,18},{21,22},{25,26},{29,30}} | collective-permute-start | bytes 786440 | tf_op jit(solution)/shard_map/ppermute | solution.py:487
  121.1 6.8 %copy-start.4 = (bf16[4,64,512]{2,1,0:T(8,128)(2,1)S(1)}, bf16[4,64,512]{2,1,0:T(8,128)(2,1)}, u32[]{:S(2)}) copy-start(bf16[4,64,512]{2,1,0:T(8,128)(2,1)} %space_end.1) | copy-start | bytes 786436
  125.2 8.0 %collective-permute-start.7 = (bf16[4,64,512]{2,1,0:T(8,128)(2,1)S(1)}, bf16[4,64,512]{2,1,0:T(8,128)(2,1)S(1)}, u32[]{:S(2)}, u32[]{:S(2)}) collective-permute-start(bf16[4,64,512]{2,1,0:T(8,128)(2,1)S(1)} %fusion.5), channel_id=1, source_target_pairs={{2,3},{6,7},{10,11},{14,15},{18,19},{22,23},{26,27},{30,31}} | collective-permute-start | bytes 786440 | tf_op jit(solution)/shard_map/ppermute | solution.py:487
  126.5 12.3 %collective-permute-start.8 = (bf16[4,64,512]{2,1,0:T(8,128)(2,1)S(1)}, bf16[4,64,512]{2,1,0:T(8,128)(2,1)S(1)}, u32[]{:S(2)}, u32[]{:S(2)}) collective-permute-start(bf16[4,64,512]{2,1,0:T(8,128)(2,1)S(1)} %fusion.7), channel_id=1, source_target_pairs={{2,3},{6,7},{10,11},{14,15},{18,19},{22,23},{26,27},{30,31}} | collective-permute-start | bytes 786440 | tf_op jit(solution)/shard_map/ppermute | solution.py:487
  127.9 21.1 %copy-start.14 = (bf16[4,64,512]{2,1,0:T(8,128)(2,1)}, bf16[4,64,512]{2,1,0:T(8,128)(2,1)S(1)}, u32[]{:S(2)}) copy-start(bf16[4,64,512]{2,1,0:T(8,128)(2,1)S(1)} %collective-permute-done.2.rest_5_) | copy-start | bytes 786436
  128.0 21.0 %collective-permute-start.10 = (bf16[4,64,512]{2,1,0:T(8,128)(2,1)S(1)}, bf16[4,64,512]{2,1,0:T(8,128)(2,1)S(1)}, u32[]{:S(2)}, u32[]{:S(2)}) collective-permute-start(bf16[4,64,512]{2,1,0:T(8,128)(2,1)S(1)} %fusion.2), channel_id=1, source_target_pairs={{1,2},{5,6},{9,10},{13,14},{17,18},{21,22},{25,26},{29,30}} | collective-permute-start | bytes 786440 | tf_op jit(solution)/shard_map/ppermute | solution.py:487
  129.3 19.7 %copy-start.15 = (bf16[4,64,512]{2,1,0:T(8,128)(2,1)}, bf16[4,64,512]{2,1,0:T(8,128)(2,1)S(1)}, u32[]{:S(2)}) copy-start(bf16[4,64,512]{2,1,0:T(8,128)(2,1)S(1)} %collective-permute-done.1.rest_3_) | copy-start | bytes 786436
  129.4 24.2 %collective-permute-start.9 = (bf16[4,64,512]{2,1,0:T(8,128)(2,1)S(1)}, bf16[4,64,512]{2,1,0:T(8,128)(2,1)S(1)}, u32[]{:S(2)}, u32[]{:S(2)}) collective-permute-start(bf16[4,64,512]{2,1,0:T(8,128)(2,1)S(1)} %fusion.1), channel_id=1, source_target_pairs={{2,3},{6,7},{10,11},{14,15},{18,19},{22,23},{26,27},{30,31}} | collective-permute-start | bytes 786440 | tf_op jit(solution)/shard_map/ppermute | solution.py:487
  133.3 5.6 %copy-start.17 = (bf16[4,64,512]{2,1,0:T(8,128)(2,1)}, bf16[4,64,512]{2,1,0:T(8,128)(2,1)S(1)}, u32[]{:S(2)}) copy-start(bf16[4,64,512]{2,1,0:T(8,128)(2,1)S(1)} %collective-permute-done.7.rest_3_) | copy-start | bytes 786436
  138.9 0.7 copy-start.18
  149.0 8.4 %copy-start.16 = (bf16[4,64,512]{2,1,0:T(8,128)(2,1)}, bf16[4,64,512]{2,1,0:T(8,128)(2,1)S(1)}, u32[]{:S(2)}) copy-start(bf16[4,64,512]{2,1,0:T(8,128)(2,1)S(1)} %collective-permute-done.10.rest_6_) | copy-start | bytes 786436
  149.1 8.3 %collective-permute-start.11 = (bf16[4,64,512]{2,1,0:T(8,128)(2,1)S(1)}, bf16[4,64,512]{2,1,0:T(8,128)(2,1)S(1)}, u32[]{:S(2)}, u32[]{:S(2)}) collective-permute-start(bf16[4,64,512]{2,1,0:T(8,128)(2,1)S(1)} %fusion.3), channel_id=1, source_target_pairs={{2,3},{6,7},{10,11},{14,15},{18,19},{22,23},{26,27},{30,31}} | collective-permute-start | bytes 786440 | tf_op jit(solution)/shard_map/ppermute | solution.py:487
  153.5 3.9 %copy-start.19 = (bf16[4,64,512]{2,1,0:T(8,128)(2,1)}, bf16[4,64,512]{2,1,0:T(8,128)(2,1)S(1)}, u32[]{:S(2)}) copy-start(bf16[4,64,512]{2,1,0:T(8,128)(2,1)S(1)} %collective-permute-done.9.rest_4_) | copy-start | bytes 786436
  157.4 0.7 copy-start.20

commit v3 on v2

--- a/solution.py
+++ b/solution.py
@@ -17,13 +17,13 @@
 LOG2E = 1.4426950408889634
 TOP = 64.0
 GROUPS = (16, 8, 8)
-RELAY = 8
+RELAY = 16
 EARLY = 1
 TIME_STEP = 8
 BF = jnp.bfloat16
 F32 = jnp.float32
 VMEM = 58 * 1024 * 1024
-VMEM_TAIL = 58 * 1024 * 1024
+VMEM_TAIL = 40 * 1024 * 1024
 
 
 def call(kernel, name, grid, in_specs, out_specs, out_shape, flops, moved, scratch=(), vmem=VMEM):
@@ -56,20 +56,23 @@
     return jnp.maximum(x, 0.0) + jnp.log1p(jnp.exp(-jnp.abs(x)))
 
 
-def split2(v):
-    high = v.astype(BF)
-    return high, (v - high.astype(F32)).astype(BF)
-
-
 def spread_heads(head0, cols):
     row = lax.broadcasted_iota(jnp.int32, (LANES, cols), 0)
     col = lax.broadcasted_iota(jnp.int32, (LANES, cols), 1)
     return jnp.where(row - HEADS - head0 == col // HEAD_DIM, 1.0, 0.0).astype(BF)
 
 
+def split2(v):
+    high = v.astype(BF)
+    return jnp.concatenate([high, (v - high.astype(F32)).astype(BF)], axis=1)
+
+
+def widen_split(parts, spread):
+    return dot(parts, jnp.concatenate([spread, spread], axis=0))
+
+
 def widen(values, spread):
-    high, low = split2(values)
-    return dot(high, spread) + dot(low, spread)
+    return widen_split(split2(values), spread)
 
 
 def full(shape):
@@ -158,12 +161,8 @@
     cum_ref[0] = cum
     row_ref[0] = rowterm.T[HEADS : 2 * HEADS]
     tail = jnp.exp2(jnp.minimum(total + rowterm, TOP))
-    t_hi, t_lo = split2(tail)
-    tail_ref[0, 0] = t_hi
-    tail_ref[0, 1] = t_lo
-    e_hi, e_lo = split2(jnp.exp2(cum))
-    ecum_ref[0, 0] = e_hi
-    ecum_ref[0, 1] = e_lo
+    tail_ref[0] = split2(tail)
+    ecum_ref[0] = split2(jnp.exp2(cum))
     b_ref[0] = b
     c_ref[0] = c
     growth = jnp.broadcast_to(jnp.exp2(total), (8, LANES))
@@ -180,8 +179,8 @@
         ((size, size), F32),
         ((size, LANES), F32),
         ((HEADS, size), F32),
-        ((2, size, LANES), BF),
-        ((2, size, LANES), BF),
+        ((size, 2 * LANES), BF),
+        ((size, 2 * LANES), BF),
         ((size, STATE), BF),
         ((size, STATE), BF),
         ((1, DI), F32),
@@ -330,7 +329,7 @@
 
 
 def end_of(x, f, tail_ref, b_ref, spread):
-    wide = dot(tail_ref[f, 0], spread) + dot(tail_ref[f, 1], spread)
+    wide = widen_split(tail_ref[f], spread)
     return dot_tn(b_ref[f], (x.astype(F32) * wide).astype(BF)).astype(BF)
 
 
@@ -381,7 +380,7 @@
             l_frames((size, size)),
             l_frames((size, LANES)),
             l_frames((HEADS, size)),
-            e_frames((2, size, LANES)),
+            e_frames((size, 2 * LANES)),
             e_frames((size, STATE)),
             full(params.shape),
         ],
@@ -396,9 +395,9 @@
     state = sum(ref[0].astype(F32) for ref in states)
     npos = local.shape[0]
     carried = dot(c_ref[0], state.astype(BF))[:npos]
-    wide = (dot(ecum_ref[0, 0], spread) + dot(ecum_ref[0, 1], spread))[:npos]
+    wide = widen_split(ecum_ref[0], spread)[:npos]
     z = z.astype(F32)
-    return (local + wide * carried) * (z * jax.nn.sigmoid(z))
+    return (local + wide * carried) * (0.5 * z * (1.0 + jnp.tanh(0.5 * z)))
 
 
 def lane_sums(v):
@@ -454,7 +453,7 @@
     wide, narrow = pl.BlockSpec((1, npos, D), per_frame), pl.BlockSpec((1, npos, LANES), per_frame)
     in_specs = [
         pl.BlockSpec((1, npos, cols), lambda f: (f, 0, own)),
-        pl.BlockSpec((1, 2, size, LANES), lambda f: (f, 0, 0, 0)),
+        pl.BlockSpec((1, size, 2 * LANES), per_frame),
         pl.BlockSpec((1, size, STATE), per_frame),
         pl.BlockSpec((1, cols), lambda f: (0, own)),
         pl.BlockSpec((cols, D), lambda f: (own, 0)),
@@ -549,35 +548,25 @@
         arrived = lax.all_to_all(outs[i], "tm", split_axis=0, concat_axis=0, tiled=True)
         arrived, outs[i + 1 :] = after((arrived, outs[i + 1 :]), ends[-1:])
         lo, hi = head0 * HEAD_DIM, (head0 + GROUPS[i]) * HEAD_DIM
-        if i < len(GROUPS) - 1:
-            local, *end = space_parts(arrived, space, params, head0, npos, True, True)
-        else:
-            end = space_parts(arrived, space, params, head0, npos, False, True)
-            (local,) = space_parts(arrived, space, params, head0, npos, True, False)
+        local, *end = space_parts(arrived, space, params, head0, npos, True, True)
         locals_.append(local)
         cuts.append((lo, hi))
         ends.append(end)
         width = RELAY * HEAD_DIM
         grows.append([growth[:, :, at : min(hi, at + width)] for at in range(lo, hi, width)])
         states.append([])
-        send(i, 0, None)
+        moved = send(i, 0, None)
         for j in range(i):
             if i - j <= hops - 1:
-                send(j, i - j, end)
-    moved = []
-    for j in range(EARLY, len(GROUPS)):
-        if len(states[j]) < hops:
-            moved.append(send(j, len(states[j]), locals_[-1]))
-    for j in range(EARLY):
-        while len(states[j]) < hops:
-            send(j, len(states[j]), locals_[-1])
+                moved = moved + send(j, i - j, end)
+    while any(len(hopped) < hops for hopped in states):
+        for j, hopped in enumerate(states):
+            if len(hopped) < hops:
+                moved = send(j, len(hopped), None)
     flat_states = lambda a, b: [r[p] for i in range(a, b) for p in range(len(ends[i])) for r in states[i]]
     acc, squares = finish(
         cuts[:EARLY], locals_[:EARLY], flat_states(0, EARLY), after(gate, moved), ecum, c, gain, w_out
     )
-    for j in range(EARLY, len(GROUPS)):
-        while len(states[j]) < hops:
-            send(j, len(states[j]), squares)
     out = finish(
         cuts[EARLY:],
         locals_[EARLY:],

time: 170 us -> 157 us (0.924)
  Pallas kernels: 77.8 us -> 70 us
  starting transfers between devices: 36.1 us -> 29.6 us
    ppermute x12 -> x9, starting transfers between devices: 16.7 us -> 10.2 us  [hop(): return lax.ppermute(state, 'space', [(k, k + 1)])]
    pallas_call x2, Pallas kernels: 19.2 us -> 14.8 us  [finish(): call(functools.partial(kernel, cuts), name, (fr,), in_specs + [pl.BlockSp...]
    all_to_all x3, waiting for transfers between devices: 22 us -> 25.8 us  [body(): lax.all_to_all(outs[i], 'tm', split_axis=0, concat_axis=0, tiled=True)]
    pallas_call x4 -> x3, Pallas kernels: 19.9 us -> 16.1 us  [space_parts(): call(functools.partial(space_kernel, head0, npos, local), 'space' + '_loc...]
    ppermute x12 -> x9, waiting for transfers between devices: 14.8 us -> 11.3 us  [hop(): return lax.ppermute(state, 'space', [(k, k + 1)])]
    convert_element_type x8 -> x6, other arithmetic: 2.14 us -> 3.48 us  [join(): return (end.astype(F32) + growth * start.astype(F32)).astype(BF)]
    unnamed x60 -> x47, local copies, waits for them, and re-layouts: 3.93 us -> 4.34 us
  transfers between devices with their start and end apart: 16 -> 13, of which waited for: 8 -> 8; matrix products, arithmetic and copies ran while one was open for 2% -> 3% of each run, Pallas kernels for 33% -> 32%
where the time goes in v3:
time: 157 us; the launch traced here: 155 us
  Pallas kernels  70 us (45%)
  waiting for transfers between devices  46.8 us (30%)
  starting transfers between devices  29.6 us (19%)
  local copies, waits for them, and re-layouts  4.96 us (3%)
  other arithmetic  3.57 us (2%)
    all_to_all x3, waiting for transfers between devices, body(): lax.all_to_all(outs[i], 'tm', split_axis=0, concat_axis=0, tiled=True)  25.8 us
    pallas_call x3, Pallas kernels, time_scan(): call(functools.partial(time_scan_kernel, n, m, fr, head0, prep is None),...  21.7 us
    pallas_call x3, Pallas kernels, space_parts(): call(functools.partial(space_kernel, head0, npos, local), 'space' + '_loc...  16.1 us
    all_to_all x3, starting transfers between devices, body(): lax.all_to_all(outs[i], 'tm', split_axis=0, concat_axis=0, tiled=True)  15 us
    pallas_call x2, Pallas kernels, finish(): call(functools.partial(kernel, cuts), name, (fr,), in_specs + [pl.BlockSp...  14.8 us
    ppermute x9, waiting for transfers between devices, hop(): return lax.ppermute(state, 'space', [(k, k + 1)])  11.3 us
    ppermute x9, starting transfers between devices, hop(): return lax.ppermute(state, 'space', [(k, k + 1)])  10.2 us
    all_to_all x1, waiting for transfers between devices, body(): lax.all_to_all(arrange(tok, n, m), 'tm', split_axis=0, concat_axis=0, til...  9.62 us
  transfers between devices with their start and end apart: 13, of which 8 were waited for; matrix products, arithmetic and copies ran while one was open for 3% of the time, Pallas kernels for 32%

profile of v3, /device:TPU:18, one launch (start us, length us, event | category | flops | bytes accessed | tf_op | source)
XLA Modules:
  0.0 155.3 jit_solution(13641709664433578325)
XLA Ops:
  0.0 2.7 %arrange.1 = bf16[8,2,4,16,1024]{4,3,2,1,0:T(8,128)(2,1)} custom-call(bf16[4,240,1024]{2,1,0:T(8,128)(2,1)} %bitcast.26), custom_call_target="tpu_custom_call" | custom-call | bytes 3932160 | tf_op jit(solution)/shard_map/arrange/pallas_call | solution.py:95
  2.7 0.0 copy-start.18
  2.7 0.0 copy-start.19
  2.7 4.4 %all-to-all-start = ((bf16[8,2,4,16,1024]{4,3,2,1,0:T(8,128)(2,1)}), bf16[8,2,4,16,1024]{4,3,2,1,0:T(8,128)(2,1)S(1)}, u32[]{:S(2)}, u32[]{:S(2)}) async-start(bf16[8,2,4,16,1024]{4,3,2,1,0:T(8,128)(2,1)} %arrange.1), calls=%async_computation | async-start | bytes 4194304 | tf_op jit(solution)/shard_map/all_to_all | solution.py:508
  7.2 0.1 fusion.9
  7.3 0.6 stack.23.par_ref.rest_2_.rest_3_
  7.9 6.7 %space_prep.1 = (f32[4,256,256]{2,1,0:T(8,128)}, f32[4,256,128]{2,1,0:T(8,128)}, f32[4,32,256]{2,1,0:T(8,128)}, bf16[4,256,256]{2,1,0:T(8,128)(2,1)}, bf16[4,256...) custom-call(bf16[4,240,1024]{2,1,0:T(8,128)(2,1)} %bitcast.27, ...), custom_call_target="tpu_custom_call" | custom-call | flops 503316480 | bytes 6291456 | tf_op jit(solution)/shard_map/space_prep/pallas_call | solution.py:188
  14.6 8.0 %gate_proj.1 = bf16[960,2048]{1,0:T(8,128)(2,1)} custom-call(bf16[960,1024]{1,0:T(8,128)(2,1)} %bitcast.28, bf16[4416,1024]{1,0:T(8,128)(2,1)} %bitcast.34), custom_call_target="tpu_custom_call" | custom-call | flops 4026531840 | bytes 10092544 | tf_op jit(solution)/shard_map/gate_proj/pallas_call | solution.py:113
  22.6 9.6 %all-to-all-done = bf16[8,2,4,16,1024]{4,3,2,1,0:T(8,128)(2,1)S(1)} async-done(((bf16[8,2,4,16,1024]{4,3,2,1,0:T(8,128)(2,1)}), bf16[8,2,4,16,1024]{4,3,2,1,0:T(8,128)(2,1)S(1)}, u32[]{:S(2)}, u32[]{:S(2)}) %all-to-all-start) | async-done | bytes 2097184 | tf_op jit(solution)/shard_map/all_to_all | solution.py:508
  32.2 1.4 copy-done.8
  33.6 10.0 %time_scan.3 = (bf16[8,2,4,16,1024]{4,3,2,1,0:T(8,128)(2,1)}, f32[4,256,256]{2,1,0:T(8,128)}, f32[4,256,128]{2,1,0:T(8,128)}, f32[4,32,256]{2,1,0:T(8,128)}) custom-call(bf16[1024,1024]{1,0:T(8,128)(2,1)} %bitcast.40, bf16[4416,1024]{1,0:T(8,128)(2,1)} %bitcast.35, bf16[4416,1024]{1,0:T(8,128)(2,1)} %bitcast.36, bf16[4416,1024]{1,0:T(8,128)(2,1)} %bitcast.37, ...), custom_call_target="tpu_custom_call" | custom-call | flops 3221225472 | bytes 8388608 | tf_op jit(solution)/shard_map/time_scan/pallas_call | solution.py:314
  43.6 5.0 %all-to-all-start.1 = ((bf16[8,2,4,16,1024]{4,3,2,1,0:T(8,128)(2,1)}), bf16[8,2,4,16,1024]{4,3,2,1,0:T(8,128)(2,1)S(1)}, u32[]{:S(2)}, u32[]{:S(2)}) async-start(bf16[8,2,4,16,1024]{4,3,2,1,0:T(8,128)(2,1)} %get-tuple-element.43), calls=%async_computation.1 | async-start | bytes 4194304 | tf_op jit(solution)/shard_map/all_to_all | solution.py:548
  48.6 5.9 %time_scan.4 = bf16[8,2,4,16,512]{4,3,2,1,0:T(8,128)(2,1)} custom-call(bf16[1024,1024]{1,0:T(8,128)(2,1)} %bitcast.41, bf16[4416,1024]{1,0:T(8,128)(2,1)} %bitcast.38, f32[4,256,256]{2,1,0:T(8,128)} %get-tuple-element.44.rest_0_, f32[4,256,128]{2,1,0:T(8,128)} %get-tuple-element.45.rest_1_, f32[4,32,256]{2,1,0:T(8,128)} %get-tuple-element.46.rest_2_, ...), custom_call_target="tpu_custom_call" | custom-call | flops 1610612736 | bytes 6291456 | tf_op jit(solution)/shard_map/time_scan/pallas_call | solution.py:314
  54.5 5.8 %time_scan.5 = bf16[8,2,4,16,512]{4,3,2,1,0:T(8,128)(2,1)} custom-call(bf16[1024,1024]{1,0:T(8,128)(2,1)} %bitcast.42, bf16[4416,1024]{1,0:T(8,128)(2,1)} %bitcast.39, f32[4,256,256]{2,1,0:T(8,128)} %get-tuple-element.44.rest_0_, f32[4,256,128]{2,1,0:T(8,128)} %get-tuple-element.45.rest_1_, f32[4,32,256]{2,1,0:T(8,128)} %get-tuple-element.46.rest_2_, ...), custom_call_target="tpu_custom_call" | custom-call | flops 1610612736 | bytes 6291456 | tf_op jit(solution)/shard_map/time_scan/pallas_call | solution.py:314
  60.3 13.4 %all-to-all-done.1.x_ref = bf16[8,2,4,16,1024]{4,3,2,1,0:T(8,128)(2,1)S(1)} async-done(((bf16[8,2,4,16,1024]{4,3,2,1,0:T(8,128)(2,1)}), bf16[8,2,4,16,1024]{4,3,2,1,0:T(8,128)(2,1)S(1)}, u32[]{:S(2)}, u32[]{:S(2)}) %all-to-all-start.1) | async-done | bytes 2097184 | tf_op jit(solution)/shard_map/all_to_all | solution.py:548
  73.8 5.0 %all-to-all-start.2 = ((bf16[8,2,4,16,512]{4,3,2,1,0:T(8,128)(2,1)}), bf16[8,2,4,16,512]{4,3,2,1,0:T(8,128)(2,1)S(1)}, u32[]{:S(2)}, u32[]{:S(2)}) async-start(bf16[8,2,4,16,512]{4,3,2,1,0:T(8,128)(2,1)} %time_scan.4), calls=%async_computation.2 | async-start | bytes 2097152 | tf_op jit(solution)/shard_map/all_to_all | solution.py:548
  78.7 6.8 %space_local_end.3 = (f32[4,240,1024]{2,1,0:T(8,128)}, bf16[4,64,1024]{2,1,0:T(8,128)(2,1)}) custom-call(bf16[8,2,4,16,1024]{4,3,2,1,0:T(8,128)(2,1)} %copy-done.9, f32[4,256,256]{2,1,0:T(8,128)} %get-tuple-element.50.score_ref, f32[4,256,128]{2,1,0:T(8,128)} %get-tuple-element.51.cum_ref, f32[4,32,256]{2,1,0:T(8,128)} %get-tuple-element.52.row_ref, ...), custom_call_target="tpu_custom_call" | custom-call | flops 1073741824 | bytes 8388608 | tf_op jit(solution)/shard_map/space_local_end/pallas_call | solution.py:374
  85.6 0.7 collective-permute-start.2
  86.3 6.4 %all-to-all-done.2.x_ref = bf16[8,2,4,16,512]{4,3,2,1,0:T(8,128)(2,1)S(1)} async-done(((bf16[8,2,4,16,512]{4,3,2,1,0:T(8,128)(2,1)}), bf16[8,2,4,16,512]{4,3,2,1,0:T(8,128)(2,1)S(1)}, u32[]{:S(2)}, u32[]{:S(2)}) %all-to-all-start.2) | async-done | bytes 1048608 | tf_op jit(solution)/shard_map/all_to_all | solution.py:548
  92.7 5.0 %all-to-all-start.3 = ((bf16[8,2,4,16,512]{4,3,2,1,0:T(8,128)(2,1)}), bf16[8,2,4,16,512]{4,3,2,1,0:T(8,128)(2,1)S(1)}, u32[]{:S(2)}, u32[]{:S(2)}) async-start(bf16[8,2,4,16,512]{4,3,2,1,0:T(8,128)(2,1)} %time_scan.5), calls=%async_computation.3 | async-start | bytes 2097152 | tf_op jit(solution)/shard_map/all_to_all | solution.py:548
  97.7 4.7 %space_local_end.4 = (f32[4,240,512]{2,1,0:T(8,128)}, bf16[4,64,512]{2,1,0:T(8,128)(2,1)}) custom-call(bf16[8,2,4,16,512]{4,3,2,1,0:T(8,128)(2,1)} %copy-done.11, f32[4,256,256]{2,1,0:T(8,128)} %get-tuple-element.50.score_ref, f32[4,256,128]{2,1,0:T(8,128)} %get-tuple-element.51.cum_ref, f32[4,32,256]{2,1,0:T(8,128)} %get-tuple-element.52.row_ref, ...), custom_call_target="tpu_custom_call" | custom-call | flops 536870912 | bytes 5242880 | tf_op jit(solution)/shard_map/space_local_end/pallas_call | solution.py:374
  102.4 1.0 fusion
  103.4 1.4 collective-permute-start.3
  104.9 0.7 collective-permute-start.5
  105.5 6.0 %all-to-all-done.3.x_ref = bf16[8,2,4,16,512]{4,3,2,1,0:T(8,128)(2,1)S(1)} async-done(((bf16[8,2,4,16,512]{4,3,2,1,0:T(8,128)(2,1)}), bf16[8,2,4,16,512]{4,3,2,1,0:T(8,128)(2,1)S(1)}, u32[]{:S(2)}, u32[]{:S(2)}) %all-to-all-start.3) | async-done | bytes 1048608 | tf_op jit(solution)/shard_map/all_to_all | solution.py:548
  111.6 1.0 copy-done.10
  112.6 4.6 %space_local_end.5 = (f32[4,240,512]{2,1,0:T(8,128)}, bf16[4,64,512]{2,1,0:T(8,128)(2,1)}) custom-call(bf16[8,2,4,16,512]{4,3,2,1,0:T(8,128)(2,1)} %copy-done.10, f32[4,256,256]{2,1,0:T(8,128)} %get-tuple-element.50.score_ref, f32[4,256,128]{2,1,0:T(8,128)} %get-tuple-element.51.cum_ref, f32[4,32,256]{2,1,0:T(8,128)} %get-tuple-element.52.row_ref, ...), custom_call_target="tpu_custom_call" | custom-call | flops 536870912 | bytes 5242880 | tf_op jit(solution)/shard_map/space_local_end/pallas_call | solution.py:374
  117.2 0.7 collective-permute-start
  117.9 1.7 %collective-permute-done.3.rest_2_ = bf16[4,64,1024]{2,1,0:T(8,128)(2,1)S(1)} collective-permute-done((bf16[4,64,1024]{2,1,0:T(8,128)(2,1)}, bf16[4,64,1024]{2,1,0:T(8,128)(2,1)S(1)}, u32[]{:S(2)}, u32[]{:S(2)}) %collective-permute-start.3) | collective-permute-done | bytes 524320 | tf_op jit(solution)/shard_map/ppermute | solution.py:486
  119.7 0.1 fusion.4
  119.8 0.0 copy-start.7
  119.8 1.6 %collective-permute-start.6 = (bf16[4,64,512]{2,1,0:T(8,128)(2,1)S(1)}, bf16[4,64,512]{2,1,0:T(8,128)(2,1)S(1)}, u32[]{:S(2)}, u32[]{:S(2)}) collective-permute-start(bf16[4,64,512]{2,1,0:T(8,128)(2,1)S(1)} %fusion.4), channel_id=1, source_target_pairs={{1,2},{5,6},{9,10},{13,14},{17,18},{21,22},{25,26},{29,30}} | collective-permute-start | bytes 786440 | tf_op jit(solution)/shard_map/ppermute | solution.py:486
  121.3 1.0 fusion.2
  122.4 1.3 collective-permute-start.1
  123.7 0.2 fusion.1
  123.9 1.3 collective-permute-start.4
  125.2 4.2 %collective-permute-done.6.rest_3_ = bf16[4,64,512]{2,1,0:T(8,128)(2,1)S(1)} collective-permute-done((bf16[4,64,512]{2,1,0:T(8,128)(2,1)S(1)}, bf16[4,64,512]{2,1,0:T(8,128)(2,1)S(1)}, u32[]{:S(2)}, u32[]{:S(2)}) %collective-permute-start.6) | collective-permute-done | bytes 262176 | tf_op jit(solution)/shard_map/ppermute | solution.py:486
  129.5 0.1 fusion.5
  129.5 1.3 collective-permute-start.7
  130.9 5.2 %collective-permute-done.1.rest_6_ = bf16[4,64,512]{2,1,0:T(8,128)(2,1)S(1)} collective-permute-done((bf16[4,64,512]{2,1,0:T(8,128)(2,1)S(1)}, bf16[4,64,512]{2,1,0:T(8,128)(2,1)S(1)}, u32[]{:S(2)}, u32[]{:S(2)}) %collective-permute-start.1) | collective-permute-done | bytes 262176 | tf_op jit(solution)/shard_map/ppermute | solution.py:486
  136.0 1.0 fusion.3
  137.1 1.3 collective-permute-start.8
  138.4 0.0 copy-start.1
  138.4 0.0 copy-start.4
  138.5 6.9 %early.1 = (f32[4,240,1024]{2,1,0:T(8,128)S(1)}, f32[4,240,128]{2,1,0:T(8,128)S(1)}) custom-call(bf16[4,240,2048]{2,1,0:T(8,128)(2,1)S(1)} %bitcast.24, bf16[4,256,256]{2,1,0:T(8,128)(2,1)S(1)} %copy-done.3, bf16[4,256,64]{2,1,0:T(8,128)(2,1)S(1)} %copy-done.6, f32[1,2048]{1,0:T(1,128)S(1)} %bitcast.30, bf16[2048,1024]{1,0:T(8,128)(2,1)} %w_ref.3, ...), custom_call_target="tpu_custom_call" | custom-call | flops 2013265920 | bytes 13893632 | tf_op jit(solution)/shard_map/early/pallas_call | solution.py:472
  145.4 1.9 %copy-done.2 = f32[4,240,1024]{2,1,0:T(8,128)} copy-done((f32[4,240,1024]{2,1,0:T(8,128)}, f32[4,240,1024]{2,1,0:T(8,128)S(1)}, u32[]{:S(2)}) %copy-start.2) | copy-done | bytes 3932184
  147.2 0.2 collective-permute-done.8.rest_7_
  147.4 7.9 %last.1 = bf16[4,240,1024]{2,1,0:T(8,128)(2,1)} custom-call(bf16[4,240,2048]{2,1,0:T(8,128)(2,1)S(1)} %bitcast.25, bf16[4,256,256]{2,1,0:T(8,128)(2,1)S(1)} %copy-done.3, bf16[4,256,64]{2,1,0:T(8,128)(2,1)S(1)} %copy-done.6, f32[1,2048]{1,0:T(1,128)S(1)} %bitcast.31, bf16[2048,1024]{1,0:T(8,128)(2,1)} %w_ref.3, f32[4,240,1024]{2,1,0:T(8,128)} %copy-done.2, ...), custom_call_target="tpu_custom_call" | custom-call | flops 2013265920 | bytes 13893632 | tf_op jit(solution)/shard_map/last/pallas_call | solution.py:472
  (50 shorter events, 0.1 us)
Async XLA Ops:
  2.7 4.4 %copy-start.20 = (f32[32]{0:T(128)S(1)}, f32[32]{0:T(128)}, u32[]{:S(2)}) copy-start(f32[32]{0:T(128)} %param.14) | copy-start | bytes 388
  2.7 4.4 %copy-start.21 = (f32[32]{0:T(128)S(1)}, f32[32]{0:T(128)}, u32[]{:S(2)}) copy-start(f32[32]{0:T(128)} %param.13) | copy-start | bytes 388
  2.7 4.5 %copy-start.16 = (f32[32]{0:T(128)S(1)}, f32[32]{0:T(128)}, u32[]{:S(2)}) copy-start(f32[32]{0:T(128)} %param.18) | copy-start | bytes 388
  2.7 4.5 %copy-start.17 = (f32[32]{0:T(128)S(1)}, f32[32]{0:T(128)}, u32[]{:S(2)}) copy-start(f32[32]{0:T(128)} %param.17) | copy-start | bytes 388
  2.7 4.5 %copy-start.18 = (f32[32]{0:T(128)S(1)}, f32[32]{0:T(128)}, u32[]{:S(2)}) copy-start(f32[32]{0:T(128)} %param.16) | copy-start | bytes 388
  2.7 4.5 %copy-start.19 = (f32[32]{0:T(128)S(1)}, f32[32]{0:T(128)}, u32[]{:S(2)}) copy-start(f32[32]{0:T(128)} %param.15) | copy-start | bytes 388
  2.7 29.5 %all-to-all-start = ((bf16[8,2,4,16,1024]{4,3,2,1,0:T(8,128)(2,1)}), bf16[8,2,4,16,1024]{4,3,2,1,0:T(8,128)(2,1)S(1)}, u32[]{:S(2)}, u32[]{:S(2)}) async-start(bf16[8,2,4,16,1024]{4,3,2,1,0:T(8,128)(2,1)} %arrange.1), calls=%async_computation | async-start | bytes 4194304 | tf_op jit(solution)/shard_map/all_to_all | solution.py:508
  32.2 1.4 copy-start.8
  43.6 30.2 %all-to-all-start.1 = ((bf16[8,2,4,16,1024]{4,3,2,1,0:T(8,128)(2,1)}), bf16[8,2,4,16,1024]{4,3,2,1,0:T(8,128)(2,1)S(1)}, u32[]{:S(2)}, u32[]{:S(2)}) async-start(bf16[8,2,4,16,1024]{4,3,2,1,0:T(8,128)(2,1)} %get-tuple-element.43), calls=%async_computation.1 | async-start | bytes 4194304 | tf_op jit(solution)/shard_map/all_to_all | solution.py:548
  73.8 5.0 %copy-start.9 = (bf16[8,2,4,16,1024]{4,3,2,1,0:T(8,128)(2,1)}, bf16[8,2,4,16,1024]{4,3,2,1,0:T(8,128)(2,1)S(1)}, u32[]{:S(2)}) copy-start(bf16[8,2,4,16,1024]{4,3,2,1,0:T(8,128)(2,1)S(1)} %all-to-all-done.1.x_ref) | copy-start | bytes 6291460
  73.8 18.9 %all-to-all-start.2 = ((bf16[8,2,4,16,512]{4,3,2,1,0:T(8,128)(2,1)}), bf16[8,2,4,16,512]{4,3,2,1,0:T(8,128)(2,1)S(1)}, u32[]{:S(2)}, u32[]{:S(2)}) async-start(bf16[8,2,4,16,512]{4,3,2,1,0:T(8,128)(2,1)} %time_scan.4), calls=%async_computation.2 | async-start | bytes 2097152 | tf_op jit(solution)/shard_map/all_to_all | solution.py:548
  85.6 12.1 %copy-start.15 = (f32[4,1,2048]{2,1,0:T(1,128)S(1)}, f32[4,1,2048]{2,1,0:T(1,128)}, u32[]{:S(2)}) copy-start(f32[4,1,2048]{2,1,0:T(1,128)} %get-tuple-element.61) | copy-start | bytes 98308
  85.6 16.8 %collective-permute-start.2 = (bf16[4,64,1024]{2,1,0:T(8,128)(2,1)}, bf16[4,64,1024]{2,1,0:T(8,128)(2,1)S(1)}, u32[]{:S(2)}, u32[]{:S(2)}) collective-permute-start(bf16[4,64,1024]{2,1,0:T(8,128)(2,1)} %get-tuple-element.55), channel_id=1, source_target_pairs={{0,1},{4,5},{8,9},{12,13},{16,17},{20,21},{24,25},{28,29}} | collective-permute-start | bytes 1572872 | tf_op jit(solution)/shard_map/ppermute | solution.py:486
  92.7 5.0 %copy-start.11 = (bf16[8,2,4,16,512]{4,3,2,1,0:T(8,128)(2,1)}, bf16[8,2,4,16,512]{4,3,2,1,0:T(8,128)(2,1)S(1)}, u32[]{:S(2)}) copy-start(bf16[8,2,4,16,512]{4,3,2,1,0:T(8,128)(2,1)S(1)} %all-to-all-done.2.x_ref) | copy-start | bytes 3145732
  92.7 18.9 %all-to-all-start.3 = ((bf16[8,2,4,16,512]{4,3,2,1,0:T(8,128)(2,1)}), bf16[8,2,4,16,512]{4,3,2,1,0:T(8,128)(2,1)S(1)}, u32[]{:S(2)}, u32[]{:S(2)}) async-start(bf16[8,2,4,16,512]{4,3,2,1,0:T(8,128)(2,1)} %time_scan.5), calls=%async_computation.3 | async-start | bytes 2097152 | tf_op jit(solution)/shard_map/all_to_all | solution.py:548
  97.7 4.7 %copy-start.12 = (bf16[4,64,1024]{2,1,0:T(8,128)(2,1)S(1)}, bf16[4,64,1024]{2,1,0:T(8,128)(2,1)}, u32[]{:S(2)}) copy-start(bf16[4,64,1024]{2,1,0:T(8,128)(2,1)} %get-tuple-element.55) | copy-start | bytes 1572868
  103.4 16.2 %copy-start.14 = (bf16[4,64,512]{2,1,0:T(8,128)(2,1)S(1)}, bf16[4,64,512]{2,1,0:T(8,128)(2,1)}, u32[]{:S(2)}) copy-start(bf16[4,64,512]{2,1,0:T(8,128)(2,1)} %get-tuple-element.58) | copy-start | bytes 786436
  103.4 20.2 %copy-start.13 = (bf16[4,64,1024]{2,1,0:T(8,128)(2,1)S(1)}, bf16[4,64,1024]{2,1,0:T(8,128)(2,1)}, u32[]{:S(2)}) copy-start(bf16[4,64,1024]{2,1,0:T(8,128)(2,1)} %get-tuple-element.55) | copy-start | bytes 1572868
  103.4 16.2 %collective-permute-start.3 = (bf16[4,64,1024]{2,1,0:T(8,128)(2,1)}, bf16[4,64,1024]{2,1,0:T(8,128)(2,1)S(1)}, u32[]{:S(2)}, u32[]{:S(2)}) collective-permute-start(bf16[4,64,1024]{2,1,0:T(8,128)(2,1)} %fusion), channel_id=1, source_target_pairs={{1,2},{5,6},{9,10},{13,14},{17,18},{21,22},{25,26},{29,30}} | collective-permute-start | bytes 1572872 | tf_op jit(solution)/shard_map/ppermute | solution.py:486
  104.9 14.8 %collective-permute-start.5 = (bf16[4,64,512]{2,1,0:T(8,128)(2,1)}, bf16[4,64,512]{2,1,0:T(8,128)(2,1)S(1)}, u32[]{:S(2)}, u32[]{:S(2)}) collective-permute-start(bf16[4,64,512]{2,1,0:T(8,128)(2,1)} %get-tuple-element.58), channel_id=1, source_target_pairs={{0,1},{4,5},{8,9},{12,13},{16,17},{20,21},{24,25},{28,29}} | collective-permute-start | bytes 786440 | tf_op jit(solution)/shard_map/ppermute | solution.py:486
  111.6 1.0 copy-start.10
  117.2 4.2 %collective-permute-start = (bf16[4,64,512]{2,1,0:T(8,128)(2,1)}, bf16[4,64,512]{2,1,0:T(8,128)(2,1)S(1)}, u32[]{:S(2)}, u32[]{:S(2)}) collective-permute-start(bf16[4,64,512]{2,1,0:T(8,128)(2,1)} %get-tuple-element.60), channel_id=1, source_target_pairs={{0,1},{4,5},{8,9},{12,13},{16,17},{20,21},{24,25},{28,29}} | collective-permute-start | bytes 786440 | tf_op jit(solution)/shard_map/ppermute | solution.py:486
  119.6 18.7 %copy-start.3 = (bf16[4,256,256]{2,1,0:T(8,128)(2,1)S(1)}, bf16[4,256,256]{2,1,0:T(8,128)(2,1)}, u32[]{:S(2)}) copy-start(bf16[4,256,256]{2,1,0:T(8,128)(2,1)} %get-tuple-element.40.ecum_ref) | copy-start | bytes 1572868
  119.6 18.8 %copy-start.6 = (bf16[4,256,64]{2,1,0:T(8,128)(2,1)S(1)}, bf16[4,256,64]{2,1,0:T(8,128)(2,1)}, u32[]{:S(2)}) copy-start(bf16[4,256,64]{2,1,0:T(8,128)(2,1)} %get-tuple-element.41.c_ref) | copy-start | bytes 393220
  119.7 18.7 %copy-start = (bf16[960,2048]{1,0:T(8,128)(2,1)S(1)}, bf16[960,2048]{1,0:T(8,128)(2,1)}, u32[]{:S(2)}) copy-start(bf16[960,2048]{1,0:T(8,128)(2,1)} %gate_proj.1) | copy-start | bytes 11796484
  119.8 18.7 %copy-start.7 = (f32[2048]{0:T(1024)S(1)}, f32[2048]{0:T(1024)}, u32[]{:S(2)}) copy-start(f32[2048]{0:T(1024)} %param.19) | copy-start | bytes 24580
  119.8 9.7 %collective-permute-start.6 = (bf16[4,64,512]{2,1,0:T(8,128)(2,1)S(1)}, bf16[4,64,512]{2,1,0:T(8,128)(2,1)S(1)}, u32[]{:S(2)}, u32[]{:S(2)}) collective-permute-start(bf16[4,64,512]{2,1,0:T(8,128)(2,1)S(1)} %fusion.4), channel_id=1, source_target_pairs={{1,2},{5,6},{9,10},{13,14},{17,18},{21,22},{25,26},{29,30}} | collective-permute-start | bytes 786440 | tf_op jit(solution)/shard_map/ppermute | solution.py:486
  122.4 13.6 %collective-permute-start.1 = (bf16[4,64,512]{2,1,0:T(8,128)(2,1)S(1)}, bf16[4,64,512]{2,1,0:T(8,128)(2,1)S(1)}, u32[]{:S(2)}, u32[]{:S(2)}) collective-permute-start(bf16[4,64,512]{2,1,0:T(8,128)(2,1)S(1)} %fusion.2), channel_id=1, source_target_pairs={{1,2},{5,6},{9,10},{13,14},{17,18},{21,22},{25,26},{29,30}} | collective-permute-start | bytes 786440 | tf_op jit(solution)/shard_map/ppermute | solution.py:486
  123.9 14.5 %collective-permute-start.4 = (bf16[4,64,1024]{2,1,0:T(8,128)(2,1)S(1)}, bf16[4,64,1024]{2,1,0:T(8,128)(2,1)S(1)}, u32[]{:S(2)}, u32[]{:S(2)}) collective-permute-start(bf16[4,64,1024]{2,1,0:T(8,128)(2,1)S(1)} %fusion.1), channel_id=1, source_target_pairs={{2,3},{6,7},{10,11},{14,15},{18,19},{22,23},{26,27},{30,31}} | collective-permute-start | bytes 1572872 | tf_op jit(solution)/shard_map/ppermute | solution.py:486
  129.5 17.7 %collective-permute-start.7 = (bf16[4,64,512]{2,1,0:T(8,128)(2,1)S(1)}, bf16[4,64,512]{2,1,0:T(8,128)(2,1)S(1)}, u32[]{:S(2)}, u32[]{:S(2)}) collective-permute-start(bf16[4,64,512]{2,1,0:T(8,128)(2,1)S(1)} %fusion.5), channel_id=1, source_target_pairs={{2,3},{6,7},{10,11},{14,15},{18,19},{22,23},{26,27},{30,31}} | collective-permute-start | bytes 786440 | tf_op jit(solution)/shard_map/ppermute | solution.py:486
  137.1 10.4 %collective-permute-start.8 = (bf16[4,64,512]{2,1,0:T(8,128)(2,1)S(1)}, bf16[4,64,512]{2,1,0:T(8,128)(2,1)S(1)}, u32[]{:S(2)}, u32[]{:S(2)}) collective-permute-start(bf16[4,64,512]{2,1,0:T(8,128)(2,1)S(1)} %fusion.3), channel_id=1, source_target_pairs={{2,3},{6,7},{10,11},{14,15},{18,19},{22,23},{26,27},{30,31}} | collective-permute-start | bytes 786440 | tf_op jit(solution)/shard_map/ppermute | solution.py:486
  138.4 9.0 %copy-start.1 = (bf16[4,3,80,1024]{3,2,1,0:T(8,128)(2,1)S(1)}, bf16[4,3,80,1024]{3,2,1,0:T(8,128)(2,1)}, u32[]{:S(2)}) copy-start(bf16[4,3,80,1024]{3,2,1,0:T(8,128)(2,1)} %param.10) | copy-start | bytes 5898244
  138.4 9.0 %copy-start.4 = (f32[4,240,512]{2,1,0:T(8,128)S(1)}, f32[4,240,512]{2,1,0:T(8,128)}, u32[]{:S(2)}) copy-start(f32[4,240,512]{2,1,0:T(8,128)} %get-tuple-element.68.rest_0_) | copy-start | bytes 5898244
  138.4 9.0 %copy-start.5 = (f32[4,240,512]{2,1,0:T(8,128)S(1)}, f32[4,240,512]{2,1,0:T(8,128)}, u32[]{:S(2)}) copy-start(f32[4,240,512]{2,1,0:T(8,128)} %get-tuple-element.69.rest_1_) | copy-start | bytes 5898244
  145.3 1.9 %copy-start.2 = (f32[4,240,1024]{2,1,0:T(8,128)}, f32[4,240,1024]{2,1,0:T(8,128)S(1)}, u32[]{:S(2)}) copy-start(f32[4,240,1024]{2,1,0:T(8,128)S(1)} %get-tuple-element.66.acc_ref) | copy-start | bytes 11796484

commit v4 on v3

--- a/solution.py
+++ b/solution.py
@@ -79,14 +79,15 @@
     return pl.BlockSpec(shape, lambda *_: (0,) * len(shape))
 
 
-def arrange_kernel(n, spare, x_ref, o_ref):
-    for f in range(x_ref.shape[0]):
-        o_ref[:, 0, f] = x_ref[f].reshape(n, BLK, D)
-    if spare:
-
-        @pl.when(pl.program_id(0) == pl.num_programs(0) - 1)
+def arrange_kernel(n, spare, x_ref, *outs):
+    last = pl.program_id(0) == pl.num_programs(0) - 1
+    for k, o_ref in enumerate(outs):
+        to = jnp.bitwise_xor(lax.axis_index("tm"), k)
+        o_ref[0] = x_ref[:, pl.ds(pl.multiple_of(to * BLK, BLK), BLK), :]
+
+        @pl.when(last & (to >= n - spare))
         def _():
-            o_ref[n - spare :, 0] = jnp.zeros((spare,) + o_ref.shape[2:], BF)
+            o_ref[0] = jnp.zeros(o_ref.shape[1:], BF)
 
 
 def arrange(tok, n, m):
@@ -97,11 +98,18 @@
         "arrange",
         (m,),
         [pl.BlockSpec((fr, n * BLK, D), lambda h: (0, h, 0))],
-        pl.BlockSpec((n, 1, fr, BLK, D), lambda h: (0, h, 0, 0, 0)),
-        jax.ShapeDtypeStruct((n, m, fr, BLK, D), BF),
+        [pl.BlockSpec((1, fr, BLK, D), lambda h: (h, 0, 0, 0))] * n,
+        [jax.ShapeDtypeStruct((m, fr, BLK, D), BF)] * n,
         0,
         4 * fr * npos * D,
     )(tok)
+
+
+def exchange(pieces):
+    n = len(pieces)
+    order = [k for k in range(n - 1, 1, -1)] + [1]
+    got = {k: lax.ppermute(pieces[k], "tm", [(i, i ^ k) for i in range(n)]) for k in order}
+    return [pieces[0]] + [got[k] for k in range(1, n)]
 
 
 def gate_kernel(x_ref, w_ref, o_ref):
@@ -263,7 +271,16 @@
     return jnp.concatenate(ys, axis=1)
 
 
-def time_scan_kernel(n, m, fr, head0, first, x_ref, w_ref, *rest):
+def time_scan_kernel(n, m, fr, head0, first, *refs):
+    pieces, w_ref, rest, x_ref = refs[:n], refs[n], refs[n + 1 : -1], refs[-1]
+
+    @pl.when(pl.program_id(0) == 0)
+    def _():
+        per = m * fr * BLK
+        for k, ref in enumerate(pieces):
+            source = jnp.bitwise_xor(lax.axis_index("tm"), k)
+            x_ref[pl.ds(pl.multiple_of(source * per, per), per), :] = ref[...]
+
     if first:
         small, (par_ref, o_ref, score_ref, cum_ref, row_ref) = rest[:2], rest[2:]
 
@@ -292,8 +309,10 @@
 
 
 def time_scan(tok_t, w_t, prep, params, head0, heads):
-    n, m, fr = tok_t.shape[:3]
-    rows = n * m * fr * BLK
+    n = len(tok_t)
+    m, fr = tok_t[0].shape[:2]
+    per = m * fr * BLK
+    rows = n * per
     q_rows = n * fr * 8
     cols = heads * HEAD_DIM
     block = TIME_STEP * HEAD_DIM
@@ -302,7 +321,7 @@
     prep_specs = [full(s) for s in shapes]
     out_specs = [pl.BlockSpec((n, m, fr, BLK, block), lambda j: (0, 0, 0, 0, j))]
     out_shapes = [jax.ShapeDtypeStruct((n, m, fr, BLK, cols), BF)]
-    in_specs = [full((rows, D)), pl.BlockSpec((block, D), lambda j: (lo + j, 0))]
+    in_specs = [full((per, D))] * n + [pl.BlockSpec((block, D), lambda j: (lo + j, 0))]
     if prep is None:
         in_specs += small_specs(0) + [full(params.shape)]
         args = (w_t, w_t, params)
@@ -320,7 +339,8 @@
         out_shapes,
         2 * rows * D * cols + 4 * rows * q_rows * cols,
         2 * (rows * D + D * cols + rows * cols) + 2 * 1024 * 1024,
-    )(tok_t.reshape(rows, D), w_t, *args)
+        scratch=[pltpu.VMEM((rows, D), BF)],
+    )(*[piece.reshape(per, D) for piece in tok_t], w_t, *args)
 
 
 def frame_rows(ref, frame):
@@ -505,7 +525,7 @@
     tok = tokens.reshape(fr, npos, D)
     flat = tokens.reshape(fr * npos, D)
 
-    tok_t = lax.all_to_all(arrange(tok, n, m), "tm", split_axis=0, concat_axis=0, tiled=True)
+    tok_t = exchange(arrange(tok, n, m))
 
     w_t = w_in.T
     fill = jnp.zeros((LANES - 2 * HEADS,), F32)

time: 157 us -> 153 us (0.975)
  waiting for transfers between devices: 46.8 us -> 40.7 us
    all_to_all x1 -> x0, waiting for transfers between devices: 9.62 us -> none  [body(): lax.all_to_all(arrange(tok, n, m), 'tm', split_axis=0, concat_axis=0, til...]
    ppermute x0 -> x7, starting transfers between devices: none -> 6.38 us  [exchange(): lax.ppermute(pieces[k], 'tm', [(i, i ^ k) for i in range(n)])]
    all_to_all x1 -> x0, starting transfers between devices: 4.4 us -> none  [body(): lax.all_to_all(arrange(tok, n, m), 'tm', split_axis=0, concat_axis=0, til...]
    ppermute x0 -> x7, waiting for transfers between devices: none -> 3.88 us  [exchange(): lax.ppermute(pieces[k], 'tm', [(i, i ^ k) for i in range(n)])]
    unnamed x47 -> x51, local copies, waits for them, and re-layouts: 4.34 us -> 3.66 us
  transfers between devices with their start and end apart: 13 -> 19, of which waited for: 8 -> 8; matrix products, arithmetic and copies ran while one was open for 3% -> 4% of each run, Pallas kernels for 32% -> 33%
where the time goes in v4:
time: 153 us; the launch traced here: 152 us
  Pallas kernels  70.4 us (46%)
  waiting for transfers between devices  40.7 us (27%)
  starting transfers between devices  30.8 us (20%)
  other arithmetic  4.99 us (3%)
  local copies, waits for them, and re-layouts  4.28 us (3%)
    all_to_all x3, waiting for transfers between devices, body(): lax.all_to_all(outs[i], 'tm', split_axis=0, concat_axis=0, tiled=True)  25.6 us
    pallas_call x3, Pallas kernels, time_scan(): call(functools.partial(time_scan_kernel, n, m, fr, head0, prep is None),...  22 us
    pallas_call x3, Pallas kernels, space_parts(): call(functools.partial(space_kernel, head0, npos, local), 'space' + '_loc...  16.2 us
    pallas_call x2, Pallas kernels, finish(): call(functools.partial(kernel, cuts), name, (fr,), in_specs + [pl.BlockSp...  14.8 us
    all_to_all x3, starting transfers between devices, body(): lax.all_to_all(outs[i], 'tm', split_axis=0, concat_axis=0, tiled=True)  14.2 us
    ppermute x9, waiting for transfers between devices, hop(): return lax.ppermute(state, 'space', [(k, k + 1)])  11.3 us
    ppermute x9, starting transfers between devices, hop(): return lax.ppermute(state, 'space', [(k, k + 1)])  10.2 us
    pallas_call x1, Pallas kernels, gate_proj(): call(gate_kernel, 'gate_proj', (2,), [full((rows, D)), pl.BlockSpec((DI /...  8.01 us
  transfers between devices with their start and end apart: 19, of which 8 were waited for; matrix products, arithmetic and copies ran while one was open for 4% of the time, Pallas kernels for 33%

profile of v4, /device:TPU:18, one launch (start us, length us, event | category | flops | bytes accessed | tf_op | source)
XLA Modules:
  0.0 151.6 jit_solution(15942659304698501148)
XLA Ops:
  0.0 2.6 %arrange.1 = (bf16[2,4,16,1024]{3,2,1,0:T(8,128)(2,1)}, bf16[2,4,16,1024]{3,2,1,0:T(8,128)(2,1)}, bf16[2,4,16,1024]{3,2,1,0:T(8,128)(2,1)}, bf16[2,4,16,1024]{3,...) custom-call(bf16[4,240,1024]{2,1,0:T(8,128)(2,1)} %bitcast.33), custom_call_target="tpu_custom_call" | custom-call | bytes 3932160 | tf_op jit(solution)/shard_map/arrange/pallas_call | solution.py:96
  2.6 0.6 collective-permute-start.1
  3.2 1.3 collective-permute-start.2
  4.5 1.5 %collective-permute-start.3 = (bf16[2,4,16,1024]{3,2,1,0:T(8,128)(2,1)}, bf16[2,4,16,1024]{3,2,1,0:T(8,128)(2,1)S(1)}, u32[]{:S(2)}, u32[]{:S(2)}) collective-permute-start(bf16[2,4,16,1024]{3,2,1,0:T(8,128)(2,1)} %get-tuple-element.57), channel_id=1, source_target_pairs={{0,16},{4,20},{8,24},{12,28},{16,0},{20,4},{24,8},{28,12},{1,17},{... | collective-permute-start | bytes 786440 | tf_op jit(solution)/shard_map/ppermute | solution.py:111
  6.0 0.2 collective-permute-start.4
  6.2 0.7 negate_multiply_fusion
  6.9 0.8 fusion.9
  7.7 0.6 stack.23.par_ref.refs_11_.refs_12_
  8.3 6.8 %space_prep.1 = (f32[4,256,256]{2,1,0:T(8,128)}, f32[4,256,128]{2,1,0:T(8,128)}, f32[4,32,256]{2,1,0:T(8,128)}, bf16[4,256,256]{2,1,0:T(8,128)(2,1)}, bf16[4,256...) custom-call(bf16[4,240,1024]{2,1,0:T(8,128)(2,1)} %bitcast.34, ...), custom_call_target="tpu_custom_call" | custom-call | flops 503316480 | bytes 6291456 | tf_op jit(solution)/shard_map/space_prep/pallas_call | solution.py:196
  15.1 1.6 %collective-permute-start.5 = (bf16[2,4,16,1024]{3,2,1,0:T(8,128)(2,1)S(1)}, bf16[2,4,16,1024]{3,2,1,0:T(8,128)(2,1)S(1)}, u32[]{:S(2)}, u32[]{:S(2)}) collective-permute-start(bf16[2,4,16,1024]{3,2,1,0:T(8,128)(2,1)S(1)} %copy-done.23), channel_id=1, source_target_pairs={{0,24},{4,28},{8,16},{12,20},{16,8},{20,12},{24,0},{28,4},{1,25},{... | collective-permute-start | bytes 786440 | tf_op jit(solution)/shard_map/ppermute | solution.py:111
  16.7 1.3 collective-permute-start.6
  17.9 8.0 %gate_proj.1 = bf16[960,2048]{1,0:T(8,128)(2,1)} custom-call(bf16[960,1024]{1,0:T(8,128)(2,1)} %bitcast.35, bf16[4416,1024]{1,0:T(8,128)(2,1)} %bitcast.41), custom_call_target="tpu_custom_call" | custom-call | flops 4026531840 | bytes 10092544 | tf_op jit(solution)/shard_map/gate_proj/pallas_call | solution.py:121
  26.0 3.9 %collective-permute-done.6 = bf16[2,4,16,1024]{3,2,1,0:T(8,128)(2,1)S(1)} collective-permute-done((bf16[2,4,16,1024]{3,2,1,0:T(8,128)(2,1)S(1)}, bf16[2,4,16,1024]{3,2,1,0:T(8,128)(2,1)S(1)}, u32[]{:S(2)}, u32[]{:S(2)}) %collective-permute-start.6) | collective-permute-done | bytes 262176 | tf_op jit(solution)/shard_map/ppermute | solution.py:111
  29.9 0.7 copy-done.17
  30.6 10.1 %time_scan.3 = (bf16[8,2,4,16,1024]{4,3,2,1,0:T(8,128)(2,1)}, f32[4,256,256]{2,1,0:T(8,128)}, f32[4,256,128]{2,1,0:T(8,128)}, f32[4,32,256]{2,1,0:T(8,128)}) custom-call(bf16[128,1024]{1,0:T(8,128)(2,1)} %bitcast.47, bf16[128,1024]{1,0:T(8,128)(2,1)} %bitcast.50, bf16[128,1024]{1,0:T(8,128)(2,1)} %bitcast.53, bf16[128,1024]{1,0:T(8,128)(2,1)} %bitcast.56, ...), custom_call_target="tpu_custom_call" | custom-call | flops 3221225472 | bytes 8388608 | tf_op jit(solution)/shard_map/time_scan/pallas_call | solution.py:333
  40.7 4.3 %all-to-all-start = ((bf16[8,2,4,16,1024]{4,3,2,1,0:T(8,128)(2,1)}), bf16[8,2,4,16,1024]{4,3,2,1,0:T(8,128)(2,1)S(1)}, u32[]{:S(2)}, u32[]{:S(2)}) async-start(bf16[8,2,4,16,1024]{4,3,2,1,0:T(8,128)(2,1)} %get-tuple-element.73), calls=%async_computation | async-start | bytes 4194304 | tf_op jit(solution)/shard_map/all_to_all | solution.py:568
  45.0 6.0 %time_scan.4 = bf16[8,2,4,16,512]{4,3,2,1,0:T(8,128)(2,1)} custom-call(bf16[128,1024]{1,0:T(8,128)(2,1)} %bitcast.48, bf16[128,1024]{1,0:T(8,128)(2,1)} %bitcast.51, bf16[128,1024]{1,0:T(8,128)(2,1)} %bitcast.54, bf16[128,1024]{1,0:T(8,128)(2,1)} %bitcast.57, bf16[128,1024]{1,0:T(8,128)(2,1)} %bitcast.60, bf16[128,1024]{1,0:T(8,128)(2,1)} %bitcast.63, ...), custom_call_target="tpu_custom_call" | custom-call | flops 1610612736 | bytes 6291456 | tf_op jit(solution)/shard_map/time_scan/pallas_call | solution.py:333
  51.0 5.9 %time_scan.5 = bf16[8,2,4,16,512]{4,3,2,1,0:T(8,128)(2,1)} custom-call(bf16[128,1024]{1,0:T(8,128)(2,1)} %bitcast.49, bf16[128,1024]{1,0:T(8,128)(2,1)} %bitcast.52, bf16[128,1024]{1,0:T(8,128)(2,1)} %bitcast.55, bf16[128,1024]{1,0:T(8,128)(2,1)} %bitcast.58, bf16[128,1024]{1,0:T(8,128)(2,1)} %bitcast.61, bf16[128,1024]{1,0:T(8,128)(2,1)} %bitcast.64, ...), custom_call_target="tpu_custom_call" | custom-call | flops 1610612736 | bytes 6291456 | tf_op jit(solution)/shard_map/time_scan/pallas_call | solution.py:333
  56.9 13.2 %all-to-all-done.x_ref = bf16[8,2,4,16,1024]{4,3,2,1,0:T(8,128)(2,1)S(1)} async-done(((bf16[8,2,4,16,1024]{4,3,2,1,0:T(8,128)(2,1)}), bf16[8,2,4,16,1024]{4,3,2,1,0:T(8,128)(2,1)S(1)}, u32[]{:S(2)}, u32[]{:S(2)}) %all-to-all-start) | async-done | bytes 2097184 | tf_op jit(solution)/shard_map/all_to_all | solution.py:568
  70.1 5.0 %all-to-all-start.1 = ((bf16[8,2,4,16,512]{4,3,2,1,0:T(8,128)(2,1)}), bf16[8,2,4,16,512]{4,3,2,1,0:T(8,128)(2,1)S(1)}, u32[]{:S(2)}, u32[]{:S(2)}) async-start(bf16[8,2,4,16,512]{4,3,2,1,0:T(8,128)(2,1)} %time_scan.4), calls=%async_computation.1 | async-start | bytes 2097152 | tf_op jit(solution)/shard_map/all_to_all | solution.py:568
  75.1 6.9 %space_local_end.3 = (f32[4,240,1024]{2,1,0:T(8,128)}, bf16[4,64,1024]{2,1,0:T(8,128)(2,1)}) custom-call(bf16[8,2,4,16,1024]{4,3,2,1,0:T(8,128)(2,1)} %copy-done.8, f32[4,256,256]{2,1,0:T(8,128)} %get-tuple-element.80.score_ref, f32[4,256,128]{2,1,0:T(8,128)} %get-tuple-element.81.cum_ref, f32[4,32,256]{2,1,0:T(8,128)} %get-tuple-element.82.row_ref, ...), custom_call_target="tpu_custom_call" | custom-call | flops 1073741824 | bytes 8388608 | tf_op jit(solution)/shard_map/space_local_end/pallas_call | solution.py:394
  82.0 0.7 collective-permute-start.9
  82.7 6.3 %all-to-all-done.1.x_ref = bf16[8,2,4,16,512]{4,3,2,1,0:T(8,128)(2,1)S(1)} async-done(((bf16[8,2,4,16,512]{4,3,2,1,0:T(8,128)(2,1)}), bf16[8,2,4,16,512]{4,3,2,1,0:T(8,128)(2,1)S(1)}, u32[]{:S(2)}, u32[]{:S(2)}) %all-to-all-start.1) | async-done | bytes 1048608 | tf_op jit(solution)/shard_map/all_to_all | solution.py:568
  89.0 5.0 %all-to-all-start.2 = ((bf16[8,2,4,16,512]{4,3,2,1,0:T(8,128)(2,1)}), bf16[8,2,4,16,512]{4,3,2,1,0:T(8,128)(2,1)S(1)}, u32[]{:S(2)}, u32[]{:S(2)}) async-start(bf16[8,2,4,16,512]{4,3,2,1,0:T(8,128)(2,1)} %time_scan.5), calls=%async_computation.2 | async-start | bytes 2097152 | tf_op jit(solution)/shard_map/all_to_all | solution.py:568
  94.0 4.7 %space_local_end.4 = (f32[4,240,512]{2,1,0:T(8,128)}, bf16[4,64,512]{2,1,0:T(8,128)(2,1)}) custom-call(bf16[8,2,4,16,512]{4,3,2,1,0:T(8,128)(2,1)} %copy-done.10, f32[4,256,256]{2,1,0:T(8,128)} %get-tuple-element.80.score_ref, f32[4,256,128]{2,1,0:T(8,128)} %get-tuple-element.81.cum_ref, f32[4,32,256]{2,1,0:T(8,128)} %get-tuple-element.82.row_ref, ...), custom_call_target="tpu_custom_call" | custom-call | flops 536870912 | bytes 5242880 | tf_op jit(solution)/shard_map/space_local_end/pallas_call | solution.py:394
  98.8 1.1 fusion
  99.8 1.4 collective-permute-start.10
  101.2 0.7 collective-permute-start.12
  101.9 6.0 %all-to-all-done.2.x_ref = bf16[8,2,4,16,512]{4,3,2,1,0:T(8,128)(2,1)S(1)} async-done(((bf16[8,2,4,16,512]{4,3,2,1,0:T(8,128)(2,1)}), bf16[8,2,4,16,512]{4,3,2,1,0:T(8,128)(2,1)S(1)}, u32[]{:S(2)}, u32[]{:S(2)}) %all-to-all-start.2) | async-done | bytes 1048608 | tf_op jit(solution)/shard_map/all_to_all | solution.py:568
  107.9 1.0 copy-done.9
  108.9 4.6 %space_local_end.5 = (f32[4,240,512]{2,1,0:T(8,128)}, bf16[4,64,512]{2,1,0:T(8,128)(2,1)}) custom-call(bf16[8,2,4,16,512]{4,3,2,1,0:T(8,128)(2,1)} %copy-done.9, f32[4,256,256]{2,1,0:T(8,128)} %get-tuple-element.80.score_ref, f32[4,256,128]{2,1,0:T(8,128)} %get-tuple-element.81.cum_ref, f32[4,32,256]{2,1,0:T(8,128)} %get-tuple-element.82.row_ref, ...), custom_call_target="tpu_custom_call" | custom-call | flops 536870912 | bytes 5242880 | tf_op jit(solution)/shard_map/space_local_end/pallas_call | solution.py:394
  113.5 0.7 collective-permute-start.7
  114.3 1.8 %collective-permute-done.10.rest_2_ = bf16[4,64,1024]{2,1,0:T(8,128)(2,1)S(1)} collective-permute-done((bf16[4,64,1024]{2,1,0:T(8,128)(2,1)}, bf16[4,64,1024]{2,1,0:T(8,128)(2,1)S(1)}, u32[]{:S(2)}, u32[]{:S(2)}) %collective-permute-start.10) | collective-permute-done | bytes 524320 | tf_op jit(solution)/shard_map/ppermute | solution.py:506
  116.2 1.6 %collective-permute-start.13 = (bf16[4,64,512]{2,1,0:T(8,128)(2,1)S(1)}, bf16[4,64,512]{2,1,0:T(8,128)(2,1)S(1)}, u32[]{:S(2)}, u32[]{:S(2)}) collective-permute-start(bf16[4,64,512]{2,1,0:T(8,128)(2,1)S(1)} %fusion.4), channel_id=1, source_target_pairs={{1,2},{5,6},{9,10},{13,14},{17,18},{21,22},{25,26},{29,30}} | collective-permute-start | bytes 786440 | tf_op jit(solution)/shard_map/ppermute | solution.py:506
  117.7 1.0 fusion.2
  118.8 1.3 collective-permute-start.8
  120.1 0.2 fusion.1
  120.3 1.3 collective-permute-start.11
  121.6 4.2 %collective-permute-done.13.rest_3_ = bf16[4,64,512]{2,1,0:T(8,128)(2,1)S(1)} collective-permute-done((bf16[4,64,512]{2,1,0:T(8,128)(2,1)S(1)}, bf16[4,64,512]{2,1,0:T(8,128)(2,1)S(1)}, u32[]{:S(2)}, u32[]{:S(2)}) %collective-permute-start.13) | collective-permute-done | bytes 262176 | tf_op jit(solution)/shard_map/ppermute | solution.py:506
  125.8 0.1 fusion.5
  125.9 1.3 collective-permute-start.14
  127.3 5.1 %collective-permute-done.8.rest_6_ = bf16[4,64,512]{2,1,0:T(8,128)(2,1)S(1)} collective-permute-done((bf16[4,64,512]{2,1,0:T(8,128)(2,1)S(1)}, bf16[4,64,512]{2,1,0:T(8,128)(2,1)S(1)}, u32[]{:S(2)}, u32[]{:S(2)}) %collective-permute-start.8) | collective-permute-done | bytes 262176 | tf_op jit(solution)/shard_map/ppermute | solution.py:506
  132.4 1.0 fusion.3
  133.4 1.3 collective-permute-start.15
  134.8 6.9 %early.1 = (f32[4,240,1024]{2,1,0:T(8,128)S(1)}, f32[4,240,128]{2,1,0:T(8,128)S(1)}) custom-call(bf16[4,240,2048]{2,1,0:T(8,128)(2,1)S(1)} %bitcast.31, bf16[4,256,256]{2,1,0:T(8,128)(2,1)S(1)} %copy-done.3, bf16[4,256,64]{2,1,0:T(8,128)(2,1)S(1)} %copy-done.6, f32[1,2048]{1,0:T(1,128)S(1)} %bitcast.37, bf16[2048,1024]{1,0:T(8,128)(2,1)} %w_ref.3, ...), custom_call_target="tpu_custom_call" | custom-call | flops 2013265920 | bytes 13893632 | tf_op jit(solution)/shard_map/early/pallas_call | solution.py:492
  141.7 1.9 %copy-done.2 = f32[4,240,1024]{2,1,0:T(8,128)} copy-done((f32[4,240,1024]{2,1,0:T(8,128)}, f32[4,240,1024]{2,1,0:T(8,128)S(1)}, u32[]{:S(2)}) %copy-start.2) | copy-done | bytes 3932184
  143.6 0.2 collective-permute-done.15.rest_7_
  143.8 7.8 %last.1 = bf16[4,240,1024]{2,1,0:T(8,128)(2,1)} custom-call(bf16[4,240,2048]{2,1,0:T(8,128)(2,1)S(1)} %bitcast.32, bf16[4,256,256]{2,1,0:T(8,128)(2,1)S(1)} %copy-done.3, bf16[4,256,64]{2,1,0:T(8,128)(2,1)S(1)} %copy-done.6, f32[1,2048]{1,0:T(1,128)S(1)} %bitcast.38, bf16[2048,1024]{1,0:T(8,128)(2,1)} %w_ref.3, f32[4,240,1024]{2,1,0:T(8,128)} %copy-done.2, ...), custom_call_target="tpu_custom_call" | custom-call | flops 2013265920 | bytes 13893632 | tf_op jit(solution)/shard_map/last/pallas_call | solution.py:492
  (66 shorter events, 0.2 us)
Async XLA Ops:
  2.6 12.5 %collective-permute-start = (bf16[2,4,16,1024]{3,2,1,0:T(8,128)(2,1)}, bf16[2,4,16,1024]{3,2,1,0:T(8,128)(2,1)S(1)}, u32[]{:S(2)}, u32[]{:S(2)}) collective-permute-start(bf16[2,4,16,1024]{3,2,1,0:T(8,128)(2,1)} %get-tuple-element.54), channel_id=1, source_target_pairs={{0,4},{4,0},{8,12},{12,8},{16,20},{20,16},{24,28},{28,24},{1,5},{5... | collective-permute-start | bytes 786440 | tf_op jit(solution)/shard_map/ppermute | solution.py:111
  2.6 14.0 %collective-permute-start.1 = (bf16[2,4,16,1024]{3,2,1,0:T(8,128)(2,1)}, bf16[2,4,16,1024]{3,2,1,0:T(8,128)(2,1)S(1)}, u32[]{:S(2)}, u32[]{:S(2)}) collective-permute-start(bf16[2,4,16,1024]{3,2,1,0:T(8,128)(2,1)} %get-tuple-element.55), channel_id=1, source_target_pairs={{0,8},{4,12},{8,0},{12,4},{16,24},{20,28},{24,16},{28,20},{1,9},{5... | collective-permute-start | bytes 786440 | tf_op jit(solution)/shard_map/ppermute | solution.py:111
  3.2 22.7 %collective-permute-start.2 = (bf16[2,4,16,1024]{3,2,1,0:T(8,128)(2,1)}, bf16[2,4,16,1024]{3,2,1,0:T(8,128)(2,1)S(1)}, u32[]{:S(2)}, u32[]{:S(2)}) collective-permute-start(bf16[2,4,16,1024]{3,2,1,0:T(8,128)(2,1)} %get-tuple-element.56), channel_id=1, source_target_pairs={{0,12},{4,8},{8,4},{12,0},{16,28},{20,24},{24,20},{28,16},{1,13},{... | collective-permute-start | bytes 786440 | tf_op jit(solution)/shard_map/ppermute | solution.py:111
  4.5 21.5 %collective-permute-start.3 = (bf16[2,4,16,1024]{3,2,1,0:T(8,128)(2,1)}, bf16[2,4,16,1024]{3,2,1,0:T(8,128)(2,1)S(1)}, u32[]{:S(2)}, u32[]{:S(2)}) collective-permute-start(bf16[2,4,16,1024]{3,2,1,0:T(8,128)(2,1)} %get-tuple-element.57), channel_id=1, source_target_pairs={{0,16},{4,20},{8,24},{12,28},{16,0},{20,4},{24,8},{28,12},{1,17},{... | collective-permute-start | bytes 786440 | tf_op jit(solution)/shard_map/ppermute | solution.py:111
  6.0 20.0 %collective-permute-start.4 = (bf16[2,4,16,1024]{3,2,1,0:T(8,128)(2,1)}, bf16[2,4,16,1024]{3,2,1,0:T(8,128)(2,1)S(1)}, u32[]{:S(2)}, u32[]{:S(2)}) collective-permute-start(bf16[2,4,16,1024]{3,2,1,0:T(8,128)(2,1)} %get-tuple-element.58), channel_id=1, source_target_pairs={{0,20},{4,16},{8,28},{12,24},{16,4},{20,0},{24,12},{28,8},{1,21},{... | collective-permute-start | bytes 786440 | tf_op jit(solution)/shard_map/ppermute | solution.py:111
  8.3 6.8 %copy-start.23 = (bf16[2,4,16,1024]{3,2,1,0:T(8,128)(2,1)S(1)}, bf16[2,4,16,1024]{3,2,1,0:T(8,128)(2,1)}, u32[]{:S(2)}) copy-start(bf16[2,4,16,1024]{3,2,1,0:T(8,128)(2,1)} %get-tuple-element.59) | copy-start | bytes 786436
  8.3 8.4 %copy-start.22 = (bf16[2,4,16,1024]{3,2,1,0:T(8,128)(2,1)S(1)}, bf16[2,4,16,1024]{3,2,1,0:T(8,128)(2,1)}, u32[]{:S(2)}) copy-start(bf16[2,4,16,1024]{3,2,1,0:T(8,128)(2,1)} %get-tuple-element.60) | copy-start | bytes 786436
  15.1 10.9 %copy-start.11 = (bf16[2,4,16,1024]{3,2,1,0:T(8,128)(2,1)}, bf16[2,4,16,1024]{3,2,1,0:T(8,128)(2,1)S(1)}, u32[]{:S(2)}) copy-start(bf16[2,4,16,1024]{3,2,1,0:T(8,128)(2,1)S(1)} %collective-permute-done) | copy-start | bytes 786436
  15.1 10.9 %collective-permute-start.5 = (bf16[2,4,16,1024]{3,2,1,0:T(8,128)(2,1)S(1)}, bf16[2,4,16,1024]{3,2,1,0:T(8,128)(2,1)S(1)}, u32[]{:S(2)}, u32[]{:S(2)}) collective-permute-start(bf16[2,4,16,1024]{3,2,1,0:T(8,128)(2,1)S(1)} %copy-done.23), channel_id=1, source_target_pairs={{0,24},{4,28},{8,16},{12,20},{16,8},{20,12},{24,0},{28,4},{1,25},{... | collective-permute-start | bytes 786440 | tf_op jit(solution)/shard_map/ppermute | solution.py:111
  16.7 9.3 %copy-start.12 = (bf16[2,4,16,1024]{3,2,1,0:T(8,128)(2,1)}, bf16[2,4,16,1024]{3,2,1,0:T(8,128)(2,1)S(1)}, u32[]{:S(2)}) copy-start(bf16[2,4,16,1024]{3,2,1,0:T(8,128)(2,1)S(1)} %collective-permute-done.1) | copy-start | bytes 786436
  16.7 13.2 %collective-permute-start.6 = (bf16[2,4,16,1024]{3,2,1,0:T(8,128)(2,1)S(1)}, bf16[2,4,16,1024]{3,2,1,0:T(8,128)(2,1)S(1)}, u32[]{:S(2)}, u32[]{:S(2)}) collective-permute-start(bf16[2,4,16,1024]{3,2,1,0:T(8,128)(2,1)S(1)} %copy-done.22), channel_id=1, source_target_pairs={{0,28},{4,24},{8,20},{12,16},{16,12},{20,8},{24,4},{28,0},{1,29},{... | collective-permute-start | bytes 786440 | tf_op jit(solution)/shard_map/ppermute | solution.py:111
  26.0 3.9 %copy-start.13 = (bf16[2,4,16,1024]{3,2,1,0:T(8,128)(2,1)}, bf16[2,4,16,1024]{3,2,1,0:T(8,128)(2,1)S(1)}, u32[]{:S(2)}) copy-start(bf16[2,4,16,1024]{3,2,1,0:T(8,128)(2,1)S(1)} %collective-permute-done.2) | copy-start | bytes 786436
  26.0 3.9 %copy-start.14 = (bf16[2,4,16,1024]{3,2,1,0:T(8,128)(2,1)}, bf16[2,4,16,1024]{3,2,1,0:T(8,128)(2,1)S(1)}, u32[]{:S(2)}) copy-start(bf16[2,4,16,1024]{3,2,1,0:T(8,128)(2,1)S(1)} %collective-permute-done.3) | copy-start | bytes 786436
  26.0 3.9 %copy-start.15 = (bf16[2,4,16,1024]{3,2,1,0:T(8,128)(2,1)}, bf16[2,4,16,1024]{3,2,1,0:T(8,128)(2,1)S(1)}, u32[]{:S(2)}) copy-start(bf16[2,4,16,1024]{3,2,1,0:T(8,128)(2,1)S(1)} %collective-permute-done.4) | copy-start | bytes 786436
  26.0 3.9 %copy-start.16 = (bf16[2,4,16,1024]{3,2,1,0:T(8,128)(2,1)}, bf16[2,4,16,1024]{3,2,1,0:T(8,128)(2,1)S(1)}, u32[]{:S(2)}) copy-start(bf16[2,4,16,1024]{3,2,1,0:T(8,128)(2,1)S(1)} %collective-permute-done.5) | copy-start | bytes 786436
  29.9 0.7 copy-start.17
  40.7 29.4 %all-to-all-start = ((bf16[8,2,4,16,1024]{4,3,2,1,0:T(8,128)(2,1)}), bf16[8,2,4,16,1024]{4,3,2,1,0:T(8,128)(2,1)S(1)}, u32[]{:S(2)}, u32[]{:S(2)}) async-start(bf16[8,2,4,16,1024]{4,3,2,1,0:T(8,128)(2,1)} %get-tuple-element.73), calls=%async_computation | async-start | bytes 4194304 | tf_op jit(solution)/shard_map/all_to_all | solution.py:568
  70.1 5.0 %copy-start.8 = (bf16[8,2,4,16,1024]{4,3,2,1,0:T(8,128)(2,1)}, bf16[8,2,4,16,1024]{4,3,2,1,0:T(8,128)(2,1)S(1)}, u32[]{:S(2)}) copy-start(bf16[8,2,4,16,1024]{4,3,2,1,0:T(8,128)(2,1)S(1)} %all-to-all-done.x_ref) | copy-start | bytes 6291460
  70.1 18.9 %all-to-all-start.1 = ((bf16[8,2,4,16,512]{4,3,2,1,0:T(8,128)(2,1)}), bf16[8,2,4,16,512]{4,3,2,1,0:T(8,128)(2,1)S(1)}, u32[]{:S(2)}, u32[]{:S(2)}) async-start(bf16[8,2,4,16,512]{4,3,2,1,0:T(8,128)(2,1)} %time_scan.4), calls=%async_computation.1 | async-start | bytes 2097152 | tf_op jit(solution)/shard_map/all_to_all | solution.py:568
  82.0 12.0 %copy-start.21 = (f32[4,1,2048]{2,1,0:T(1,128)S(1)}, f32[4,1,2048]{2,1,0:T(1,128)}, u32[]{:S(2)}) copy-start(f32[4,1,2048]{2,1,0:T(1,128)} %get-tuple-element.91) | copy-start | bytes 98308
  82.0 16.7 %collective-permute-start.9 = (bf16[4,64,1024]{2,1,0:T(8,128)(2,1)}, bf16[4,64,1024]{2,1,0:T(8,128)(2,1)S(1)}, u32[]{:S(2)}, u32[]{:S(2)}) collective-permute-start(bf16[4,64,1024]{2,1,0:T(8,128)(2,1)} %get-tuple-element.85), channel_id=1, source_target_pairs={{0,1},{4,5},{8,9},{12,13},{16,17},{20,21},{24,25},{28,29}} | collective-permute-start | bytes 1572872 | tf_op jit(solution)/shard_map/ppermute | solution.py:506
  89.0 5.0 %copy-start.10 = (bf16[8,2,4,16,512]{4,3,2,1,0:T(8,128)(2,1)}, bf16[8,2,4,16,512]{4,3,2,1,0:T(8,128)(2,1)S(1)}, u32[]{:S(2)}) copy-start(bf16[8,2,4,16,512]{4,3,2,1,0:T(8,128)(2,1)S(1)} %all-to-all-done.1.x_ref) | copy-start | bytes 3145732
  89.0 18.9 %all-to-all-start.2 = ((bf16[8,2,4,16,512]{4,3,2,1,0:T(8,128)(2,1)}), bf16[8,2,4,16,512]{4,3,2,1,0:T(8,128)(2,1)S(1)}, u32[]{:S(2)}, u32[]{:S(2)}) async-start(bf16[8,2,4,16,512]{4,3,2,1,0:T(8,128)(2,1)} %time_scan.5), calls=%async_computation.2 | async-start | bytes 2097152 | tf_op jit(solution)/shard_map/all_to_all | solution.py:568
  94.0 4.7 %copy-start.18 = (bf16[4,64,1024]{2,1,0:T(8,128)(2,1)S(1)}, bf16[4,64,1024]{2,1,0:T(8,128)(2,1)}, u32[]{:S(2)}) copy-start(bf16[4,64,1024]{2,1,0:T(8,128)(2,1)} %get-tuple-element.85) | copy-start | bytes 1572868
  99.8 16.2 %copy-start.20 = (bf16[4,64,512]{2,1,0:T(8,128)(2,1)S(1)}, bf16[4,64,512]{2,1,0:T(8,128)(2,1)}, u32[]{:S(2)}) copy-start(bf16[4,64,512]{2,1,0:T(8,128)(2,1)} %get-tuple-element.88) | copy-start | bytes 786436
  99.8 20.3 %copy-start.19 = (bf16[4,64,1024]{2,1,0:T(8,128)(2,1)S(1)}, bf16[4,64,1024]{2,1,0:T(8,128)(2,1)}, u32[]{:S(2)}) copy-start(bf16[4,64,1024]{2,1,0:T(8,128)(2,1)} %get-tuple-element.85) | copy-start | bytes 1572868
  99.8 16.2 %collective-permute-start.10 = (bf16[4,64,1024]{2,1,0:T(8,128)(2,1)}, bf16[4,64,1024]{2,1,0:T(8,128)(2,1)S(1)}, u32[]{:S(2)}, u32[]{:S(2)}) collective-permute-start(bf16[4,64,1024]{2,1,0:T(8,128)(2,1)} %fusion), channel_id=1, source_target_pairs={{1,2},{5,6},{9,10},{13,14},{17,18},{21,22},{25,26},{29,30}} | collective-permute-start | bytes 1572872 | tf_op jit(solution)/shard_map/ppermute | solution.py:506
  101.2 14.8 %collective-permute-start.12 = (bf16[4,64,512]{2,1,0:T(8,128)(2,1)}, bf16[4,64,512]{2,1,0:T(8,128)(2,1)S(1)}, u32[]{:S(2)}, u32[]{:S(2)}) collective-permute-start(bf16[4,64,512]{2,1,0:T(8,128)(2,1)} %get-tuple-element.88), channel_id=1, source_target_pairs={{0,1},{4,5},{8,9},{12,13},{16,17},{20,21},{24,25},{28,29}} | collective-permute-start | bytes 786440 | tf_op jit(solution)/shard_map/ppermute | solution.py:506
  107.9 1.0 copy-start.9
  113.5 4.2 %collective-permute-start.7 = (bf16[4,64,512]{2,1,0:T(8,128)(2,1)}, bf16[4,64,512]{2,1,0:T(8,128)(2,1)S(1)}, u32[]{:S(2)}, u32[]{:S(2)}) collective-permute-start(bf16[4,64,512]{2,1,0:T(8,128)(2,1)} %get-tuple-element.90), channel_id=1, source_target_pairs={{0,1},{4,5},{8,9},{12,13},{16,17},{20,21},{24,25},{28,29}} | collective-permute-start | bytes 786440 | tf_op jit(solution)/shard_map/ppermute | solution.py:506
  116.0 18.7 %copy-start.3 = (bf16[4,256,256]{2,1,0:T(8,128)(2,1)S(1)}, bf16[4,256,256]{2,1,0:T(8,128)(2,1)}, u32[]{:S(2)}) copy-start(bf16[4,256,256]{2,1,0:T(8,128)(2,1)} %get-tuple-element.63.ecum_ref) | copy-start | bytes 1572868
  116.0 18.7 %copy-start.6 = (bf16[4,256,64]{2,1,0:T(8,128)(2,1)S(1)}, bf16[4,256,64]{2,1,0:T(8,128)(2,1)}, u32[]{:S(2)}) copy-start(bf16[4,256,64]{2,1,0:T(8,128)(2,1)} %get-tuple-element.64.c_ref) | copy-start | bytes 393220
  116.1 18.6 %copy-start = (bf16[960,2048]{1,0:T(8,128)(2,1)S(1)}, bf16[960,2048]{1,0:T(8,128)(2,1)}, u32[]{:S(2)}) copy-start(bf16[960,2048]{1,0:T(8,128)(2,1)} %gate_proj.1) | copy-start | bytes 11796484
  116.1 18.6 %copy-start.7 = (f32[2048]{0:T(1024)S(1)}, f32[2048]{0:T(1024)}, u32[]{:S(2)}) copy-start(f32[2048]{0:T(1024)} %param.19) | copy-start | bytes 24580
  116.2 9.7 %collective-permute-start.13 = (bf16[4,64,512]{2,1,0:T(8,128)(2,1)S(1)}, bf16[4,64,512]{2,1,0:T(8,128)(2,1)S(1)}, u32[]{:S(2)}, u32[]{:S(2)}) collective-permute-start(bf16[4,64,512]{2,1,0:T(8,128)(2,1)S(1)} %fusion.4), channel_id=1, source_target_pairs={{1,2},{5,6},{9,10},{13,14},{17,18},{21,22},{25,26},{29,30}} | collective-permute-start | bytes 786440 | tf_op jit(solution)/shard_map/ppermute | solution.py:506
  118.8 13.6 %collective-permute-start.8 = (bf16[4,64,512]{2,1,0:T(8,128)(2,1)S(1)}, bf16[4,64,512]{2,1,0:T(8,128)(2,1)S(1)}, u32[]{:S(2)}, u32[]{:S(2)}) collective-permute-start(bf16[4,64,512]{2,1,0:T(8,128)(2,1)S(1)} %fusion.2), channel_id=1, source_target_pairs={{1,2},{5,6},{9,10},{13,14},{17,18},{21,22},{25,26},{29,30}} | collective-permute-start | bytes 786440 | tf_op jit(solution)/shard_map/ppermute | solution.py:506
  120.3 14.4 %collective-permute-start.11 = (bf16[4,64,1024]{2,1,0:T(8,128)(2,1)S(1)}, bf16[4,64,1024]{2,1,0:T(8,128)(2,1)S(1)}, u32[]{:S(2)}, u32[]{:S(2)}) collective-permute-start(bf16[4,64,1024]{2,1,0:T(8,128)(2,1)S(1)} %fusion.1), channel_id=1, source_target_pairs={{2,3},{6,7},{10,11},{14,15},{18,19},{22,23},{26,27},{30,31}} | collective-permute-start | bytes 1572872 | tf_op jit(solution)/shard_map/ppermute | solution.py:506
  125.9 17.7 %collective-permute-start.14 = (bf16[4,64,512]{2,1,0:T(8,128)(2,1)S(1)}, bf16[4,64,512]{2,1,0:T(8,128)(2,1)S(1)}, u32[]{:S(2)}, u32[]{:S(2)}) collective-permute-start(bf16[4,64,512]{2,1,0:T(8,128)(2,1)S(1)} %fusion.5), channel_id=1, source_target_pairs={{2,3},{6,7},{10,11},{14,15},{18,19},{22,23},{26,27},{30,31}} | collective-permute-start | bytes 786440 | tf_op jit(solution)/shard_map/ppermute | solution.py:506
  133.4 10.4 %collective-permute-start.15 = (bf16[4,64,512]{2,1,0:T(8,128)(2,1)S(1)}, bf16[4,64,512]{2,1,0:T(8,128)(2,1)S(1)}, u32[]{:S(2)}, u32[]{:S(2)}) collective-permute-start(bf16[4,64,512]{2,1,0:T(8,128)(2,1)S(1)} %fusion.3), channel_id=1, source_target_pairs={{2,3},{6,7},{10,11},{14,15},{18,19},{22,23},{26,27},{30,31}} | collective-permute-start | bytes 786440 | tf_op jit(solution)/shard_map/ppermute | solution.py:506
  134.8 9.0 %copy-start.1 = (bf16[4,3,80,1024]{3,2,1,0:T(8,128)(2,1)S(1)}, bf16[4,3,80,1024]{3,2,1,0:T(8,128)(2,1)}, u32[]{:S(2)}) copy-start(bf16[4,3,80,1024]{3,2,1,0:T(8,128)(2,1)} %param.10) | copy-start | bytes 5898244
  134.8 9.0 %copy-start.4 = (f32[4,240,512]{2,1,0:T(8,128)S(1)}, f32[4,240,512]{2,1,0:T(8,128)}, u32[]{:S(2)}) copy-start(f32[4,240,512]{2,1,0:T(8,128)} %get-tuple-element.98.rest_0_) | copy-start | bytes 5898244
  134.8 9.0 %copy-start.5 = (f32[4,240,512]{2,1,0:T(8,128)S(1)}, f32[4,240,512]{2,1,0:T(8,128)}, u32[]{:S(2)}) copy-start(f32[4,240,512]{2,1,0:T(8,128)} %get-tuple-element.99.rest_1_) | copy-start | bytes 5898244
  141.7 1.9 %copy-start.2 = (f32[4,240,1024]{2,1,0:T(8,128)}, f32[4,240,1024]{2,1,0:T(8,128)S(1)}, u32[]{:S(2)}) copy-start(f32[4,240,1024]{2,1,0:T(8,128)S(1)} %get-tuple-element.96.acc_ref) | copy-start | bytes 11796484

commit v5 on v4

--- a/solution.py
+++ b/solution.py
@@ -79,26 +79,29 @@
     return pl.BlockSpec(shape, lambda *_: (0,) * len(shape))
 
 
-def arrange_kernel(n, spare, x_ref, *outs):
-    last = pl.program_id(0) == pl.num_programs(0) - 1
+def arrange_kernel(n, x_ref, *outs):
+    rows = x_ref.shape[1]
     for k, o_ref in enumerate(outs):
         to = jnp.bitwise_xor(lax.axis_index("tm"), k)
-        o_ref[0] = x_ref[:, pl.ds(pl.multiple_of(to * BLK, BLK), BLK), :]
-
-        @pl.when(last & (to >= n - spare))
-        def _():
-            o_ref[0] = jnp.zeros(o_ref.shape[1:], BF)
+        for h in range(o_ref.shape[0]):
+            at = (h * n + to) * BLK
+            start = pl.multiple_of(jnp.minimum(at, rows - BLK), BLK)
+            o_ref[h] = x_ref[:, pl.ds(start, BLK), :]
+
+            @pl.when(at >= rows)
+            def _():
+                o_ref[h] = jnp.zeros(o_ref.shape[1:], BF)
 
 
 def arrange(tok, n, m):
     fr, npos, _ = tok.shape
-    spare = n * m - npos // BLK
+    step = 2 if fr % 2 == 0 else 1
     return call(
-        functools.partial(arrange_kernel, n, spare),
+        functools.partial(arrange_kernel, n),
         "arrange",
-        (m,),
-        [pl.BlockSpec((fr, n * BLK, D), lambda h: (0, h, 0))],
-        [pl.BlockSpec((1, fr, BLK, D), lambda h: (h, 0, 0, 0))] * n,
+        (fr // step,),
+        [pl.BlockSpec((step, npos, D), lambda f: (f, 0, 0))],
+        [pl.BlockSpec((m, step, BLK, D), lambda f: (0, f, 0, 0))] * n,
         [jax.ShapeDtypeStruct((m, fr, BLK, D), BF)] * n,
         0,
         4 * fr * npos * D,

time: 153 us -> 153 us (level)
  no operation moved by 1% of the time
where the time goes in v5:
time: 153 us; the launch traced here: 152 us
  Pallas kernels  70.4 us (46%)
  waiting for transfers between devices  40.7 us (27%)
  starting transfers between devices  30.8 us (20%)
  other arithmetic  4.99 us (3%)
  local copies, waits for them, and re-layouts  4.28 us (3%)
    all_to_all x3, waiting for transfers between devices, body(): lax.all_to_all(outs[i], 'tm', split_axis=0, concat_axis=0, tiled=True)  25.6 us
    pallas_call x3, Pallas kernels, time_scan(): call(functools.partial(time_scan_kernel, n, m, fr, head0, prep is None),...  22 us
    pallas_call x3, Pallas kernels, space_parts(): call(functools.partial(space_kernel, head0, npos, local), 'space' + '_loc...  16.2 us
    pallas_call x2, Pallas kernels, finish(): call(functools.partial(kernel, cuts), name, (fr,), in_specs + [pl.BlockSp...  14.7 us
    all_to_all x3, starting transfers between devices, body(): lax.all_to_all(outs[i], 'tm', split_axis=0, concat_axis=0, tiled=True)  14.2 us
    ppermute x9, waiting for transfers between devices, hop(): return lax.ppermute(state, 'space', [(k, k + 1)])  11.3 us
    ppermute x9, starting transfers between devices, hop(): return lax.ppermute(state, 'space', [(k, k + 1)])  10.2 us
    pallas_call x1, Pallas kernels, gate_proj(): call(gate_kernel, 'gate_proj', (2,), [full((rows, D)), pl.BlockSpec((DI /...  8.01 us
  transfers between devices with their start and end apart: 19, of which 8 were waited for; matrix products, arithmetic and copies ran while one was open for 4% of the time, Pallas kernels for 33%

profile of v5, /device:TPU:18, one launch (start us, length us, event | category | flops | bytes accessed | tf_op | source)
XLA Modules:
  0.0 151.7 jit_solution(11275975079136400992)
XLA Ops:
  0.0 2.6 %arrange.1 = (bf16[2,4,16,1024]{3,2,1,0:T(8,128)(2,1)}, bf16[2,4,16,1024]{3,2,1,0:T(8,128)(2,1)}, bf16[2,4,16,1024]{3,2,1,0:T(8,128)(2,1)}, bf16[2,4,16,1024]{3,...) custom-call(bf16[4,240,1024]{2,1,0:T(8,128)(2,1)} %bitcast.33), custom_call_target="tpu_custom_call" | custom-call | bytes 3932160 | tf_op jit(solution)/shard_map/arrange/pallas_call | solution.py:99
  2.7 0.6 collective-permute-start.1
  3.3 1.3 collective-permute-start.2
  4.5 1.5 %collective-permute-start.3 = (bf16[2,4,16,1024]{3,2,1,0:T(8,128)(2,1)}, bf16[2,4,16,1024]{3,2,1,0:T(8,128)(2,1)S(1)}, u32[]{:S(2)}, u32[]{:S(2)}) collective-permute-start(bf16[2,4,16,1024]{3,2,1,0:T(8,128)(2,1)} %get-tuple-element.57), channel_id=1, source_target_pairs={{0,16},{4,20},{8,24},{12,28},{16,0},{20,4},{24,8},{28,12},{1,17},{... | collective-permute-start | bytes 786440 | tf_op jit(solution)/shard_map/ppermute | solution.py:114
  6.0 0.2 collective-permute-start.4
  6.2 0.7 negate_multiply_fusion
  6.9 0.8 fusion.9
  7.7 0.6 stack.23.par_ref.refs_11_.refs_12_
  8.3 6.8 %space_prep.1 = (f32[4,256,256]{2,1,0:T(8,128)}, f32[4,256,128]{2,1,0:T(8,128)}, f32[4,32,256]{2,1,0:T(8,128)}, bf16[4,256,256]{2,1,0:T(8,128)(2,1)}, bf16[4,256...) custom-call(bf16[4,240,1024]{2,1,0:T(8,128)(2,1)} %bitcast.34, ...), custom_call_target="tpu_custom_call" | custom-call | flops 503316480 | bytes 6291456 | tf_op jit(solution)/shard_map/space_prep/pallas_call | solution.py:199
  15.1 1.6 %collective-permute-start.5 = (bf16[2,4,16,1024]{3,2,1,0:T(8,128)(2,1)S(1)}, bf16[2,4,16,1024]{3,2,1,0:T(8,128)(2,1)S(1)}, u32[]{:S(2)}, u32[]{:S(2)}) collective-permute-start(bf16[2,4,16,1024]{3,2,1,0:T(8,128)(2,1)S(1)} %copy-done.23), channel_id=1, source_target_pairs={{0,24},{4,28},{8,16},{12,20},{16,8},{20,12},{24,0},{28,4},{1,25},{... | collective-permute-start | bytes 786440 | tf_op jit(solution)/shard_map/ppermute | solution.py:114
  16.7 1.3 collective-permute-start.6
  18.0 8.0 %gate_proj.1 = bf16[960,2048]{1,0:T(8,128)(2,1)} custom-call(bf16[960,1024]{1,0:T(8,128)(2,1)} %bitcast.35, bf16[4416,1024]{1,0:T(8,128)(2,1)} %bitcast.41), custom_call_target="tpu_custom_call" | custom-call | flops 4026531840 | bytes 10092544 | tf_op jit(solution)/shard_map/gate_proj/pallas_call | solution.py:124
  26.1 3.9 %collective-permute-done.6 = bf16[2,4,16,1024]{3,2,1,0:T(8,128)(2,1)S(1)} collective-permute-done((bf16[2,4,16,1024]{3,2,1,0:T(8,128)(2,1)S(1)}, bf16[2,4,16,1024]{3,2,1,0:T(8,128)(2,1)S(1)}, u32[]{:S(2)}, u32[]{:S(2)}) %collective-permute-start.6) | collective-permute-done | bytes 262176 | tf_op jit(solution)/shard_map/ppermute | solution.py:114
  29.9 0.7 copy-done.17
  30.6 10.1 %time_scan.3 = (bf16[8,2,4,16,1024]{4,3,2,1,0:T(8,128)(2,1)}, f32[4,256,256]{2,1,0:T(8,128)}, f32[4,256,128]{2,1,0:T(8,128)}, f32[4,32,256]{2,1,0:T(8,128)}) custom-call(bf16[128,1024]{1,0:T(8,128)(2,1)} %bitcast.47, bf16[128,1024]{1,0:T(8,128)(2,1)} %bitcast.50, bf16[128,1024]{1,0:T(8,128)(2,1)} %bitcast.53, bf16[128,1024]{1,0:T(8,128)(2,1)} %bitcast.56, ...), custom_call_target="tpu_custom_call" | custom-call | flops 3221225472 | bytes 8388608 | tf_op jit(solution)/shard_map/time_scan/pallas_call | solution.py:336
  40.8 4.3 %all-to-all-start = ((bf16[8,2,4,16,1024]{4,3,2,1,0:T(8,128)(2,1)}), bf16[8,2,4,16,1024]{4,3,2,1,0:T(8,128)(2,1)S(1)}, u32[]{:S(2)}, u32[]{:S(2)}) async-start(bf16[8,2,4,16,1024]{4,3,2,1,0:T(8,128)(2,1)} %get-tuple-element.73), calls=%async_computation | async-start | bytes 4194304 | tf_op jit(solution)/shard_map/all_to_all | solution.py:571
  45.0 6.0 %time_scan.4 = bf16[8,2,4,16,512]{4,3,2,1,0:T(8,128)(2,1)} custom-call(bf16[128,1024]{1,0:T(8,128)(2,1)} %bitcast.48, bf16[128,1024]{1,0:T(8,128)(2,1)} %bitcast.51, bf16[128,1024]{1,0:T(8,128)(2,1)} %bitcast.54, bf16[128,1024]{1,0:T(8,128)(2,1)} %bitcast.57, bf16[128,1024]{1,0:T(8,128)(2,1)} %bitcast.60, bf16[128,1024]{1,0:T(8,128)(2,1)} %bitcast.63, ...), custom_call_target="tpu_custom_call" | custom-call | flops 1610612736 | bytes 6291456 | tf_op jit(solution)/shard_map/time_scan/pallas_call | solution.py:336
  51.0 5.9 %time_scan.5 = bf16[8,2,4,16,512]{4,3,2,1,0:T(8,128)(2,1)} custom-call(bf16[128,1024]{1,0:T(8,128)(2,1)} %bitcast.49, bf16[128,1024]{1,0:T(8,128)(2,1)} %bitcast.52, bf16[128,1024]{1,0:T(8,128)(2,1)} %bitcast.55, bf16[128,1024]{1,0:T(8,128)(2,1)} %bitcast.58, bf16[128,1024]{1,0:T(8,128)(2,1)} %bitcast.61, bf16[128,1024]{1,0:T(8,128)(2,1)} %bitcast.64, ...), custom_call_target="tpu_custom_call" | custom-call | flops 1610612736 | bytes 6291456 | tf_op jit(solution)/shard_map/time_scan/pallas_call | solution.py:336
  56.9 13.2 %all-to-all-done.x_ref = bf16[8,2,4,16,1024]{4,3,2,1,0:T(8,128)(2,1)S(1)} async-done(((bf16[8,2,4,16,1024]{4,3,2,1,0:T(8,128)(2,1)}), bf16[8,2,4,16,1024]{4,3,2,1,0:T(8,128)(2,1)S(1)}, u32[]{:S(2)}, u32[]{:S(2)}) %all-to-all-start) | async-done | bytes 2097184 | tf_op jit(solution)/shard_map/all_to_all | solution.py:571
  70.2 5.0 %all-to-all-start.1 = ((bf16[8,2,4,16,512]{4,3,2,1,0:T(8,128)(2,1)}), bf16[8,2,4,16,512]{4,3,2,1,0:T(8,128)(2,1)S(1)}, u32[]{:S(2)}, u32[]{:S(2)}) async-start(bf16[8,2,4,16,512]{4,3,2,1,0:T(8,128)(2,1)} %time_scan.4), calls=%async_computation.1 | async-start | bytes 2097152 | tf_op jit(solution)/shard_map/all_to_all | solution.py:571
  75.1 6.9 %space_local_end.3 = (f32[4,240,1024]{2,1,0:T(8,128)}, bf16[4,64,1024]{2,1,0:T(8,128)(2,1)}) custom-call(bf16[8,2,4,16,1024]{4,3,2,1,0:T(8,128)(2,1)} %copy-done.8, f32[4,256,256]{2,1,0:T(8,128)} %get-tuple-element.80.score_ref, f32[4,256,128]{2,1,0:T(8,128)} %get-tuple-element.81.cum_ref, f32[4,32,256]{2,1,0:T(8,128)} %get-tuple-element.82.row_ref, ...), custom_call_target="tpu_custom_call" | custom-call | flops 1073741824 | bytes 8388608 | tf_op jit(solution)/shard_map/space_local_end/pallas_call | solution.py:397
  82.0 0.7 collective-permute-start.9
  82.7 6.3 %all-to-all-done.1.x_ref = bf16[8,2,4,16,512]{4,3,2,1,0:T(8,128)(2,1)S(1)} async-done(((bf16[8,2,4,16,512]{4,3,2,1,0:T(8,128)(2,1)}), bf16[8,2,4,16,512]{4,3,2,1,0:T(8,128)(2,1)S(1)}, u32[]{:S(2)}, u32[]{:S(2)}) %all-to-all-start.1) | async-done | bytes 1048608 | tf_op jit(solution)/shard_map/all_to_all | solution.py:571
  89.1 5.0 %all-to-all-start.2 = ((bf16[8,2,4,16,512]{4,3,2,1,0:T(8,128)(2,1)}), bf16[8,2,4,16,512]{4,3,2,1,0:T(8,128)(2,1)S(1)}, u32[]{:S(2)}, u32[]{:S(2)}) async-start(bf16[8,2,4,16,512]{4,3,2,1,0:T(8,128)(2,1)} %time_scan.5), calls=%async_computation.2 | async-start | bytes 2097152 | tf_op jit(solution)/shard_map/all_to_all | solution.py:571
  94.1 4.7 %space_local_end.4 = (f32[4,240,512]{2,1,0:T(8,128)}, bf16[4,64,512]{2,1,0:T(8,128)(2,1)}) custom-call(bf16[8,2,4,16,512]{4,3,2,1,0:T(8,128)(2,1)} %copy-done.10, f32[4,256,256]{2,1,0:T(8,128)} %get-tuple-element.80.score_ref, f32[4,256,128]{2,1,0:T(8,128)} %get-tuple-element.81.cum_ref, f32[4,32,256]{2,1,0:T(8,128)} %get-tuple-element.82.row_ref, ...), custom_call_target="tpu_custom_call" | custom-call | flops 536870912 | bytes 5242880 | tf_op jit(solution)/shard_map/space_local_end/pallas_call | solution.py:397
  98.8 1.1 fusion
  99.8 1.4 collective-permute-start.10
  101.3 0.7 collective-permute-start.12
  102.0 6.0 %all-to-all-done.2.x_ref = bf16[8,2,4,16,512]{4,3,2,1,0:T(8,128)(2,1)S(1)} async-done(((bf16[8,2,4,16,512]{4,3,2,1,0:T(8,128)(2,1)}), bf16[8,2,4,16,512]{4,3,2,1,0:T(8,128)(2,1)S(1)}, u32[]{:S(2)}, u32[]{:S(2)}) %all-to-all-start.2) | async-done | bytes 1048608 | tf_op jit(solution)/shard_map/all_to_all | solution.py:571
  108.0 1.0 copy-done.9
  109.0 4.6 %space_local_end.5 = (f32[4,240,512]{2,1,0:T(8,128)}, bf16[4,64,512]{2,1,0:T(8,128)(2,1)}) custom-call(bf16[8,2,4,16,512]{4,3,2,1,0:T(8,128)(2,1)} %copy-done.9, f32[4,256,256]{2,1,0:T(8,128)} %get-tuple-element.80.score_ref, f32[4,256,128]{2,1,0:T(8,128)} %get-tuple-element.81.cum_ref, f32[4,32,256]{2,1,0:T(8,128)} %get-tuple-element.82.row_ref, ...), custom_call_target="tpu_custom_call" | custom-call | flops 536870912 | bytes 5242880 | tf_op jit(solution)/shard_map/space_local_end/pallas_call | solution.py:397
  113.6 0.7 collective-permute-start.7
  114.3 1.8 %collective-permute-done.10.rest_2_ = bf16[4,64,1024]{2,1,0:T(8,128)(2,1)S(1)} collective-permute-done((bf16[4,64,1024]{2,1,0:T(8,128)(2,1)}, bf16[4,64,1024]{2,1,0:T(8,128)(2,1)S(1)}, u32[]{:S(2)}, u32[]{:S(2)}) %collective-permute-start.10) | collective-permute-done | bytes 524320 | tf_op jit(solution)/shard_map/ppermute | solution.py:509
  116.2 1.6 %collective-permute-start.13 = (bf16[4,64,512]{2,1,0:T(8,128)(2,1)S(1)}, bf16[4,64,512]{2,1,0:T(8,128)(2,1)S(1)}, u32[]{:S(2)}, u32[]{:S(2)}) collective-permute-start(bf16[4,64,512]{2,1,0:T(8,128)(2,1)S(1)} %fusion.4), channel_id=1, source_target_pairs={{1,2},{5,6},{9,10},{13,14},{17,18},{21,22},{25,26},{29,30}} | collective-permute-start | bytes 786440 | tf_op jit(solution)/shard_map/ppermute | solution.py:509
  117.8 1.0 fusion.2
  118.8 1.3 collective-permute-start.8
  120.1 0.2 fusion.1
  120.3 1.3 collective-permute-start.11
  121.7 4.2 %collective-permute-done.13.rest_3_ = bf16[4,64,512]{2,1,0:T(8,128)(2,1)S(1)} collective-permute-done((bf16[4,64,512]{2,1,0:T(8,128)(2,1)S(1)}, bf16[4,64,512]{2,1,0:T(8,128)(2,1)S(1)}, u32[]{:S(2)}, u32[]{:S(2)}) %collective-permute-start.13) | collective-permute-done | bytes 262176 | tf_op jit(solution)/shard_map/ppermute | solution.py:509
  125.9 0.1 fusion.5
  126.0 1.3 collective-permute-start.14
  127.3 5.1 %collective-permute-done.8.rest_6_ = bf16[4,64,512]{2,1,0:T(8,128)(2,1)S(1)} collective-permute-done((bf16[4,64,512]{2,1,0:T(8,128)(2,1)S(1)}, bf16[4,64,512]{2,1,0:T(8,128)(2,1)S(1)}, u32[]{:S(2)}, u32[]{:S(2)}) %collective-permute-start.8) | collective-permute-done | bytes 262176 | tf_op jit(solution)/shard_map/ppermute | solution.py:509
  132.4 1.0 fusion.3
  133.5 1.3 collective-permute-start.15
  134.9 6.9 %early.1 = (f32[4,240,1024]{2,1,0:T(8,128)S(1)}, f32[4,240,128]{2,1,0:T(8,128)S(1)}) custom-call(bf16[4,240,2048]{2,1,0:T(8,128)(2,1)S(1)} %bitcast.31, bf16[4,256,256]{2,1,0:T(8,128)(2,1)S(1)} %copy-done.3, bf16[4,256,64]{2,1,0:T(8,128)(2,1)S(1)} %copy-done.6, f32[1,2048]{1,0:T(1,128)S(1)} %bitcast.37, bf16[2048,1024]{1,0:T(8,128)(2,1)} %w_ref.3, ...), custom_call_target="tpu_custom_call" | custom-call | flops 2013265920 | bytes 13893632 | tf_op jit(solution)/shard_map/early/pallas_call | solution.py:495
  141.8 1.9 %copy-done.2 = f32[4,240,1024]{2,1,0:T(8,128)} copy-done((f32[4,240,1024]{2,1,0:T(8,128)}, f32[4,240,1024]{2,1,0:T(8,128)S(1)}, u32[]{:S(2)}) %copy-start.2) | copy-done | bytes 3932184
  143.7 0.1 collective-permute-done.15.rest_7_
  143.8 7.8 %last.1 = bf16[4,240,1024]{2,1,0:T(8,128)(2,1)} custom-call(bf16[4,240,2048]{2,1,0:T(8,128)(2,1)S(1)} %bitcast.32, bf16[4,256,256]{2,1,0:T(8,128)(2,1)S(1)} %copy-done.3, bf16[4,256,64]{2,1,0:T(8,128)(2,1)S(1)} %copy-done.6, f32[1,2048]{1,0:T(1,128)S(1)} %bitcast.38, bf16[2048,1024]{1,0:T(8,128)(2,1)} %w_ref.3, f32[4,240,1024]{2,1,0:T(8,128)} %copy-done.2, ...), custom_call_target="tpu_custom_call" | custom-call | flops 2013265920 | bytes 13893632 | tf_op jit(solution)/shard_map/last/pallas_call | solution.py:495
  (66 shorter events, 0.2 us)
Async XLA Ops:
  2.6 12.5 %collective-permute-start = (bf16[2,4,16,1024]{3,2,1,0:T(8,128)(2,1)}, bf16[2,4,16,1024]{3,2,1,0:T(8,128)(2,1)S(1)}, u32[]{:S(2)}, u32[]{:S(2)}) collective-permute-start(bf16[2,4,16,1024]{3,2,1,0:T(8,128)(2,1)} %get-tuple-element.54), channel_id=1, source_target_pairs={{0,4},{4,0},{8,12},{12,8},{16,20},{20,16},{24,28},{28,24},{1,5},{5... | collective-permute-start | bytes 786440 | tf_op jit(solution)/shard_map/ppermute | solution.py:114
  2.7 14.0 %collective-permute-start.1 = (bf16[2,4,16,1024]{3,2,1,0:T(8,128)(2,1)}, bf16[2,4,16,1024]{3,2,1,0:T(8,128)(2,1)S(1)}, u32[]{:S(2)}, u32[]{:S(2)}) collective-permute-start(bf16[2,4,16,1024]{3,2,1,0:T(8,128)(2,1)} %get-tuple-element.55), channel_id=1, source_target_pairs={{0,8},{4,12},{8,0},{12,4},{16,24},{20,28},{24,16},{28,20},{1,9},{5... | collective-permute-start | bytes 786440 | tf_op jit(solution)/shard_map/ppermute | solution.py:114
  3.3 22.7 %collective-permute-start.2 = (bf16[2,4,16,1024]{3,2,1,0:T(8,128)(2,1)}, bf16[2,4,16,1024]{3,2,1,0:T(8,128)(2,1)S(1)}, u32[]{:S(2)}, u32[]{:S(2)}) collective-permute-start(bf16[2,4,16,1024]{3,2,1,0:T(8,128)(2,1)} %get-tuple-element.56), channel_id=1, source_target_pairs={{0,12},{4,8},{8,4},{12,0},{16,28},{20,24},{24,20},{28,16},{1,13},{... | collective-permute-start | bytes 786440 | tf_op jit(solution)/shard_map/ppermute | solution.py:114
  4.5 21.5 %collective-permute-start.3 = (bf16[2,4,16,1024]{3,2,1,0:T(8,128)(2,1)}, bf16[2,4,16,1024]{3,2,1,0:T(8,128)(2,1)S(1)}, u32[]{:S(2)}, u32[]{:S(2)}) collective-permute-start(bf16[2,4,16,1024]{3,2,1,0:T(8,128)(2,1)} %get-tuple-element.57), channel_id=1, source_target_pairs={{0,16},{4,20},{8,24},{12,28},{16,0},{20,4},{24,8},{28,12},{1,17},{... | collective-permute-start | bytes 786440 | tf_op jit(solution)/shard_map/ppermute | solution.py:114
  6.0 20.0 %collective-permute-start.4 = (bf16[2,4,16,1024]{3,2,1,0:T(8,128)(2,1)}, bf16[2,4,16,1024]{3,2,1,0:T(8,128)(2,1)S(1)}, u32[]{:S(2)}, u32[]{:S(2)}) collective-permute-start(bf16[2,4,16,1024]{3,2,1,0:T(8,128)(2,1)} %get-tuple-element.58), channel_id=1, source_target_pairs={{0,20},{4,16},{8,28},{12,24},{16,4},{20,0},{24,12},{28,8},{1,21},{... | collective-permute-start | bytes 786440 | tf_op jit(solution)/shard_map/ppermute | solution.py:114
  8.3 6.8 %copy-start.23 = (bf16[2,4,16,1024]{3,2,1,0:T(8,128)(2,1)S(1)}, bf16[2,4,16,1024]{3,2,1,0:T(8,128)(2,1)}, u32[]{:S(2)}) copy-start(bf16[2,4,16,1024]{3,2,1,0:T(8,128)(2,1)} %get-tuple-element.59) | copy-start | bytes 786436
  8.3 8.4 %copy-start.22 = (bf16[2,4,16,1024]{3,2,1,0:T(8,128)(2,1)S(1)}, bf16[2,4,16,1024]{3,2,1,0:T(8,128)(2,1)}, u32[]{:S(2)}) copy-start(bf16[2,4,16,1024]{3,2,1,0:T(8,128)(2,1)} %get-tuple-element.60) | copy-start | bytes 786436
  15.1 10.9 %copy-start.11 = (bf16[2,4,16,1024]{3,2,1,0:T(8,128)(2,1)}, bf16[2,4,16,1024]{3,2,1,0:T(8,128)(2,1)S(1)}, u32[]{:S(2)}) copy-start(bf16[2,4,16,1024]{3,2,1,0:T(8,128)(2,1)S(1)} %collective-permute-done) | copy-start | bytes 786436
  15.1 10.9 %collective-permute-start.5 = (bf16[2,4,16,1024]{3,2,1,0:T(8,128)(2,1)S(1)}, bf16[2,4,16,1024]{3,2,1,0:T(8,128)(2,1)S(1)}, u32[]{:S(2)}, u32[]{:S(2)}) collective-permute-start(bf16[2,4,16,1024]{3,2,1,0:T(8,128)(2,1)S(1)} %copy-done.23), channel_id=1, source_target_pairs={{0,24},{4,28},{8,16},{12,20},{16,8},{20,12},{24,0},{28,4},{1,25},{... | collective-permute-start | bytes 786440 | tf_op jit(solution)/shard_map/ppermute | solution.py:114
  16.7 9.3 %copy-start.12 = (bf16[2,4,16,1024]{3,2,1,0:T(8,128)(2,1)}, bf16[2,4,16,1024]{3,2,1,0:T(8,128)(2,1)S(1)}, u32[]{:S(2)}) copy-start(bf16[2,4,16,1024]{3,2,1,0:T(8,128)(2,1)S(1)} %collective-permute-done.1) | copy-start | bytes 786436
  16.7 13.2 %collective-permute-start.6 = (bf16[2,4,16,1024]{3,2,1,0:T(8,128)(2,1)S(1)}, bf16[2,4,16,1024]{3,2,1,0:T(8,128)(2,1)S(1)}, u32[]{:S(2)}, u32[]{:S(2)}) collective-permute-start(bf16[2,4,16,1024]{3,2,1,0:T(8,128)(2,1)S(1)} %copy-done.22), channel_id=1, source_target_pairs={{0,28},{4,24},{8,20},{12,16},{16,12},{20,8},{24,4},{28,0},{1,29},{... | collective-permute-start | bytes 786440 | tf_op jit(solution)/shard_map/ppermute | solution.py:114
  26.0 3.9 %copy-start.13 = (bf16[2,4,16,1024]{3,2,1,0:T(8,128)(2,1)}, bf16[2,4,16,1024]{3,2,1,0:T(8,128)(2,1)S(1)}, u32[]{:S(2)}) copy-start(bf16[2,4,16,1024]{3,2,1,0:T(8,128)(2,1)S(1)} %collective-permute-done.2) | copy-start | bytes 786436
  26.0 3.9 %copy-start.14 = (bf16[2,4,16,1024]{3,2,1,0:T(8,128)(2,1)}, bf16[2,4,16,1024]{3,2,1,0:T(8,128)(2,1)S(1)}, u32[]{:S(2)}) copy-start(bf16[2,4,16,1024]{3,2,1,0:T(8,128)(2,1)S(1)} %collective-permute-done.3) | copy-start | bytes 786436
  26.0 3.9 %copy-start.15 = (bf16[2,4,16,1024]{3,2,1,0:T(8,128)(2,1)}, bf16[2,4,16,1024]{3,2,1,0:T(8,128)(2,1)S(1)}, u32[]{:S(2)}) copy-start(bf16[2,4,16,1024]{3,2,1,0:T(8,128)(2,1)S(1)} %collective-permute-done.4) | copy-start | bytes 786436
  26.0 3.9 %copy-start.16 = (bf16[2,4,16,1024]{3,2,1,0:T(8,128)(2,1)}, bf16[2,4,16,1024]{3,2,1,0:T(8,128)(2,1)S(1)}, u32[]{:S(2)}) copy-start(bf16[2,4,16,1024]{3,2,1,0:T(8,128)(2,1)S(1)} %collective-permute-done.5) | copy-start | bytes 786436
  29.9 0.7 copy-start.17
  40.8 29.4 %all-to-all-start = ((bf16[8,2,4,16,1024]{4,3,2,1,0:T(8,128)(2,1)}), bf16[8,2,4,16,1024]{4,3,2,1,0:T(8,128)(2,1)S(1)}, u32[]{:S(2)}, u32[]{:S(2)}) async-start(bf16[8,2,4,16,1024]{4,3,2,1,0:T(8,128)(2,1)} %get-tuple-element.73), calls=%async_computation | async-start | bytes 4194304 | tf_op jit(solution)/shard_map/all_to_all | solution.py:571
  70.2 5.0 %copy-start.8 = (bf16[8,2,4,16,1024]{4,3,2,1,0:T(8,128)(2,1)}, bf16[8,2,4,16,1024]{4,3,2,1,0:T(8,128)(2,1)S(1)}, u32[]{:S(2)}) copy-start(bf16[8,2,4,16,1024]{4,3,2,1,0:T(8,128)(2,1)S(1)} %all-to-all-done.x_ref) | copy-start | bytes 6291460
  70.2 18.9 %all-to-all-start.1 = ((bf16[8,2,4,16,512]{4,3,2,1,0:T(8,128)(2,1)}), bf16[8,2,4,16,512]{4,3,2,1,0:T(8,128)(2,1)S(1)}, u32[]{:S(2)}, u32[]{:S(2)}) async-start(bf16[8,2,4,16,512]{4,3,2,1,0:T(8,128)(2,1)} %time_scan.4), calls=%async_computation.1 | async-start | bytes 2097152 | tf_op jit(solution)/shard_map/all_to_all | solution.py:571
  82.0 12.0 %copy-start.21 = (f32[4,1,2048]{2,1,0:T(1,128)S(1)}, f32[4,1,2048]{2,1,0:T(1,128)}, u32[]{:S(2)}) copy-start(f32[4,1,2048]{2,1,0:T(1,128)} %get-tuple-element.91) | copy-start | bytes 98308
  82.0 16.7 %collective-permute-start.9 = (bf16[4,64,1024]{2,1,0:T(8,128)(2,1)}, bf16[4,64,1024]{2,1,0:T(8,128)(2,1)S(1)}, u32[]{:S(2)}, u32[]{:S(2)}) collective-permute-start(bf16[4,64,1024]{2,1,0:T(8,128)(2,1)} %get-tuple-element.85), channel_id=1, source_target_pairs={{0,1},{4,5},{8,9},{12,13},{16,17},{20,21},{24,25},{28,29}} | collective-permute-start | bytes 1572872 | tf_op jit(solution)/shard_map/ppermute | solution.py:509
  89.1 5.0 %copy-start.10 = (bf16[8,2,4,16,512]{4,3,2,1,0:T(8,128)(2,1)}, bf16[8,2,4,16,512]{4,3,2,1,0:T(8,128)(2,1)S(1)}, u32[]{:S(2)}) copy-start(bf16[8,2,4,16,512]{4,3,2,1,0:T(8,128)(2,1)S(1)} %all-to-all-done.1.x_ref) | copy-start | bytes 3145732
  89.1 18.9 %all-to-all-start.2 = ((bf16[8,2,4,16,512]{4,3,2,1,0:T(8,128)(2,1)}), bf16[8,2,4,16,512]{4,3,2,1,0:T(8,128)(2,1)S(1)}, u32[]{:S(2)}, u32[]{:S(2)}) async-start(bf16[8,2,4,16,512]{4,3,2,1,0:T(8,128)(2,1)} %time_scan.5), calls=%async_computation.2 | async-start | bytes 2097152 | tf_op jit(solution)/shard_map/all_to_all | solution.py:571
  94.1 4.7 %copy-start.18 = (bf16[4,64,1024]{2,1,0:T(8,128)(2,1)S(1)}, bf16[4,64,1024]{2,1,0:T(8,128)(2,1)}, u32[]{:S(2)}) copy-start(bf16[4,64,1024]{2,1,0:T(8,128)(2,1)} %get-tuple-element.85) | copy-start | bytes 1572868
  99.8 16.2 %copy-start.20 = (bf16[4,64,512]{2,1,0:T(8,128)(2,1)S(1)}, bf16[4,64,512]{2,1,0:T(8,128)(2,1)}, u32[]{:S(2)}) copy-start(bf16[4,64,512]{2,1,0:T(8,128)(2,1)} %get-tuple-element.88) | copy-start | bytes 786436
  99.8 20.3 %copy-start.19 = (bf16[4,64,1024]{2,1,0:T(8,128)(2,1)S(1)}, bf16[4,64,1024]{2,1,0:T(8,128)(2,1)}, u32[]{:S(2)}) copy-start(bf16[4,64,1024]{2,1,0:T(8,128)(2,1)} %get-tuple-element.85) | copy-start | bytes 1572868
  99.8 16.2 %collective-permute-start.10 = (bf16[4,64,1024]{2,1,0:T(8,128)(2,1)}, bf16[4,64,1024]{2,1,0:T(8,128)(2,1)S(1)}, u32[]{:S(2)}, u32[]{:S(2)}) collective-permute-start(bf16[4,64,1024]{2,1,0:T(8,128)(2,1)} %fusion), channel_id=1, source_target_pairs={{1,2},{5,6},{9,10},{13,14},{17,18},{21,22},{25,26},{29,30}} | collective-permute-start | bytes 1572872 | tf_op jit(solution)/shard_map/ppermute | solution.py:509
  101.3 14.8 %collective-permute-start.12 = (bf16[4,64,512]{2,1,0:T(8,128)(2,1)}, bf16[4,64,512]{2,1,0:T(8,128)(2,1)S(1)}, u32[]{:S(2)}, u32[]{:S(2)}) collective-permute-start(bf16[4,64,512]{2,1,0:T(8,128)(2,1)} %get-tuple-element.88), channel_id=1, source_target_pairs={{0,1},{4,5},{8,9},{12,13},{16,17},{20,21},{24,25},{28,29}} | collective-permute-start | bytes 786440 | tf_op jit(solution)/shard_map/ppermute | solution.py:509
  108.0 1.0 copy-start.9
  113.6 4.2 %collective-permute-start.7 = (bf16[4,64,512]{2,1,0:T(8,128)(2,1)}, bf16[4,64,512]{2,1,0:T(8,128)(2,1)S(1)}, u32[]{:S(2)}, u32[]{:S(2)}) collective-permute-start(bf16[4,64,512]{2,1,0:T(8,128)(2,1)} %get-tuple-element.90), channel_id=1, source_target_pairs={{0,1},{4,5},{8,9},{12,13},{16,17},{20,21},{24,25},{28,29}} | collective-permute-start | bytes 786440 | tf_op jit(solution)/shard_map/ppermute | solution.py:509
  116.1 18.7 %copy-start.3 = (bf16[4,256,256]{2,1,0:T(8,128)(2,1)S(1)}, bf16[4,256,256]{2,1,0:T(8,128)(2,1)}, u32[]{:S(2)}) copy-start(bf16[4,256,256]{2,1,0:T(8,128)(2,1)} %get-tuple-element.63.ecum_ref) | copy-start | bytes 1572868
  116.1 18.7 %copy-start.6 = (bf16[4,256,64]{2,1,0:T(8,128)(2,1)S(1)}, bf16[4,256,64]{2,1,0:T(8,128)(2,1)}, u32[]{:S(2)}) copy-start(bf16[4,256,64]{2,1,0:T(8,128)(2,1)} %get-tuple-element.64.c_ref) | copy-start | bytes 393220
  116.2 18.6 %copy-start = (bf16[960,2048]{1,0:T(8,128)(2,1)S(1)}, bf16[960,2048]{1,0:T(8,128)(2,1)}, u32[]{:S(2)}) copy-start(bf16[960,2048]{1,0:T(8,128)(2,1)} %gate_proj.1) | copy-start | bytes 11796484
  116.2 18.6 %copy-start.7 = (f32[2048]{0:T(1024)S(1)}, f32[2048]{0:T(1024)}, u32[]{:S(2)}) copy-start(f32[2048]{0:T(1024)} %param.19) | copy-start | bytes 24580
  116.2 9.7 %collective-permute-start.13 = (bf16[4,64,512]{2,1,0:T(8,128)(2,1)S(1)}, bf16[4,64,512]{2,1,0:T(8,128)(2,1)S(1)}, u32[]{:S(2)}, u32[]{:S(2)}) collective-permute-start(bf16[4,64,512]{2,1,0:T(8,128)(2,1)S(1)} %fusion.4), channel_id=1, source_target_pairs={{1,2},{5,6},{9,10},{13,14},{17,18},{21,22},{25,26},{29,30}} | collective-permute-start | bytes 786440 | tf_op jit(solution)/shard_map/ppermute | solution.py:509
  118.8 13.6 %collective-permute-start.8 = (bf16[4,64,512]{2,1,0:T(8,128)(2,1)S(1)}, bf16[4,64,512]{2,1,0:T(8,128)(2,1)S(1)}, u32[]{:S(2)}, u32[]{:S(2)}) collective-permute-start(bf16[4,64,512]{2,1,0:T(8,128)(2,1)S(1)} %fusion.2), channel_id=1, source_target_pairs={{1,2},{5,6},{9,10},{13,14},{17,18},{21,22},{25,26},{29,30}} | collective-permute-start | bytes 786440 | tf_op jit(solution)/shard_map/ppermute | solution.py:509
  120.3 14.5 %collective-permute-start.11 = (bf16[4,64,1024]{2,1,0:T(8,128)(2,1)S(1)}, bf16[4,64,1024]{2,1,0:T(8,128)(2,1)S(1)}, u32[]{:S(2)}, u32[]{:S(2)}) collective-permute-start(bf16[4,64,1024]{2,1,0:T(8,128)(2,1)S(1)} %fusion.1), channel_id=1, source_target_pairs={{2,3},{6,7},{10,11},{14,15},{18,19},{22,23},{26,27},{30,31}} | collective-permute-start | bytes 1572872 | tf_op jit(solution)/shard_map/ppermute | solution.py:509
  126.0 17.7 %collective-permute-start.14 = (bf16[4,64,512]{2,1,0:T(8,128)(2,1)S(1)}, bf16[4,64,512]{2,1,0:T(8,128)(2,1)S(1)}, u32[]{:S(2)}, u32[]{:S(2)}) collective-permute-start(bf16[4,64,512]{2,1,0:T(8,128)(2,1)S(1)} %fusion.5), channel_id=1, source_target_pairs={{2,3},{6,7},{10,11},{14,15},{18,19},{22,23},{26,27},{30,31}} | collective-permute-start | bytes 786440 | tf_op jit(solution)/shard_map/ppermute | solution.py:509
  133.5 10.3 %collective-permute-start.15 = (bf16[4,64,512]{2,1,0:T(8,128)(2,1)S(1)}, bf16[4,64,512]{2,1,0:T(8,128)(2,1)S(1)}, u32[]{:S(2)}, u32[]{:S(2)}) collective-permute-start(bf16[4,64,512]{2,1,0:T(8,128)(2,1)S(1)} %fusion.3), channel_id=1, source_target_pairs={{2,3},{6,7},{10,11},{14,15},{18,19},{22,23},{26,27},{30,31}} | collective-permute-start | bytes 786440 | tf_op jit(solution)/shard_map/ppermute | solution.py:509
  134.8 9.0 %copy-start.1 = (bf16[4,3,80,1024]{3,2,1,0:T(8,128)(2,1)S(1)}, bf16[4,3,80,1024]{3,2,1,0:T(8,128)(2,1)}, u32[]{:S(2)}) copy-start(bf16[4,3,80,1024]{3,2,1,0:T(8,128)(2,1)} %param.10) | copy-start | bytes 5898244
  134.8 9.0 %copy-start.4 = (f32[4,240,512]{2,1,0:T(8,128)S(1)}, f32[4,240,512]{2,1,0:T(8,128)}, u32[]{:S(2)}) copy-start(f32[4,240,512]{2,1,0:T(8,128)} %get-tuple-element.98.rest_0_) | copy-start | bytes 5898244
  134.9 9.0 %copy-start.5 = (f32[4,240,512]{2,1,0:T(8,128)S(1)}, f32[4,240,512]{2,1,0:T(8,128)}, u32[]{:S(2)}) copy-start(f32[4,240,512]{2,1,0:T(8,128)} %get-tuple-element.99.rest_1_) | copy-start | bytes 5898244
  141.8 1.9 %copy-start.2 = (f32[4,240,1024]{2,1,0:T(8,128)}, f32[4,240,1024]{2,1,0:T(8,128)S(1)}, u32[]{:S(2)}) copy-start(f32[4,240,1024]{2,1,0:T(8,128)S(1)} %get-tuple-element.96.acc_ref) | copy-start | bytes 11796484
